TPU v7x, 256 devices: a whole 4x4x8 slice. The times are simulated.
256 devices in a mesh: head: 4 (over x), vocab: 32 (over y_lo, z, core), width: 2 (over y_hi).
Axes of the slice: x: 4, y: 4 (y_hi: 2, y_lo: 2; y = y_hi * 2 + y_lo), z: 8, core: 2. Of those that a mesh axis runs over, the one named last changes fastest.
Arguments:
- trunk_rows: bfloat16 [256, 6656], P(('vocab', 'width')), may hold values from -12 to 12
- res_weight: bfloat16 [4, 6656, 6656], P('head', None, ('width', 'vocab')), may hold values from -0.078125 to 0.078125
- res_bias: bfloat16 [4, 6656], P('head', ('width', 'vocab')), may hold values from -4 to 4
- lm_weight: bfloat16 [4, 6656, 20480], P('head', 'width', 'vocab'), may hold values from -0.08849741 to 0.08849741
- next_ids: int32 [260], replicated, may hold values from 0 to 20479
- valid_mask: int32 [260], replicated, may hold values 0 or 1
Outputs:
- trunk_grad: float32 [256, 6656], P(('vocab', 'width'))
- res_weight_grad: bfloat16 [4, 6656, 6656], P('head', None, ('width', 'vocab'))
- res_bias_grad: float32 [4, 6656], P('head', ('width', 'vocab'))
- lm_weight_grad: bfloat16 [4, 6656, 20480], P('head', 'width', 'vocab')
All inputs are finite; a program needn't handle non-finite values.
Results may differ from a plain program's by a relative error of at most 0.01125.
Values may be sent and summed in bfloat16 or wider, within the bound.
No kernel may reach another device: no remote copies, remote signals or barrier semaphores. Data moves between devices by JAX's collectives and lax.ppermute only.
A program may use at most 128 MiB of HBM per device.

v0:
```python
import jax
import jax.numpy as jnp
from jax import lax
from jax.sharding import PartitionSpec as P

loss_scale = 16.0


def silu_grad(value):
    sigma = jax.nn.sigmoid(value)
    return sigma * (1.0 + value * (1.0 - sigma))


def on_device(trunk_rows, res_weight, res_bias, lm_weight, next_ids, valid_mask):
    trunk_full = lax.all_gather(trunk_rows, ("vocab", "width"), axis=0, tiled=True)
    tok_rows = trunk_full.shape[0]
    head_idx = lax.axis_index("head")
    vocab_idx = lax.axis_index("vocab")
    width_idx = lax.axis_index("width")
    res_cols = res_weight[0]
    lm_rows = lm_weight[0]
    col_width = res_cols.shape[1]
    vocab_width = lm_rows.shape[1]
    col_start = (width_idx * lax.axis_size("vocab") + vocab_idx) * col_width
    pre_act = jnp.dot(trunk_full, res_cols, preferred_element_type=jnp.float32)
    pre_act = pre_act + res_bias[0].astype(jnp.float32)[None, :]
    own_cols = lax.dynamic_slice_in_dim(trunk_full, col_start, col_width, 1)
    hidden = (own_cols.astype(jnp.float32) + jax.nn.silu(pre_act)).astype(jnp.bfloat16)
    hidden_half = lax.all_gather(hidden, "vocab", axis=1, tiled=True)
    logits = lax.psum(jnp.dot(hidden_half, lm_rows, preferred_element_type=jnp.float32), "width")
    top_val = lax.pmax(jnp.max(logits, axis=1), "vocab")
    row_exp = jnp.exp(logits - top_val[:, None])
    total_val = lax.psum(jnp.sum(row_exp, axis=1), "vocab")
    row_probs = row_exp / total_val[:, None]
    tok_ids = lax.dynamic_slice_in_dim(next_ids, head_idx + 1, tok_rows)
    live_rows = lax.dynamic_slice_in_dim(valid_mask, head_idx + 1, tok_rows).astype(jnp.float32)
    local_ids = tok_ids - vocab_idx * vocab_width
    onehot = (local_ids[:, None] == lax.broadcasted_iota(jnp.int32, (1, vocab_width), 1)).astype(
        jnp.float32
    )
    head_scale = loss_scale * jnp.power(jnp.float32(0.8), head_idx.astype(jnp.float32))
    grad_logits = (head_scale * live_rows[:, None] * (row_probs - onehot)).astype(jnp.bfloat16)
    lm_grad = lax.dot_general(
        hidden_half, grad_logits, (((0,), (0,)), ((), ())), preferred_element_type=jnp.float32
    ).astype(jnp.bfloat16)
    hidden_grad = lax.psum_scatter(
        lax.dot_general(
            lm_rows, grad_logits, (((1,), (1,)), ((), ())), preferred_element_type=jnp.float32
        ),
        "vocab",
        scatter_dimension=0,
        tiled=True,
    ).T
    pre_grad = hidden_grad * silu_grad(pre_act)
    pre_round = pre_grad.astype(jnp.bfloat16)
    res_grad = lax.dot_general(
        trunk_full, pre_round, (((0,), (0,)), ((), ())), preferred_element_type=jnp.float32
    ).astype(jnp.bfloat16)
    bias_grad = jnp.sum(pre_grad, axis=0)
    partial_value = lax.dot_general(
        pre_round, res_cols, (((1,), (1,)), ((), ())), preferred_element_type=jnp.float32
    )
    with_direct = lax.dynamic_slice_in_dim(partial_value, col_start, col_width, 1) + hidden_grad
    summed = lax.psum_scatter(
        lax.dynamic_update_slice_in_dim(partial_value, with_direct, col_start, 1),
        ("vocab", "width"),
        scatter_dimension=0,
        tiled=True,
    )
    trunk_grad = lax.psum(summed.astype(jnp.bfloat16), "head").astype(jnp.float32)
    return (trunk_grad, res_grad[None], bias_grad[None], lm_grad[None])


def solution(mesh):
    in_specs = (
        P(("vocab", "width"), None),
        P("head", None, ("width", "vocab")),
        P("head", ("width", "vocab")),
        P("head", "width", "vocab"),
        P(),
        P(),
    )
    out_specs = (
        P(("vocab", "width"), None),
        P("head", None, ("width", "vocab")),
        P("head", ("width", "vocab")),
        P("head", "width", "vocab"),
    )
    return jax.shard_map(
        on_device, mesh=mesh, in_specs=in_specs, out_specs=out_specs, check_vma=False
    )
```

profile of v0, /device:TPU:72, one launch (start us, length us, event | category | flops | bytes accessed | tf_op | source)
XLA Modules:
  0.0 967.1 jit_solution(3284742407720062444)
XLA Ops:
  7.2 0.7 all-gather.6.cloned.1.call-update
  8.0 0.7 bitcast_convert_fusion
  8.6 185.3 %all-gather.6.cloned.1.call-done = bf16[64,4,6656]{2,1,0:T(4,128)(2,1)} async-done(((bf16[1,4,6656]{2,1,0:T(4,128)(2,1)}), bf16[64,4,6656]{2,1,0:T(4,128)(2,1)}) %all-gather.6.cloned.1.call-update) | async-done | bytes 3407888 | tf_op jit(solution)/shard_map/all_gather | solution.py:15
  193.9 6.6 reshape.15
  200.4 1.0 constant_dynamic-slice_fusion.1
  201.4 0.1 copy.23
  201.6 3.8 add_convert_fusion
  205.4 70.8 %all-gather.4.cloned.1.call-done = bf16[256,3328]{0,1:T(8,128)(2,1)} async-done(((bf16[256,104]{0,1:T(8,128)(2,1)}), bf16[256,3328]{0,1:T(8,128)(2,1)}) %all-gather.4.cloned.1.call-update) | async-done | bytes 1703952 | tf_op jit(solution)/shard_map/all_gather | solution.py:29
  276.3 5.1 fusion.3
  281.5 0.1 dynamic-slice_subtract_fusion
  281.7 43.9 %all-reduce.4.cloned.1.call-done = f32[256,640]{1,0:T(8,128)} async-done(((f32[256,640]{1,0:T(8,128)}), f32[256,640]{1,0:T(8,128)}) %all-reduce.4.cloned.1.call-update) | async-done | bytes 655376 | tf_op jit(solution)/shard_map/psum | solution.py:30
  325.5 1.2 reduce_max.9
  326.7 48.8 %pmax.7 = f32[256]{0:T(256)S(1)} all-reduce(f32[256]{0:T(256)S(1)} %reduce_max.9), channel_id=1, replica_groups=mesh['head'=4,'vocab'=32,'width'=2] {'vocab'}, use_global_device_ids=true, to_apply=%region_2.3 | all-reduce | flops 256 | bytes 2048 | tf_op jit(solution)/shard_map/pmax | solution.py:31
  375.5 1.3 fusion.12
  376.9 53.0 %psum.22 = f32[256]{0:T(256)S(1)} all-reduce(f32[256]{0:T(256)S(1)} %fusion.12), channel_id=1, replica_groups=mesh['head'=4,'vocab'=32,'width'=2] {'vocab'}, use_global_device_ids=true, to_apply=%region_4.5 | all-reduce | flops 256 | bytes 2048 | tf_op jit(solution)/shard_map/psum | solution.py:33
  429.9 5.9 convolution_bitcast_fusion
  435.8 0.6 copy-done.6
  436.5 0.6 dynamic-slice
  437.7 5.2 fusion.1
  442.9 107.6 %reduce-scatter.2.cloned.1.call-done = f32[104,256]{1,0:T(8,128)} async-done(((f32[3328,256]{1,0:T(8,128)}), f32[104,256]{1,0:T(8,128)}) %reduce-scatter.2.cloned.1.call-update) | async-done | bytes 106512 | tf_op jit(solution)/shard_map/reduce_scatter | solution.py:46
  550.5 1.6 fusion.15
  552.0 3.7 fusion
  555.8 1.1 fusion.5
  556.8 2.8 copy-done.1
  559.6 0.1 constant_dynamic-slice_fusion
  559.7 0.1 copy.24
  559.9 0.1 copy.21
  559.9 1.9 dynamic_update_slice.3
  561.9 357.2 %all-reduce.5 = bf16[256,6656]{1,0:T(8,128)(2,1)} all-reduce(f32[256,6656]{1,0:T(8,128)} %dynamic_update_slice.3), channel_id=3, replica_groups=mesh['head'=4,'vocab'=32,'width'=2] {'vocab','width'}, use_global_device_ids=true, to_apply=%region_6.7.clone | all-reduce | flops 1703936 | bytes 10223616
  919.1 0.9 dynamic-slice_convert_fusion
  920.0 39.9 %psum.23 = bf16[4,6656]{1,0:T(4,128)(2,1)S(1)} all-reduce(bf16[4,6656]{1,0:T(4,128)(2,1)S(1)} %dynamic-slice_convert_fusion), channel_id=1, replica_groups=mesh['head'=4,'vocab'=32,'width'=2] {'head'}, use_global_device_ids=true, to_apply=%region_7.8 | all-reduce | flops 26624 | bytes 106496 | tf_op jit(solution)/shard_map/psum | solution.py:70
  959.9 0.7 convert_element_type.46
  (21 shorter events, 0.3 us)
Async XLA Ops:
  7.2 194.4 %copy-start = (bf16[1,6656,104]{1,2,0:T(8,128)(2,1)S(1)}, bf16[1,6656,104]{1,2,0:T(8,128)(2,1)}, u32[]{:S(2)}) copy-start(bf16[1,6656,104]{1,2,0:T(8,128)(2,1)} %param.7) | copy-start | bytes 4153348
  7.2 186.7 %all-gather.6.cloned.1.call-start = ((), (), s32[]{:S(2)}) async-start(), calls=%async_computation.4 | async-start | bytes 3461120 | tf_op jit(solution)/shard_map/all_gather | solution.py:15
  7.9 268.4 %all-gather.4.cloned.1.call-start = ((), (), s32[]{:S(2)}) async-start(), calls=%async_computation.1 | async-start | bytes 1757184 | tf_op jit(solution)/shard_map/all_gather | solution.py:29
  205.3 76.1 %copy-start.4 = (s32[260]{0:T(512)S(1)}, s32[260]{0:T(512)}, u32[]{:S(2)}) copy-start(s32[260]{0:T(512)} %param.10) | copy-start | bytes 3124
  205.4 76.2 %copy-start.5 = (s32[260]{0:T(512)S(1)}, s32[260]{0:T(512)}, u32[]{:S(2)}) copy-start(s32[260]{0:T(512)} %param.11) | copy-start | bytes 3124
  205.4 120.2 %all-reduce.4.cloned.1.call-start = ((), (), s32[]{:S(2)}) async-start(), calls=%async_computation.2 | async-start | bytes 1310720 | tf_op jit(solution)/shard_map/psum | solution.py:30
  281.4 269.1 %reduce-scatter.2.cloned.1.call-start = ((), (), s32[]{:S(2)}) async-start(), calls=%async_computation.3 | async-start | bytes 3514368 | tf_op jit(solution)/shard_map/reduce_scatter | solution.py:46
  435.8 0.7 copy-start.6
  435.8 1.9 copy-start.2
  555.8 4.1 copy-start.3
  556.8 2.8 copy-start.1
Sparse Core Ops, SparseCore 0:
  9.8 184.0 all-gather.5
  205.5 70.7 all-gather.3
  281.5 43.9 all-reduce.3
  435.9 114.5 reduce-scatter.1
where the time goes:
time: 968 us; the launch traced here: 967 us
  blocking collectives  499 us (52%)
  waiting for transfers between devices  408 us (42%)
  matrix products  24.7 us (3%)
  local copies, waits for them, and re-layouts  14.8 us (2%)
  between operations  14.6 us (2%)
    unnamed x1, blocking collectives  357 us
    all_gather x1, waiting for transfers between devices, on_device(): lax.all_gather(trunk_rows, ('vocab', 'width'), axis=0, tiled=True)  185 us
    reduce_scatter x1, waiting for transfers between devices, on_device(): lax.psum_scatter(lax.dot_general(lm_rows, grad_logits, (((1,), (1,)), (()...  108 us
    all_gather x1, waiting for transfers between devices, on_device(): hidden_half = lax.all_gather(hidden, 'vocab', axis=1, tiled=True)  70.8 us
    psum x1, blocking collectives, on_device(): total_val = lax.psum(jnp.sum(row_exp, axis=1), 'vocab')  53 us
    pmax x1, blocking collectives, on_device(): top_val = lax.pmax(jnp.max(logits, axis=1), 'vocab')  48.8 us
    psum x1, waiting for transfers between devices, on_device(): lax.psum(jnp.dot(hidden_half, lm_rows, preferred_element_type=jnp.float32...  43.9 us
    psum x1, blocking collectives, on_device(): lax.psum(summed.astype(jnp.bfloat16), 'head').astype(jnp.float32)  39.9 us
  transfers between devices with their start and end apart: 4, of which 4 were waited for; matrix products, arithmetic and copies ran while one was open for 1% of the time, Pallas kernels for 0%

commit v1 on v0

v1 whole, which is shorter than its diff:
```python
import jax
import jax.numpy as jnp
from jax import lax
from jax.sharding import Mesh
from jax.sharding import PartitionSpec as P

loss_scale = 16.0
f32 = jnp.float32
bf16 = jnp.bfloat16
plane = ("ylo", "z")
plane_all = ("ylo", "z", "yhi")


def silu_grad(value):
    sigma = jax.nn.sigmoid(value)
    return sigma * (1.0 + value * (1.0 - sigma))


def swap(value, axis):
    return lax.ppermute(value, axis, [(0, 1), (1, 0)])


def exchange(value, axes):
    return lax.all_to_all(value, axes, 0, 0, tiled=True)


def dot(a, b, contract):
    return lax.dot_general(a, b, ((contract[0], contract[1]), ((), ())), preferred_element_type=f32)


def on_device(trunk_rows, res_weight, res_bias, lm_weight, next_ids, valid_mask):
    head = lax.axis_index("x")
    ylo, z, core, yhi = (lax.axis_index(a) for a in ("ylo", "z", "core", "yhi"))
    n_x = lax.axis_size("x")
    n_plane = lax.axis_size("ylo") * lax.axis_size("z")
    n_all = n_plane * lax.axis_size("yhi")
    rows, width = trunk_rows.shape
    quarter = width // n_x
    toks = n_all * rows

    res_own = res_weight[0].T
    cols = res_own.shape[0]
    pair = 2 * cols
    lm_own = lm_weight[0]
    half, vocab_width = lm_own.shape
    res_other = swap(res_own, "core")
    lm_other = swap(lm_own, "core")
    first = core == 0
    res_pair = jnp.concatenate(
        [jnp.where(first, res_own, res_other), jnp.where(first, res_other, res_own)], 0
    )
    bias_own = res_bias[0].astype(f32)
    bias_other = swap(bias_own, "core")
    bias_pair = jnp.concatenate(
        [jnp.where(first, bias_own, bias_other), jnp.where(first, bias_other, bias_own)]
    )

    mine = lax.dynamic_slice_in_dim(trunk_rows, head * quarter, quarter, 1)
    part = exchange(jnp.broadcast_to(mine[None], (n_all, rows, quarter)), plane_all)
    part = part.reshape(toks, quarter)
    trunk = exchange(jnp.broadcast_to(part[None], (n_x, toks, quarter)), "x")

    chip = ylo * lax.axis_size("z") + z
    per_quarter = quarter // pair
    block = yhi * n_plane + chip
    pre = bias_pair[:, None]
    for q in range(n_x):
        pre = pre + dot(res_pair[:, q * quarter : (q + 1) * quarter], trunk[q], ((1,), (1,)))
    own_cols = lax.dynamic_slice(
        trunk, (block // per_quarter, 0, (block % per_quarter) * pair), (1, toks, pair)
    )[0].T
    hidden = (own_cols.astype(f32) + jax.nn.silu(pre)).astype(bf16)
    hidden_half = exchange(
        jnp.broadcast_to(hidden[None], (n_plane, pair, toks)), plane
    ).reshape(half, toks)

    logits_own = dot(hidden_half, lm_own, ((0,), (0,)))
    logits_other = dot(hidden_half, lm_other, ((0,), (0,)))
    logits_own = logits_own + swap(logits_own, "yhi")
    logits_other = logits_other + swap(logits_other, "yhi")
    top = jnp.maximum(jnp.max(logits_own, axis=1), jnp.max(logits_other, axis=1))
    exp_own = jnp.exp(logits_own - top[:, None])
    exp_other = jnp.exp(logits_other - top[:, None])
    total = jnp.sum(exp_own, axis=1) + jnp.sum(exp_other, axis=1)
    stats = jnp.stack([top, total])
    stats = exchange(jnp.broadcast_to(stats[None], (n_plane, 2, toks)), plane)
    all_top = jnp.max(stats[:, 0], axis=0)
    all_total = jnp.sum(stats[:, 1] * jnp.exp(stats[:, 0] - all_top[None]), axis=0)

    def own_tokens(values):
        values = lax.dynamic_slice_in_dim(values, head + 1, 2 * toks)
        values = values.reshape(n_plane, 2, toks // n_plane)
        return lax.dynamic_index_in_dim(values, core, 1, keepdims=False).reshape(toks)

    tok_ids = own_tokens(next_ids)
    live = own_tokens(valid_mask).astype(f32)
    scale = loss_scale * jnp.power(jnp.float32(0.8), head.astype(f32)) * live
    ratio = scale * jnp.exp(top - all_top) / all_total
    lanes = lax.broadcasted_iota(jnp.int32, (1, vocab_width), 1)

    def grad_of(exps, owner):
        local = tok_ids - (chip * 2 + owner) * vocab_width
        onehot = (local[:, None] == lanes).astype(f32)
        return (ratio[:, None] * exps - scale[:, None] * onehot).astype(bf16)

    grad_own = grad_of(exp_own, core)
    grad_other = grad_of(exp_other, 1 - core)

    part_grad = dot(lm_own, grad_own, ((1,), (1,))) + dot(lm_other, grad_other, ((1,), (1,)))
    parts = exchange(part_grad.astype(bf16).reshape(n_plane, pair, toks), plane)
    hidden_grad = jnp.sum(parts.astype(f32), axis=0)
    pre_grad = hidden_grad * silu_grad(pre)
    pre_round = pre_grad.astype(bf16)

    outs = [
        dot(pre_round, res_pair[:, q * quarter : (q + 1) * quarter], ((0,), (0,)))
        for q in range(n_x)
    ]
    partial = jnp.stack(outs)
    spot = (block // per_quarter, 0, (block % per_quarter) * pair)
    direct = lax.dynamic_slice(partial, spot, (1, toks, pair)) + hidden_grad.T[None]
    partial = lax.dynamic_update_slice(partial, direct, spot).astype(bf16)
    by_x = jnp.sum(exchange(partial, "x").astype(f32), axis=0).astype(bf16)
    by_plane = exchange(by_x.reshape(n_all, rows, quarter), plane_all)
    summed = jnp.sum(by_plane.astype(f32), axis=0)
    quarters = exchange(jnp.broadcast_to(summed[None], (n_x, rows, quarter)), "x")
    trunk_grad = quarters.transpose(1, 0, 2).reshape(rows, width)

    hidden_both = jnp.concatenate([hidden_half, swap(hidden_half, "core")], 1)
    grad_both = jnp.concatenate([grad_own, swap(grad_other, "core")], 0)
    lm_grad = dot(hidden_both, grad_both, ((1,), (0,))).astype(bf16)
    pre_own = lax.dynamic_slice_in_dim(pre_grad, core * cols, cols, 0)
    pre_sibling = swap(lax.dynamic_slice_in_dim(pre_grad, (1 - core) * cols, cols, 0), "core")
    bias_grad = jnp.sum(pre_own, axis=1) + jnp.sum(pre_sibling, axis=1)
    pre_both = jnp.concatenate([pre_own, pre_sibling], 1).astype(bf16)
    trunk_both = jnp.concatenate([trunk, swap(trunk, "core")], 1)
    res_grad = jnp.concatenate(
        [dot(pre_both, trunk_both[q], ((1,), (0,))) for q in range(n_x)], 1
    ).astype(bf16)
    return (trunk_grad, res_grad.T[None], bias_grad[None], lm_grad[None])


def solution(mesh):
    fine = Mesh(mesh.devices.reshape(4, 2, 8, 2, 2), ("x", "ylo", "z", "core", "yhi"))
    vocab = ("ylo", "z", "core")
    in_specs = (
        P((*vocab, "yhi"), None),
        P("x", None, ("yhi", *vocab)),
        P("x", ("yhi", *vocab)),
        P("x", "yhi", vocab),
        P(),
        P(),
    )
    out_specs = (
        P((*vocab, "yhi"), None),
        P("x", None, ("yhi", *vocab)),
        P("x", ("yhi", *vocab)),
        P("x", "yhi", vocab),
    )
    return jax.shard_map(
        on_device, mesh=fine, in_specs=in_specs, out_specs=out_specs, check_vma=False
    )
```

time: 968 us -> 220 us (0.23)
  the two profiles are of different devices: /device:TPU:72 before, /device:TPU:6 now
where the time goes in v1:
time: 220 us; the launch traced here: 218 us
  waiting for transfers between devices  76.5 us (35%)
  starting transfers between devices  52.4 us (24%)
  matrix products  33.9 us (15%)
  blocking collectives  25.2 us (11%)
  other arithmetic  15 us (7%)
  local copies, waits for them, and re-layouts  13.9 us (6%)
    all_to_all x7, waiting for transfers between devices, exchange(): return lax.all_to_all(value, axes, 0, 0, tiled=True)  66.9 us
    all_to_all x7, starting transfers between devices, exchange(): return lax.all_to_all(value, axes, 0, 0, tiled=True)  47.4 us
    dot_general x17, matrix products, dot(): lax.dot_general(a, b, ((contract[0], contract[1]), ((), ())), preferred_e...  33.9 us
    all_to_all x1, blocking collectives, exchange(): return lax.all_to_all(value, axes, 0, 0, tiled=True)  25.2 us
    ppermute x9, waiting for transfers between devices, swap(): return lax.ppermute(value, axis, [(0, 1), (1, 0)])  9.57 us
    ppermute x9, starting transfers between devices, swap(): return lax.ppermute(value, axis, [(0, 1), (1, 0)])  5.01 us
  transfers between devices with their start and end apart: 16, of which 11 were waited for; matrix products, arithmetic and copies ran while one was open for 26% of the time, Pallas kernels for 0%

profile of v1, /device:TPU:6, one launch (start us, length us, event | category | flops | bytes accessed | tf_op | source)
XLA Modules:
  0.0 218.0 jit_solution(9868359028777533677)
XLA Ops:
  2.3 11.5 %all-to-all-start = ((bf16[32,4,1664]{2,1,0:T(4,128)(2,1)}), bf16[32,4,1664]{2,1,0:T(4,128)(2,1)S(1)}, u32[]{:S(2)}, u32[]{:S(2)}) async-start(bf16[32,4,1664]{2,1,0:T(4,128)(2,1)} %broadcast_in_dim.18), calls=%async_computation | async-start | bytes 851968 | tf_op jit(solution)/shard_map/all_to_all | solution.py:24
  16.3 13.2 %all-to-all-done = bf16[32,4,1664]{2,1,0:T(4,128)(2,1)S(1)} async-done(((bf16[32,4,1664]{2,1,0:T(4,128)(2,1)}), bf16[32,4,1664]{2,1,0:T(4,128)(2,1)S(1)}, u32[]{:S(2)}, u32[]{:S(2)}) %all-to-all-start) | async-done | bytes 426016 | tf_op jit(solution)/shard_map/all_to_all | solution.py:24
  31.3 4.9 %all-to-all-start.1 = ((bf16[4,128,1664]{1,2,0:T(8,128)(2,1)}), bf16[4,128,1664]{1,2,0:T(8,128)(2,1)S(1)}, u32[]{:S(2)}, u32[]{:S(2)}) async-start(bf16[4,128,1664]{1,2,0:T(8,128)(2,1)} %broadcast_in_dim.20), calls=%async_computation.1 | async-start | bytes 3407872 | tf_op jit(solution)/shard_map/all_to_all | solution.py:24
  39.0 15.5 %all-to-all-done.1 = bf16[4,128,1664]{1,2,0:T(8,128)(2,1)S(1)} async-done(((bf16[4,128,1664]{1,2,0:T(8,128)(2,1)}), bf16[4,128,1664]{1,2,0:T(8,128)(2,1)S(1)}, u32[]{:S(2)}, u32[]{:S(2)}) %all-to-all-start.1) | async-done | bytes 1703968 | tf_op jit(solution)/shard_map/all_to_all | solution.py:24
  57.9 25.2 %all_to_all.40 = bf16[16,208,128]{2,1,0:T(8,128)(2,1)S(1)} all-to-all(bf16[16,208,128]{2,1,0:T(8,128)(2,1)S(1)} %broadcast_in_dim.21), channel_id=1, replica_groups=mesh['x'=4,'ylo'=2,'z'=8,'core'=2,'yhi'=2] {'ylo','z'}, dimensions={0} | all-to-all | bytes 1703936 | tf_op jit(solution)/shard_map/all_to_all | solution.py:24
  83.1 3.1 %fusion.24 = f32[128,640]{1,0:T(8,128)S(1)} fusion(bf16[3328,128]{1,0:T(8,128)(2,1)S(1)} %bitcast.107, bf16[1,3328,640]{2,1,0:T(8,128)(2,1)} %param.9), kind=kOutput, calls=%fused_computation.85 | convolution fusion | flops 545259520 | bytes 5439488 | tf_op jit(solution)/shard_map/dot_general | solution.py:28
  86.2 1.6 collective-permute-start.2
  87.8 3.1 %fusion.31 = f32[128,640]{1,0:T(8,128)S(1)} fusion(bf16[3328,128]{1,0:T(8,128)(2,1)S(1)} %bitcast.108, bf16[3328,640]{1,0:T(8,128)(2,1)} %collective-permute-done.3), kind=kOutput, calls=%fused_computation.92 | convolution fusion | flops 545259520 | bytes 5439488 | tf_op jit(solution)/shard_map/dot_general | solution.py:28
  90.9 2.1 collective-permute-start.4
  93.0 4.4 %collective-permute-done.2 = f32[128,640]{1,0:T(8,128)S(1)} collective-permute-done((f32[128,640]{1,0:T(8,128)S(1)}, f32[128,640]{1,0:T(8,128)S(1)}, u32[]{:S(2)}, u32[]{:S(2)}) %collective-permute-start.2) | collective-permute-done | bytes 327712 | tf_op jit(solution)/shard_map/ppermute | solution.py:20
  97.5 3.4 %collective-permute-done.4 = f32[128,640]{1,0:T(8,128)S(1)} collective-permute-done((f32[128,640]{1,0:T(8,128)S(1)}, f32[128,640]{1,0:T(8,128)S(1)}, u32[]{:S(2)}, u32[]{:S(2)}) %collective-permute-start.4) | collective-permute-done | bytes 327712 | tf_op jit(solution)/shard_map/ppermute | solution.py:20
  102.4 7.1 %all-to-all-start.3 = ((f32[16,2,128]{2,1,0:T(2,128)}), f32[16,2,128]{2,1,0:T(2,128)S(1)}, u32[]{:S(2)}, u32[]{:S(2)}) async-start(f32[16,2,128]{2,1,0:T(2,128)} %broadcast_in_dim.22), calls=%async_computation.3 | async-start | bytes 32768 | tf_op jit(solution)/shard_map/all_to_all | solution.py:24
  110.4 7.6 %all-to-all-done.3 = f32[16,2,128]{2,1,0:T(2,128)S(1)} async-done(((f32[16,2,128]{2,1,0:T(2,128)}), f32[16,2,128]{2,1,0:T(2,128)S(1)}, u32[]{:S(2)}, u32[]{:S(2)}) %all-to-all-start.3) | async-done | bytes 16416 | tf_op jit(solution)/shard_map/all_to_all | solution.py:24
  118.0 2.0 subtract_convert_fusion
  120.0 3.5 %fusion.22 = f32[128,3328]{1,0:T(8,128)S(1)} fusion(bf16[128,640]{1,0:T(8,128)(2,1)S(1)} %get-tuple-element.29, bf16[1,3328,640]{2,1,0:T(8,128)(2,1)} %param.9), kind=kOutput, calls=%fused_computation.83 | convolution fusion | flops 545259520 | bytes 6127616 | tf_op jit(solution)/shard_map/dot_general | solution.py:28
  123.5 4.5 %fusion.2 = bf16[3328,128]{0,1:T(8,128)(2,1)} fusion(f32[128,3328]{1,0:T(8,128)S(1)} %fusion.22, bf16[128,640]{1,0:T(8,128)(2,1)} %get-tuple-element.28, bf16[3328,640]{1,0:T(8,128)(2,1)} %collective-permute-done.3), kind=kOutput, calls=%fused_computation.4 | convolution fusion | flops 546111488 | bytes 6979584 | tf_op jit(solution)/shard_map/dot_general | solution.py:28
  128.1 2.2 %copy.47 = bf16[3328,128]{1,0:T(8,128)(2,1)} copy(bf16[3328,128]{0,1:T(8,128)(2,1)} %fusion.2) | data formatting | bytes 1703936 | tf_op jit(solution)/shard_map/convert_element_type | solution.py:110
  130.2 4.3 %all-to-all-start.4 = ((bf16[16,208,128]{2,1,0:T(8,128)(2,1)}), bf16[16,208,128]{2,1,0:T(8,128)(2,1)}, u32[]{:S(2)}, u32[]{:S(2)}) async-start(bf16[16,208,128]{2,1,0:T(8,128)(2,1)} %bitcast.111), calls=%async_computation.4 | async-start | bytes 1703936 | tf_op jit(solution)/shard_map/all_to_all | solution.py:24
  135.9 2.8 %constant_dynamic-update-slice_fusion = bf16[4,256,1664]{1,2,0:T(8,128)(2,1)} fusion(bf16[4,256,1664]{1,2,0:T(8,128)(2,1)} %constant_dynamic-update-slice_fusion.1, bf16[4,128,1664]{1,2,0:T(8,128)(2,1)} %collective-permute-done.6), kind=kLoop, calls=%fused_computation.70 | loop fusion | bytes 3407872 | tf_op jit(solution)/shard_map/concatenate | solution.py:136
  139.2 15.2 %all-to-all-done.4 = bf16[16,208,128]{2,1,0:T(8,128)(2,1)} async-done(((bf16[16,208,128]{2,1,0:T(8,128)(2,1)}), bf16[16,208,128]{2,1,0:T(8,128)(2,1)}, u32[]{:S(2)}, u32[]{:S(2)}) %all-to-all-start.4) | async-done | bytes 852000 | tf_op jit(solution)/shard_map/all_to_all | solution.py:24
  155.7 1.6 fusion.26
  158.8 1.6 convolution_bitcast_fusion.1
  163.1 5.6 %all-to-all-start.5 = ((bf16[4,128,1664]{1,2,0:T(8,128)(2,1)}), bf16[4,128,1664]{1,2,0:T(8,128)(2,1)S(1)}, u32[]{:S(2)}, u32[]{:S(2)}) async-start(bf16[4,128,1664]{1,2,0:T(8,128)(2,1)} %convert_element_type.79), calls=%async_computation.5 | async-start | bytes 3407872 | tf_op jit(solution)/shard_map/all_to_all | solution.py:24
  168.7 4.7 %fusion = bf16[1,3328,640]{2,1,0:T(8,128)(2,1)} fusion(bf16[3328,128]{1,0:T(8,128)(2,1)} %collective-permute-done.7, bf16[3328,128]{1,0:T(8,128)(2,1)S(1)} %bitcast.110, bf16[128,640]{1,0:T(8,128)(2,1)} %collective-permute-done.8, bf16[128,640]{1,0:T(8,128)(2,1)S(1)} %get-tuple-element.29), kind=kOutput, calls=%fused_computation.1 | convolution fusion | flops 1096712192 | bytes 6291456 | tf_op jit(solution)/shard_map/dot_general | solution.py:28
  176.5 2.3 %convolution_convert_fusion.2 = bf16[104,1664]{1,0:T(8,128)(2,1)} fusion(bf16[4,256,1664]{1,2,0:T(8,128)(2,1)} %constant_dynamic-update-slice_fusion, bf16[104,128]{1,0:T(8,128)(2,1)S(1)} %get-tuple-element.25, bf16[104,128]{1,0:T(8,128)(2,1)S(1)} %dynamic-slice_convert_fusion), kind=kOutput, calls=%fused_computation.17 | convolution fusion | flops 88884224 | bytes 1251328 | tf_op jit(solution)/shard_map/dot_general | solution.py:28
  178.8 2.3 %convolution_convert_fusion.3 = bf16[104,1664]{1,0:T(8,128)(2,1)} fusion(bf16[4,256,1664]{1,2,0:T(8,128)(2,1)} %constant_dynamic-update-slice_fusion, bf16[104,128]{1,0:T(8,128)(2,1)S(1)} %get-tuple-element.25, bf16[104,128]{1,0:T(8,128)(2,1)S(1)} %dynamic-slice_convert_fusion), kind=kOutput, calls=%fused_computation.18 | convolution fusion | flops 88884224 | bytes 1251328 | tf_op jit(solution)/shard_map/dot_general | solution.py:28
  181.1 2.3 %all-to-all-done.5 = bf16[4,128,1664]{1,2,0:T(8,128)(2,1)S(1)} async-done(((bf16[4,128,1664]{1,2,0:T(8,128)(2,1)}), bf16[4,128,1664]{1,2,0:T(8,128)(2,1)S(1)}, u32[]{:S(2)}, u32[]{:S(2)}) %all-to-all-start.5) | async-done | bytes 1703968 | tf_op jit(solution)/shard_map/all_to_all | solution.py:24
  185.1 8.7 %all-to-all-start.6 = ((bf16[32,4,1664]{2,1,0:T(4,128)(2,1)}), bf16[32,4,1664]{2,1,0:T(4,128)(2,1)S(1)}, u32[]{:S(2)}, u32[]{:S(2)}) async-start(bf16[32,4,1664]{2,1,0:T(4,128)(2,1)} %reshape.124), calls=%async_computation.6 | async-start | bytes 851968 | tf_op jit(solution)/shard_map/all_to_all | solution.py:24
  195.3 2.2 maximum_bitcast_fusion
  197.5 9.9 %all-to-all-done.6 = bf16[32,4,1664]{2,1,0:T(4,128)(2,1)S(1)} async-done(((bf16[32,4,1664]{2,1,0:T(4,128)(2,1)}), bf16[32,4,1664]{2,1,0:T(4,128)(2,1)S(1)}, u32[]{:S(2)}, u32[]{:S(2)}) %all-to-all-start.6) | async-done | bytes 426016 | tf_op jit(solution)/shard_map/all_to_all | solution.py:24
  208.2 5.4 %all-to-all-start.7 = ((f32[4,4,1664]{2,1,0:T(4,128)}), f32[4,4,1664]{2,1,0:T(4,128)S(1)}, u32[]{:S(2)}, u32[]{:S(2)}) async-start(f32[4,4,1664]{2,1,0:T(4,128)} %broadcast_in_dim.24), calls=%async_computation.7 | async-start | bytes 212992 | tf_op jit(solution)/shard_map/all_to_all | solution.py:24
  214.1 3.3 %all-to-all-done.7 = f32[4,4,1664]{2,1,0:T(4,128)S(1)} async-done(((f32[4,4,1664]{2,1,0:T(4,128)}), f32[4,4,1664]{2,1,0:T(4,128)S(1)}, u32[]{:S(2)}, u32[]{:S(2)}) %all-to-all-start.7) | async-done | bytes 106528 | tf_op jit(solution)/shard_map/all_to_all | solution.py:24
  (91 shorter events, 30.2 us)
Async XLA Ops:
  0.6 0.8 copy-start
  0.6 35.6 %collective-permute-start.1 = (bf16[104,6656]{1,0:T(8,128)(2,1)}, bf16[104,6656]{1,0:T(8,128)(2,1)}, u32[]{:S(2)}, u32[]{:S(2)}) collective-permute-start(bf16[104,6656]{1,0:T(8,128)(2,1)} %bitcast.112), channel_id=1, source_target_pairs={{0,2},{2,0},{1,3},{3,1},{4,6},{6,4},{5,7},{7,5},{8,10},{10,8},{9,1... | collective-permute-start | bytes 4153352 | tf_op jit(solution)/shard_map/ppermute | solution.py:20
  2.3 27.2 %all-to-all-start = ((bf16[32,4,1664]{2,1,0:T(4,128)(2,1)}), bf16[32,4,1664]{2,1,0:T(4,128)(2,1)S(1)}, u32[]{:S(2)}, u32[]{:S(2)}) async-start(bf16[32,4,1664]{2,1,0:T(4,128)(2,1)} %broadcast_in_dim.18), calls=%async_computation | async-start | bytes 851968 | tf_op jit(solution)/shard_map/all_to_all | solution.py:24
  14.5 1.1 collective-permute-start
  14.5 73.3 %collective-permute-start.3 = (bf16[3328,640]{1,0:T(8,128)(2,1)}, bf16[3328,640]{1,0:T(8,128)(2,1)}, u32[]{:S(2)}, u32[]{:S(2)}) collective-permute-start(bf16[3328,640]{1,0:T(8,128)(2,1)} %bitcast.106), channel_id=1, source_target_pairs={{0,2},{2,0},{1,3},{3,1},{4,6},{6,4},{5,7},{7,5},{8,10},{10,8},{9,1... | collective-permute-start | bytes 12779528 | tf_op jit(solution)/shard_map/ppermute | solution.py:20
  31.3 4.9 %copy-start.6 = (bf16[1,6656,104]{1,2,0:T(8,128)(2,1)S(1)}, bf16[1,6656,104]{1,2,0:T(8,128)(2,1)}, u32[]{:S(2)}) copy-start(bf16[1,6656,104]{1,2,0:T(8,128)(2,1)} %param.7) | copy-start | bytes 4153348
  31.3 23.2 %all-to-all-start.1 = ((bf16[4,128,1664]{1,2,0:T(8,128)(2,1)}), bf16[4,128,1664]{1,2,0:T(8,128)(2,1)S(1)}, u32[]{:S(2)}, u32[]{:S(2)}) async-start(bf16[4,128,1664]{1,2,0:T(8,128)(2,1)} %broadcast_in_dim.20), calls=%async_computation.1 | async-start | bytes 3407872 | tf_op jit(solution)/shard_map/all_to_all | solution.py:24
  39.0 18.7 %copy-start.1 = (bf16[208,1664]{1,0:T(8,128)(2,1)}, bf16[208,1664]{1,0:T(8,128)(2,1)S(1)}, u32[]{:S(2)}) copy-start(bf16[208,1664]{1,0:T(8,128)(2,1)S(1)} %get-tuple-element.17) | copy-start | bytes 2076676
  54.5 2.2 %copy-start.5 = (bf16[208,1664]{1,0:T(8,128)(2,1)S(1)}, bf16[208,1664]{1,0:T(8,128)(2,1)}, u32[]{:S(2)}) copy-start(bf16[208,1664]{1,0:T(8,128)(2,1)} %get-tuple-element.18) | copy-start | bytes 2076676
  86.2 23.3 %copy-start.9 = (s32[260]{0:T(512)S(1)}, s32[260]{0:T(512)}, u32[]{:S(2)}) copy-start(s32[260]{0:T(512)} %param.10) | copy-start | bytes 3124
  86.2 23.6 %copy-start.10 = (s32[260]{0:T(512)S(1)}, s32[260]{0:T(512)}, u32[]{:S(2)}) copy-start(s32[260]{0:T(512)} %param.11) | copy-start | bytes 3124
  86.2 11.1 %collective-permute-start.2 = (f32[128,640]{1,0:T(8,128)S(1)}, f32[128,640]{1,0:T(8,128)S(1)}, u32[]{:S(2)}, u32[]{:S(2)}) collective-permute-start(f32[128,640]{1,0:T(8,128)S(1)} %fusion.24), channel_id=1, source_target_pairs={{0,1},{1,0},{2,3},{3,2},{4,5},{5,4},{6,7},{7,6},{8,9},{9,8},{10,11... | collective-permute-start | bytes 983048 | tf_op jit(solution)/shard_map/ppermute | solution.py:20
  90.9 10.0 %collective-permute-start.4 = (f32[128,640]{1,0:T(8,128)S(1)}, f32[128,640]{1,0:T(8,128)S(1)}, u32[]{:S(2)}, u32[]{:S(2)}) collective-permute-start(f32[128,640]{1,0:T(8,128)S(1)} %fusion.31), channel_id=1, source_target_pairs={{0,1},{1,0},{2,3},{3,2},{4,5},{5,4},{6,7},{7,6},{8,9},{9,8},{10,11... | collective-permute-start | bytes 983048 | tf_op jit(solution)/shard_map/ppermute | solution.py:20
  97.5 3.5 %copy-start.3 = (f32[128,640]{1,0:T(8,128)}, f32[128,640]{1,0:T(8,128)S(1)}, u32[]{:S(2)}) copy-start(f32[128,640]{1,0:T(8,128)S(1)} %get-tuple-element.13) | copy-start | bytes 983044
  101.0 0.7 copy-start.4
  102.4 15.6 %all-to-all-start.3 = ((f32[16,2,128]{2,1,0:T(2,128)}), f32[16,2,128]{2,1,0:T(2,128)S(1)}, u32[]{:S(2)}, u32[]{:S(2)}) async-start(f32[16,2,128]{2,1,0:T(2,128)} %broadcast_in_dim.22), calls=%async_computation.3 | async-start | bytes 32768 | tf_op jit(solution)/shard_map/all_to_all | solution.py:24
  110.3 25.6 %collective-permute-start.6 = (bf16[4,128,1664]{1,2,0:T(8,128)(2,1)S(1)}, bf16[4,128,1664]{1,2,0:T(8,128)(2,1)}, u32[]{:S(2)}, u32[]{:S(2)}) collective-permute-start(bf16[4,128,1664]{1,2,0:T(8,128)(2,1)S(1)} %all-to-all-done.1), channel_id=1, source_target_pairs={{0,2},{2,0},{1,3},{3,1},{4,6},{6,4},{5,7},{7,5},{8,10},{10,8},{9,1... | collective-permute-start | bytes 5111816 | tf_op jit(solution)/shard_map/ppermute | solution.py:20
  130.2 24.1 %all-to-all-start.4 = ((bf16[16,208,128]{2,1,0:T(8,128)(2,1)}), bf16[16,208,128]{2,1,0:T(8,128)(2,1)}, u32[]{:S(2)}, u32[]{:S(2)}) async-start(bf16[16,208,128]{2,1,0:T(8,128)(2,1)} %bitcast.111), calls=%async_computation.4 | async-start | bytes 1703936 | tf_op jit(solution)/shard_map/all_to_all | solution.py:24
  135.9 32.8 %collective-permute-start.7 = (bf16[3328,128]{1,0:T(8,128)(2,1)S(1)}, bf16[3328,128]{1,0:T(8,128)(2,1)}, u32[]{:S(2)}, u32[]{:S(2)}) collective-permute-start(bf16[3328,128]{1,0:T(8,128)(2,1)S(1)} %bitcast.109), channel_id=1, source_target_pairs={{0,2},{2,0},{1,3},{3,1},{4,6},{6,4},{5,7},{7,5},{8,10},{10,8},{9,1... | collective-permute-start | bytes 2555912 | tf_op jit(solution)/shard_map/ppermute | solution.py:20
  138.7 21.7 %copy-start.2 = (bf16[208,1664]{1,0:T(8,128)(2,1)S(1)}, bf16[208,1664]{1,0:T(8,128)(2,1)}, u32[]{:S(2)}) copy-start(bf16[208,1664]{1,0:T(8,128)(2,1)} %copy-done.1) | copy-start | bytes 2076676
  138.7 30.0 %collective-permute-start.8 = (bf16[128,640]{1,0:T(8,128)(2,1)}, bf16[128,640]{1,0:T(8,128)(2,1)}, u32[]{:S(2)}, u32[]{:S(2)}) collective-permute-start(bf16[128,640]{1,0:T(8,128)(2,1)} %get-tuple-element.28), channel_id=1, source_target_pairs={{0,2},{2,0},{1,3},{3,1},{4,6},{6,4},{5,7},{7,5},{8,10},{10,8},{9,1... | collective-permute-start | bytes 491528 | tf_op jit(solution)/shard_map/ppermute | solution.py:20
  163.1 20.4 %all-to-all-start.5 = ((bf16[4,128,1664]{1,2,0:T(8,128)(2,1)}), bf16[4,128,1664]{1,2,0:T(8,128)(2,1)S(1)}, u32[]{:S(2)}, u32[]{:S(2)}) async-start(bf16[4,128,1664]{1,2,0:T(8,128)(2,1)} %convert_element_type.79), calls=%async_computation.5 | async-start | bytes 3407872 | tf_op jit(solution)/shard_map/all_to_all | solution.py:24
  168.7 4.8 %copy-start.8 = (f32[208,128]{1,0:T(8,128)S(1)}, f32[208,128]{1,0:T(8,128)}, u32[]{:S(2)}) copy-start(f32[208,128]{1,0:T(8,128)} %get-tuple-element.9) | copy-start | bytes 319492
  173.5 1.3 collective-permute-start.5
  183.9 11.4 %copy-start.7 = (bf16[104,1664]{1,0:T(8,128)(2,1)S(1)}, bf16[104,1664]{1,0:T(8,128)(2,1)}, u32[]{:S(2)}) copy-start(bf16[104,1664]{1,0:T(8,128)(2,1)} %convolution_convert_fusion.3) | copy-start | bytes 1038340
  185.1 22.3 %all-to-all-start.6 = ((bf16[32,4,1664]{2,1,0:T(4,128)(2,1)}), bf16[32,4,1664]{2,1,0:T(4,128)(2,1)S(1)}, u32[]{:S(2)}, u32[]{:S(2)}) async-start(bf16[32,4,1664]{2,1,0:T(4,128)(2,1)} %reshape.124), calls=%async_computation.6 | async-start | bytes 851968 | tf_op jit(solution)/shard_map/all_to_all | solution.py:24
  208.2 9.1 %all-to-all-start.7 = ((f32[4,4,1664]{2,1,0:T(4,128)}), f32[4,4,1664]{2,1,0:T(4,128)S(1)}, u32[]{:S(2)}, u32[]{:S(2)}) async-start(f32[4,4,1664]{2,1,0:T(4,128)} %broadcast_in_dim.24), calls=%async_computation.7 | async-start | bytes 212992 | tf_op jit(solution)/shard_map/all_to_all | solution.py:24

commit v2 on v1

v2 whole, which is shorter than its diff:
```python
import jax
import jax.numpy as jnp
from jax import lax
from jax.experimental import pallas as pl
from jax.experimental.pallas import tpu as pltpu
from jax.sharding import Mesh
from jax.sharding import PartitionSpec as P

loss_scale = 16.0
f32 = jnp.float32
bf16 = jnp.bfloat16
plane = ("ylo", "z")
plane_all = ("ylo", "z", "yhi")


def silu_grad(value):
    sigma = jax.nn.sigmoid(value)
    return sigma * (1.0 + value * (1.0 - sigma))


def swap(value, axis):
    return lax.ppermute(value, axis, [(0, 1), (1, 0)])


def exchange(value, axes):
    return lax.all_to_all(value, axes, 0, 0, tiled=True)


def dot(a, b, contract):
    return lax.dot_general(a, b, ((contract[0], contract[1]), ((), ())), preferred_element_type=f32)


def vocab_product(lm_a, lm_b, rows_a, rows_b, dtype):
    half, columns = lm_a.shape
    toks = rows_a.shape[0]
    step = half // 2

    def kernel(a_ref, b_ref, ra_ref, rb_ref, out_ref):
        total = dot(a_ref[...], ra_ref[...], ((1,), (1,)))
        total = total + dot(b_ref[...], rb_ref[...], ((1,), (1,)))
        out_ref[...] = total.astype(out_ref.dtype)

    weights = pl.BlockSpec((step, columns), lambda i: (i, 0))
    whole = pl.BlockSpec((toks, columns), lambda i: (0, 0))
    return pl.pallas_call(
        kernel,
        grid=(half // step,),
        in_specs=[weights, weights, whole, whole],
        out_specs=pl.BlockSpec((step, toks), lambda i: (i, 0)),
        out_shape=jax.ShapeDtypeStruct((half, toks), dtype),
        cost_estimate=pl.CostEstimate(
            flops=4 * half * columns * toks,
            bytes_accessed=4 * half * columns + 4 * half * toks,
            transcendentals=0,
        ),
        compiler_params=pltpu.CompilerParams(vmem_limit_bytes=24 * 2**20),
    )(lm_a, lm_b, rows_a, rows_b)


def combine(stats, own, product, target_cols):
    half, toks = product.shape
    step = half // 2

    def kernel(stats_ref, own_ref, product_ref, target_ref, out_ref, ratio_ref):
        tops, rests, targets = stats_ref[:, 0, :], stats_ref[:, 1, :], stats_ref[:, 2, :]
        top, scale = own_ref[0:1, :], own_ref[1:2, :]
        all_top = jnp.max(tops, axis=0, keepdims=True)
        weight = jnp.exp(tops - all_top)
        rest = jnp.sum(rests * weight, axis=0, keepdims=True)
        total = rest + jnp.sum(targets * weight, axis=0, keepdims=True)
        ratio = scale * jnp.exp(top - all_top) / total
        ratio_ref[...] = ratio
        value = product_ref[...] * ratio - target_ref[...].astype(f32) * (scale * rest / total)
        out_ref[...] = value.astype(out_ref.dtype)

    rows = pl.BlockSpec((step, toks), lambda i: (i, 0))
    return pl.pallas_call(
        kernel,
        grid=(half // step,),
        in_specs=[
            pl.BlockSpec(stats.shape, lambda i: (0, 0, 0)),
            pl.BlockSpec(own.shape, lambda i: (0, 0)),
            rows,
            rows,
        ],
        out_specs=[rows, pl.BlockSpec((1, toks), lambda i: (0, 0))],
        out_shape=[
            jax.ShapeDtypeStruct((half, toks), bf16),
            jax.ShapeDtypeStruct((1, toks), f32),
        ],
        cost_estimate=pl.CostEstimate(
            flops=4 * half * toks, bytes_accessed=8 * half * toks, transcendentals=0
        ),
    )(stats, own, product, target_cols)


def on_device(trunk_rows, res_weight, res_bias, lm_weight, next_ids, valid_mask):
    head = lax.axis_index("x")
    ylo, z, core, yhi = (lax.axis_index(a) for a in ("ylo", "z", "core", "yhi"))
    n_x = lax.axis_size("x")
    n_plane = lax.axis_size("ylo") * lax.axis_size("z")
    n_all = n_plane * lax.axis_size("yhi")
    rows, width = trunk_rows.shape
    toks = n_all * rows

    res_own = res_weight[0].T
    cols = res_own.shape[0]
    pair = 2 * cols
    lm_own = lm_weight[0]
    half, vocab_width = lm_own.shape
    res_other = swap(res_own, "core")
    lm_other = swap(lm_own, "core")
    first = core == 0
    res_pair = jnp.concatenate(
        [jnp.where(first, res_own, res_other), jnp.where(first, res_other, res_own)], 0
    )
    bias_own = res_bias[0].astype(f32)
    bias_other = swap(bias_own, "core")
    bias_pair = jnp.concatenate(
        [jnp.where(first, bias_own, bias_other), jnp.where(first, bias_other, bias_own)]
    )

    chip = ylo * lax.axis_size("z") + z
    block = yhi * n_plane + chip
    odd = head % 2
    half_cols = width // 2
    quarter = half_cols // 2
    iota_r = lax.broadcasted_iota(jnp.int32, (pair, half_cols), 0)
    iota_c = lax.broadcasted_iota(jnp.int32, (pair, half_cols), 1)

    def aug(side):
        weights = jnp.where(side == 0, res_pair[:, :half_cols], res_pair[:, half_cols:])
        select = (iota_r + block * pair == iota_c + side * half_cols).astype(bf16)
        return jnp.concatenate([weights, select], 0)

    near, far = aug(odd), aug(1 - odd)

    def shift(value, step):
        return lax.ppermute(value, "x", [(i, (i + step) % n_x) for i in range(n_x)])

    mine = lax.dynamic_slice_in_dim(trunk_rows, odd * half_cols, half_cols, 1)
    part = exchange(jnp.broadcast_to(mine[None], (n_all, rows, half_cols)), plane_all)
    part = part.reshape(toks, half_cols)

    def own_tokens(values):
        values = lax.dynamic_slice_in_dim(values, head + 1, 2 * toks)
        values = values.reshape(n_plane, 2, toks // n_plane)
        return lax.dynamic_index_in_dim(values, core, 1, keepdims=False).reshape(toks)

    tok_ids = own_tokens(next_ids)
    live = own_tokens(valid_mask).astype(f32)
    scale = loss_scale * jnp.power(jnp.float32(0.8), head.astype(f32)) * live
    lanes = lax.broadcasted_iota(jnp.int32, (1, vocab_width), 1)

    def onehot(owner):
        return (tok_ids - (chip * 2 + owner) * vocab_width)[:, None] == lanes

    hot_own, hot_other = onehot(core), onehot(1 - core)
    target_cols = vocab_product(
        lm_own, lm_other, hot_own.astype(bf16), hot_other.astype(bf16), bf16
    )
    from_right = shift(part[:, :quarter], -1)
    from_left = shift(part[:, quarter:], 1)

    both = dot(near, part, ((1,), (1,)))
    both = both + dot(far[:, :quarter], from_right, ((1,), (1,)))
    both = both + dot(far[:, quarter:], from_left, ((1,), (1,)))
    pre = both[:pair] + bias_pair[:, None]
    hidden = (both[pair:] + jax.nn.silu(pre)).astype(bf16)
    hidden_half = exchange(
        jnp.broadcast_to(hidden[None], (n_plane, pair, toks)), plane
    ).reshape(half, toks)
    target_cols, hidden_half = lax.optimization_barrier((target_cols, hidden_half))

    logits_own = dot(hidden_half, lm_own, ((0,), (0,)))
    logits_other = dot(hidden_half, lm_other, ((0,), (0,)))
    logits_own = logits_own + swap(logits_own, "yhi")
    logits_other = logits_other + swap(logits_other, "yhi")
    top = jnp.maximum(jnp.max(logits_own, axis=1), jnp.max(logits_other, axis=1))
    exp_own = jnp.exp(logits_own - top[:, None])
    exp_other = jnp.exp(logits_other - top[:, None])
    rest_own = jnp.where(hot_own, 0.0, exp_own)
    rest_other = jnp.where(hot_other, 0.0, exp_other)
    rest = jnp.sum(rest_own, axis=1) + jnp.sum(rest_other, axis=1)
    at_target = jnp.sum(jnp.where(hot_own, exp_own, 0.0), axis=1) + jnp.sum(
        jnp.where(hot_other, exp_other, 0.0), axis=1
    )
    stats = jnp.stack([top, rest, at_target])
    stats = exchange(jnp.broadcast_to(stats[None], (n_plane, 3, toks)), plane)
    part_grad = vocab_product(
        lm_own, lm_other, rest_own.astype(bf16), rest_other.astype(bf16), f32
    )
    part_grad, ratio = combine(stats, jnp.stack([top, scale]), part_grad, target_cols)
    ratio = ratio[0]
    parts = exchange(part_grad.reshape(n_plane, pair, toks), plane)
    hidden_grad = jnp.sum(parts.astype(f32), axis=0)
    pre_grad = hidden_grad * silu_grad(pre)
    pre_round = pre_grad.astype(bf16)

    both_grad = jnp.concatenate([pre_round, hidden_grad.astype(bf16)], 0)
    keep = dot(both_grad, near, ((0,), (0,)))
    give_left = dot(both_grad, far[:, :quarter], ((0,), (0,))).astype(bf16)
    give_right = dot(both_grad, far[:, quarter:], ((0,), (0,))).astype(bf16)
    got_left = shift(give_right, 1)
    got_right = shift(give_left, -1)
    by_x = jnp.concatenate(
        [keep[:, :quarter] + got_right.astype(f32), keep[:, quarter:] + got_left.astype(f32)], 1
    ).astype(bf16)
    by_plane = exchange(by_x.reshape(n_all, rows, half_cols), plane_all)
    summed = jnp.sum(by_plane.astype(f32), axis=0)
    here = summed + shift(summed, 2)
    there = shift(summed, 1) + shift(summed, -1)
    trunk_grad = jnp.concatenate(
        [jnp.where(odd == 0, here, there), jnp.where(odd == 0, there, here)], 1
    )

    def grad_of(exps, hot):
        return jnp.where(hot, ratio[:, None] * exps - scale[:, None], ratio[:, None] * exps).astype(
            bf16
        )

    grad_own = grad_of(exp_own, hot_own)
    grad_other = grad_of(exp_other, hot_other)
    hidden_both = jnp.concatenate([hidden_half, swap(hidden_half, "core")], 1)
    grad_both = jnp.concatenate([grad_own, swap(grad_other, "core")], 0)
    lm_grad = dot(hidden_both, grad_both, ((1,), (0,))).astype(bf16)
    pre_own = lax.dynamic_slice_in_dim(pre_grad, core * cols, cols, 0)
    pre_sibling = swap(lax.dynamic_slice_in_dim(pre_grad, (1 - core) * cols, cols, 0), "core")
    bias_grad = jnp.sum(pre_own, axis=1) + jnp.sum(pre_sibling, axis=1)
    pre_both = jnp.concatenate([pre_own, pre_sibling], 1).astype(bf16)

    def with_sibling(value):
        return jnp.concatenate([value, swap(value, "core")], 0)

    res_near = dot(pre_both, with_sibling(part), ((1,), (0,))).astype(bf16)
    res_far = jnp.concatenate(
        [dot(pre_both, with_sibling(v), ((1,), (0,))) for v in (from_right, from_left)], 1
    ).astype(bf16)
    res_grad = jnp.concatenate(
        [jnp.where(odd == 0, res_near, res_far), jnp.where(odd == 0, res_far, res_near)], 1
    )
    return (trunk_grad, res_grad.T[None], bias_grad[None], lm_grad[None])


def solution(mesh):
    fine = Mesh(mesh.devices.reshape(4, 2, 8, 2, 2), ("x", "ylo", "z", "core", "yhi"))
    vocab = ("ylo", "z", "core")
    in_specs = (
        P((*vocab, "yhi"), None),
        P("x", None, ("yhi", *vocab)),
        P("x", ("yhi", *vocab)),
        P("x", "yhi", vocab),
        P(),
        P(),
    )
    out_specs = (
        P((*vocab, "yhi"), None),
        P("x", None, ("yhi", *vocab)),
        P("x", ("yhi", *vocab)),
        P("x", "yhi", vocab),
    )
    return jax.shard_map(
        on_device, mesh=fine, in_specs=in_specs, out_specs=out_specs, check_vma=False
    )
```

time: 220 us -> 207 us (0.941)
  blocking collectives: 25.2 us -> 0 us
  matrix products: 33.9 us -> 19.1 us
  Pallas kernels: 0 us -> 11.2 us
  waiting for transfers between devices: 76.5 us -> 86.6 us
  other arithmetic: 15 us -> 19.1 us
    all_to_all x1 -> x0, blocking collectives: 25.2 us -> none  [exchange(): return lax.all_to_all(value, axes, 0, 0, tiled=True)]
    dot_general x17 -> x12, matrix products: 33.9 us -> 19.1 us  [dot(): lax.dot_general(a, b, ((contract[0], contract[1]), ((), ())), preferred_e...]
    ppermute x0 -> x7, waiting for transfers between devices: none -> 13.7 us  [shift(): return lax.ppermute(value, 'x', [(i, (i + step) % n_x) for i in range(n_x)])]
    pallas_call x0 -> x3, Pallas kernels: none -> 11.2 us  [the longest x2 8.63 us: vocab_product(): pl.pallas_call(kernel, grid=(half // step,), in_specs=[weights, weights,...]
    all_to_all x7 -> x5, starting transfers between devices: 47.4 us -> 39.2 us  [exchange(): return lax.all_to_all(value, axes, 0, 0, tiled=True)]
    unnamed x24 -> x56, local copies, waits for them, and re-layouts: 3.17 us -> 11 us
    ppermute x0 -> x7, starting transfers between devices: none -> 6.44 us  [shift(): return lax.ppermute(value, 'x', [(i, (i + step) % n_x) for i in range(n_x)])]
    concatenate x1 -> x2, local copies, waits for them, and re-layouts: 2.79 us -> 0.21 us  [on_device(): jnp.concatenate([keep[:, :quarter] + got_right.astype(f32), keep[:, quart...]
  transfers between devices with their start and end apart: 16 -> 23, of which waited for: 11 -> 14; matrix products, arithmetic and copies ran while one was open for 26% -> 18% of each run, Pallas kernels for 0% -> 4%
where the time goes in v2:
time: 207 us; the launch traced here: 205 us
  waiting for transfers between devices  86.6 us (42%)
  starting transfers between devices  51.7 us (25%)
  other arithmetic  19.1 us (9%)
  matrix products  19.1 us (9%)
  local copies, waits for them, and re-layouts  15.5 us (7%)
  Pallas kernels  11.2 us (5%)
    all_to_all x5, waiting for transfers between devices, exchange(): return lax.all_to_all(value, axes, 0, 0, tiled=True)  65.6 us
    all_to_all x5, starting transfers between devices, exchange(): return lax.all_to_all(value, axes, 0, 0, tiled=True)  39.2 us
    dot_general x12, matrix products, dot(): lax.dot_general(a, b, ((contract[0], contract[1]), ((), ())), preferred_e...  19.1 us
    ppermute x7, waiting for transfers between devices, shift(): return lax.ppermute(value, 'x', [(i, (i + step) % n_x) for i in range(n_x)])  13.7 us
    unnamed x56, local copies, waits for them, and re-layouts  11 us
    pallas_call x2, Pallas kernels, vocab_product(): pl.pallas_call(kernel, grid=(half // step,), in_specs=[weights, weights,...  8.63 us
    ppermute x11, waiting for transfers between devices, swap(): return lax.ppermute(value, axis, [(0, 1), (1, 0)])  7.3 us
    ppermute x7, starting transfers between devices, shift(): return lax.ppermute(value, 'x', [(i, (i + step) % n_x) for i in range(n_x)])  6.44 us
  transfers between devices with their start and end apart: 23, of which 14 were waited for; matrix products, arithmetic and copies ran while one was open for 18% of the time, Pallas kernels for 4%

profile of v2, /device:TPU:6, one launch (start us, length us, event | category | flops | bytes accessed | tf_op | source)
XLA Modules:
  0.0 204.6 jit_solution(3287784757296652751)
XLA Ops:
  2.6 11.5 %all-to-all-start = ((bf16[32,4,3328]{2,1,0:T(4,128)(2,1)}), bf16[32,4,3328]{2,1,0:T(4,128)(2,1)S(1)}, u32[]{:S(2)}, u32[]{:S(2)}) async-start(bf16[32,4,3328]{2,1,0:T(4,128)(2,1)} %broadcast_in_dim.18), calls=%async_computation | async-start | bytes 1703936 | tf_op jit(solution)/shard_map/all_to_all | solution.py:26
  14.8 1.6 compare_convert_fusion
  16.4 3.5 %broadcast_select_fusion.2 = (bf16[104,6656]{1,0:T(8,128)(2,1)}, bf16[104,6656]{1,0:T(8,128)(2,1)}) fusion(bf16[104,6656]{1,0:T(8,128)(2,1)} %collective-permute-done.1, pred[]{:T(512)S(6)} %eq.54, bf16[1,6656,104]{1,2,0:T(8,128)(2,1)} %param.7), kind=kLoop, calls=%fused_computation.31 | loop fusion | flops 1384448 | bytes 5537793 | tf_op jit(solution)/shard_map/jit(_where)/select_n | solution.py:115
  19.9 18.4 %all-to-all-done = bf16[32,4,3328]{2,1,0:T(4,128)(2,1)S(1)} async-done(((bf16[32,4,3328]{2,1,0:T(4,128)(2,1)}), bf16[32,4,3328]{2,1,0:T(4,128)(2,1)S(1)}, u32[]{:S(2)}, u32[]{:S(2)}) %all-to-all-start) | async-done | bytes 852000 | tf_op jit(solution)/shard_map/all_to_all | solution.py:26
  40.2 1.8 broadcast_select_fusion
  43.1 4.9 %collective-permute-done.3 = bf16[128,1664]{1,0:T(8,128)(2,1)S(1)} collective-permute-done((bf16[128,1664]{1,0:T(8,128)(2,1)S(1)}, bf16[128,1664]{1,0:T(8,128)(2,1)S(1)}, u32[]{:S(2)}, u32[]{:S(2)}) %collective-permute-start.3) | collective-permute-done | bytes 426016 | tf_op jit(solution)/shard_map/ppermute | solution.py:139
  49.2 3.3 %collective-permute-done.2 = bf16[128,1664]{1,0:T(8,128)(2,1)S(1)} collective-permute-done((bf16[128,1664]{1,0:T(8,128)(2,1)S(1)}, bf16[128,1664]{1,0:T(8,128)(2,1)S(1)}, u32[]{:S(2)}, u32[]{:S(2)}) %collective-permute-start.2) | collective-permute-done | bytes 426016 | tf_op jit(solution)/shard_map/ppermute | solution.py:139
  55.9 6.4 %all-to-all-start.1 = ((bf16[16,208,128]{2,1,0:T(8,128)(2,1)}), bf16[16,208,128]{2,1,0:T(8,128)(2,1)}, u32[]{:S(2)}, u32[]{:S(2)}) async-start(bf16[16,208,128]{2,1,0:T(8,128)(2,1)} %broadcast_in_dim.19), calls=%async_computation.1 | async-start | bytes 1703936 | tf_op jit(solution)/shard_map/all_to_all | solution.py:26
  63.1 2.2 %copy-done.1 = bf16[1,3328,640]{2,1,0:T(8,128)(2,1)S(1)} copy-done((bf16[1,3328,640]{2,1,0:T(8,128)(2,1)S(1)}, bf16[1,3328,640]{2,1,0:T(8,128)(2,1)}, u32[]{:S(2)}) %copy-start.1) | copy-done | bytes 4259864
  65.3 4.3 %shard_map.93.target_ref = bf16[3328,128]{1,0:T(8,128)(2,1)S(1)} custom-call(bf16[3328,640]{1,0:T(8,128)(2,1)S(1)} %bitcast.41, bf16[3328,640]{1,0:T(8,128)(2,1)} %collective-permute-done.b_ref, bf16[128,640]{1,0:T(8,128)(2,1)S(1)} %get-tuple-element.56.ra_ref, bf16[128,640]{1,0:T(8,128)(2,1)S(1)} %get-tuple-element.55.rb_ref), custom_call_target="tpu_custom_call" | custom-call | flops 1090519040 | bytes 10223616 | tf_op jit(solution)/shard_map/pallas_call | solution.py:45
  70.5 12.7 %all-to-all-done.1 = bf16[16,208,128]{2,1,0:T(8,128)(2,1)} async-done(((bf16[16,208,128]{2,1,0:T(8,128)(2,1)}), bf16[16,208,128]{2,1,0:T(8,128)(2,1)}, u32[]{:S(2)}, u32[]{:S(2)}) %all-to-all-start.1) | async-done | bytes 852000 | tf_op jit(solution)/shard_map/all_to_all | solution.py:26
  83.2 3.3 %fusion.45 = f32[128,640]{1,0:T(8,128)S(1)} fusion(bf16[3328,128]{1,0:T(8,128)(2,1)} %bitcast.6, bf16[1,3328,640]{2,1,0:T(8,128)(2,1)} %param.9), kind=kOutput, calls=%fused_computation.109 | convolution fusion | flops 545259520 | bytes 5439488 | tf_op jit(solution)/shard_map/dot_general | solution.py:30
  86.6 1.7 collective-permute-start.5
  88.3 3.3 %fusion.54 = f32[128,640]{1,0:T(8,128)S(1)} fusion(bf16[3328,128]{1,0:T(8,128)(2,1)} %bitcast.6, bf16[3328,640]{1,0:T(8,128)(2,1)} %collective-permute-done.b_ref), kind=kOutput, calls=%fused_computation.118 | convolution fusion | flops 545259520 | bytes 5439488 | tf_op jit(solution)/shard_map/dot_general | solution.py:30
  91.7 2.2 %collective-permute-start.6 = (f32[128,640]{1,0:T(8,128)S(1)}, f32[128,640]{1,0:T(8,128)}, u32[]{:S(2)}, u32[]{:S(2)}) collective-permute-start(f32[128,640]{1,0:T(8,128)S(1)} %fusion.54), channel_id=1, source_target_pairs={{0,1},{1,0},{2,3},{3,2},{4,5},{5,4},{6,7},{7,6},{8,9},{9,8},{10,11... | collective-permute-start | bytes 983048 | tf_op jit(solution)/shard_map/ppermute | solution.py:22
  95.1 3.6 %collective-permute-done.5 = f32[128,640]{1,0:T(8,128)} collective-permute-done((f32[128,640]{1,0:T(8,128)S(1)}, f32[128,640]{1,0:T(8,128)}, u32[]{:S(2)}, u32[]{:S(2)}) %collective-permute-start.5) | collective-permute-done | bytes 327712 | tf_op jit(solution)/shard_map/ppermute | solution.py:22
  99.9 2.5 %collective-permute-done.6 = f32[128,640]{1,0:T(8,128)} collective-permute-done((f32[128,640]{1,0:T(8,128)S(1)}, f32[128,640]{1,0:T(8,128)}, u32[]{:S(2)}, u32[]{:S(2)}) %collective-permute-start.6) | collective-permute-done | bytes 327712 | tf_op jit(solution)/shard_map/ppermute | solution.py:22
  105.2 5.9 %all-to-all-start.2 = ((f32[16,3,128]{2,1,0:T(4,128)}), f32[16,3,128]{2,1,0:T(4,128)S(1)}, u32[]{:S(2)}, u32[]{:S(2)}) async-start(f32[16,3,128]{2,1,0:T(4,128)} %broadcast_in_dim.21), calls=%async_computation.2 | async-start | bytes 65536 | tf_op jit(solution)/shard_map/all_to_all | solution.py:26
  111.7 2.2 %copy-done.2 = bf16[1,3328,640]{2,1,0:T(8,128)(2,1)S(1)} copy-done((bf16[1,3328,640]{2,1,0:T(8,128)(2,1)S(1)}, bf16[1,3328,640]{2,1,0:T(8,128)(2,1)}, u32[]{:S(2)}) %copy-start.2) | copy-done | bytes 4259864
  113.9 4.3 %shard_map.94.product_ref = f32[3328,128]{1,0:T(8,128)S(1)} custom-call(bf16[3328,640]{1,0:T(8,128)(2,1)S(1)} %bitcast.42, bf16[3328,640]{1,0:T(8,128)(2,1)} %collective-permute-done.b_ref, bf16[128,640]{1,0:T(8,128)(2,1)S(1)} %get-tuple-element.39.ra_ref, bf16[128,640]{1,0:T(8,128)(2,1)S(1)} %get-tuple-element.38.rb_ref), custom_call_target="tpu_custom_call" | custom-call | flops 1090519040 | bytes 10223616 | tf_op jit(solution)/shard_map/pallas_call | solution.py:45
  120.2 2.6 %shard_map.95 = (bf16[3328,128]{1,0:T(8,128)(2,1)}, f32[1,128]{1,0:T(1,128)}) custom-call(f32[16,3,128]{2,1,0:T(4,128)} %copy-done.23, f32[2,128]{1,0:T(2,128)} %pad_maximum_fusion.24.own_ref, f32[3328,128]{1,0:T(8,128)} %copy-done.3, bf16[3328,128]{1,0:T(8,128)(2,1)} %copy-done.4), custom_call_target="tpu_custom_call" | custom-call | flops 1703936 | bytes 3407872 | tf_op jit(solution)/shard_map/pallas_call | solution.py:77
  122.8 8.1 %all-to-all-start.3 = ((bf16[16,208,128]{2,1,0:T(8,128)(2,1)}), bf16[16,208,128]{2,1,0:T(8,128)(2,1)}, u32[]{:S(2)}, u32[]{:S(2)}) async-start(bf16[16,208,128]{2,1,0:T(8,128)(2,1)} %bitcast.44), calls=%async_computation.3 | async-start | bytes 1703936 | tf_op jit(solution)/shard_map/all_to_all | solution.py:26
  132.6 18.2 %all-to-all-done.3 = bf16[16,208,128]{2,1,0:T(8,128)(2,1)} async-done(((bf16[16,208,128]{2,1,0:T(8,128)(2,1)}), bf16[16,208,128]{2,1,0:T(8,128)(2,1)}, u32[]{:S(2)}, u32[]{:S(2)}) %all-to-all-start.3) | async-done | bytes 852000 | tf_op jit(solution)/shard_map/all_to_all | solution.py:26
  150.8 1.4 convert_reduce_fusion.1
  155.0 2.0 collective-permute-start.7
  157.6 5.2 %fusion = bf16[1,3328,640]{2,1,0:T(8,128)(2,1)} fusion(bf16[3328,128]{1,0:T(8,128)(2,1)} %collective-permute-done.16, bf16[3328,128]{1,0:T(8,128)(2,1)} %bitcast.6, bf16[128,640]{1,0:T(8,128)(2,1)} %collective-permute-done.17, bf16[128,640]{1,0:T(8,128)(2,1)} %get-tuple-element.47), kind=kOutput, calls=%fused_computation.1 | convolution fusion | flops 1096712192 | bytes 6291456 | tf_op jit(solution)/shard_map/dot_general | solution.py:30
  165.0 1.3 pad_maximum_fusion.9
  166.3 7.4 %all-to-all-start.4 = ((bf16[32,4,3328]{2,1,0:T(4,128)(2,1)}), bf16[32,4,3328]{2,1,0:T(4,128)(2,1)S(1)}, u32[]{:S(2)}, u32[]{:S(2)}) async-start(bf16[32,4,3328]{2,1,0:T(4,128)(2,1)} %pad_maximum_fusion.9), calls=%async_computation.4 | async-start | bytes 1703936 | tf_op jit(solution)/shard_map/all_to_all | solution.py:26
  176.9 1.3 convolution_convert_fusion.4
  179.8 16.0 %all-to-all-done.4 = bf16[32,4,3328]{2,1,0:T(4,128)(2,1)S(1)} async-done(((bf16[32,4,3328]{2,1,0:T(4,128)(2,1)}), bf16[32,4,3328]{2,1,0:T(4,128)(2,1)S(1)}, u32[]{:S(2)}, u32[]{:S(2)}) %all-to-all-start.4) | async-done | bytes 852000 | tf_op jit(solution)/shard_map/all_to_all | solution.py:26
  196.1 1.3 collective-permute-start.10
  200.3 2.5 %collective-permute-done.11 = f32[4,3328]{1,0:T(4,128)S(1)} collective-permute-done((f32[4,3328]{1,0:T(4,128)S(1)}, f32[4,3328]{1,0:T(4,128)S(1)}, u32[]{:S(2)}, u32[]{:S(2)}) %collective-permute-start.11) | collective-permute-done | bytes 53280 | tf_op jit(solution)/shard_map/ppermute | solution.py:139
  (136 shorter events, 36.3 us)
Async XLA Ops:
  0.6 13.5 %copy-start.25 = (bf16[1,104]{1,0:T(2,128)(2,1)S(1)}, bf16[1,104]{1,0:T(2,128)(2,1)}, u32[]{:S(2)}) copy-start(bf16[1,104]{1,0:T(2,128)(2,1)} %param.8) | copy-start | bytes 628
  0.7 15.8 %collective-permute-start.1 = (bf16[104,6656]{1,0:T(8,128)(2,1)}, bf16[104,6656]{1,0:T(8,128)(2,1)}, u32[]{:S(2)}, u32[]{:S(2)}) collective-permute-start(bf16[104,6656]{1,0:T(8,128)(2,1)} %bitcast.43), channel_id=1, source_target_pairs={{0,2},{2,0},{1,3},{3,1},{4,6},{6,4},{5,7},{7,5},{8,10},{10,8},{9,1... | collective-permute-start | bytes 4153352 | tf_op jit(solution)/shard_map/ppermute | solution.py:22
  2.6 35.8 %all-to-all-start = ((bf16[32,4,3328]{2,1,0:T(4,128)(2,1)}), bf16[32,4,3328]{2,1,0:T(4,128)(2,1)S(1)}, u32[]{:S(2)}, u32[]{:S(2)}) async-start(bf16[32,4,3328]{2,1,0:T(4,128)(2,1)} %broadcast_in_dim.18), calls=%async_computation | async-start | bytes 1703936 | tf_op jit(solution)/shard_map/all_to_all | solution.py:26
  14.1 2.2 %collective-permute-start.4 = (f32[104]{0:T(128)S(1)}, f32[104]{0:T(128)S(1)}, u32[]{:S(2)}, u32[]{:S(2)}) collective-permute-start(f32[104]{0:T(128)S(1)} %bitcast_convert_fusion), channel_id=1, source_target_pairs={{0,2},{2,0},{1,3},{3,1},{4,6},{6,4},{5,7},{7,5},{8,10},{10,8},{9,1... | collective-permute-start | bytes 1256 | tf_op jit(solution)/shard_map/ppermute | solution.py:22
  14.2 48.8 %collective-permute-start = (bf16[3328,640]{1,0:T(8,128)(2,1)}, bf16[3328,640]{1,0:T(8,128)(2,1)}, u32[]{:S(2)}, u32[]{:S(2)}) collective-permute-start(bf16[3328,640]{1,0:T(8,128)(2,1)} %bitcast.40), channel_id=1, source_target_pairs={{0,2},{2,0},{1,3},{3,1},{4,6},{6,4},{5,7},{7,5},{8,10},{10,8},{9,1... | collective-permute-start | bytes 12779528 | tf_op jit(solution)/shard_map/ppermute | solution.py:22
  38.7 9.3 %collective-permute-start.3 = (bf16[128,1664]{1,0:T(8,128)(2,1)S(1)}, bf16[128,1664]{1,0:T(8,128)(2,1)S(1)}, u32[]{:S(2)}, u32[]{:S(2)}) collective-permute-start(bf16[128,1664]{1,0:T(8,128)(2,1)S(1)} %get-tuple-element.37), channel_id=1, source_target_pairs={{0,64},{64,128},{128,192},{192,0},{1,65},{65,129},{129,193},{193,1... | collective-permute-start | bytes 1277960 | tf_op jit(solution)/shard_map/ppermute | solution.py:139
  42.1 11.0 %copy-start.9 = (bf16[208,3328]{1,0:T(8,128)(2,1)}, bf16[208,3328]{1,0:T(8,128)(2,1)S(1)}, u32[]{:S(2)}) copy-start(bf16[208,3328]{1,0:T(8,128)(2,1)S(1)} %get-tuple-element.29) | copy-start | bytes 4153348
  42.1 10.5 %collective-permute-start.2 = (bf16[128,1664]{1,0:T(8,128)(2,1)S(1)}, bf16[128,1664]{1,0:T(8,128)(2,1)S(1)}, u32[]{:S(2)}, u32[]{:S(2)}) collective-permute-start(bf16[128,1664]{1,0:T(8,128)(2,1)S(1)} %get-tuple-element.36), channel_id=1, source_target_pairs={{0,192},{64,0},{128,64},{192,128},{1,193},{65,1},{129,65},{193,129... | collective-permute-start | bytes 1277960 | tf_op jit(solution)/shard_map/ppermute | solution.py:139
  43.1 10.0 %copy-start.5 = (bf16[416,1664]{1,0:T(8,128)(2,1)}, bf16[416,1664]{1,0:T(8,128)(2,1)S(1)}, u32[]{:S(2)}) copy-start(bf16[416,1664]{1,0:T(8,128)(2,1)S(1)} %fusion.9) | copy-start | bytes 4153348
  54.7 7.5 %copy-start.26 = (s32[260]{0:T(512)S(1)}, s32[260]{0:T(512)}, u32[]{:S(2)}) copy-start(s32[260]{0:T(512)} %param.10) | copy-start | bytes 3124
  54.7 7.9 %copy-start.27 = (s32[260]{0:T(512)S(1)}, s32[260]{0:T(512)}, u32[]{:S(2)}) copy-start(s32[260]{0:T(512)} %param.11) | copy-start | bytes 3124
  55.9 27.4 %all-to-all-start.1 = ((bf16[16,208,128]{2,1,0:T(8,128)(2,1)}), bf16[16,208,128]{2,1,0:T(8,128)(2,1)}, u32[]{:S(2)}, u32[]{:S(2)}) async-start(bf16[16,208,128]{2,1,0:T(8,128)(2,1)} %broadcast_in_dim.19), calls=%async_computation.1 | async-start | bytes 1703936 | tf_op jit(solution)/shard_map/all_to_all | solution.py:26
  86.6 12.1 %collective-permute-start.5 = (f32[128,640]{1,0:T(8,128)S(1)}, f32[128,640]{1,0:T(8,128)}, u32[]{:S(2)}, u32[]{:S(2)}) collective-permute-start(f32[128,640]{1,0:T(8,128)S(1)} %fusion.45), channel_id=1, source_target_pairs={{0,1},{1,0},{2,3},{3,2},{4,5},{5,4},{6,7},{7,6},{8,9},{9,8},{10,11... | collective-permute-start | bytes 983048 | tf_op jit(solution)/shard_map/ppermute | solution.py:22
  91.7 10.7 %collective-permute-start.6 = (f32[128,640]{1,0:T(8,128)S(1)}, f32[128,640]{1,0:T(8,128)}, u32[]{:S(2)}, u32[]{:S(2)}) collective-permute-start(f32[128,640]{1,0:T(8,128)S(1)} %fusion.54), channel_id=1, source_target_pairs={{0,1},{1,0},{2,3},{3,2},{4,5},{5,4},{6,7},{7,6},{8,9},{9,8},{10,11... | collective-permute-start | bytes 983048 | tf_op jit(solution)/shard_map/ppermute | solution.py:22
  105.2 14.4 %all-to-all-start.2 = ((f32[16,3,128]{2,1,0:T(4,128)}), f32[16,3,128]{2,1,0:T(4,128)S(1)}, u32[]{:S(2)}, u32[]{:S(2)}) async-start(f32[16,3,128]{2,1,0:T(4,128)} %broadcast_in_dim.21), calls=%async_computation.2 | async-start | bytes 65536 | tf_op jit(solution)/shard_map/all_to_all | solution.py:26
  119.4 11.7 %copy-start.16 = (f32[128,640]{1,0:T(8,128)S(1)}, f32[128,640]{1,0:T(8,128)}, u32[]{:S(2)}) copy-start(f32[128,640]{1,0:T(8,128)} %copy-done.15) | copy-start | bytes 983044
  122.8 8.3 %copy-start.24 = (f32[1,128]{1,0:T(1,128)S(1)}, f32[1,128]{1,0:T(1,128)}, u32[]{:S(2)}) copy-start(f32[1,128]{1,0:T(1,128)} %get-tuple-element.11) | copy-start | bytes 1540
  122.8 28.0 %all-to-all-start.3 = ((bf16[16,208,128]{2,1,0:T(8,128)(2,1)}), bf16[16,208,128]{2,1,0:T(8,128)(2,1)}, u32[]{:S(2)}, u32[]{:S(2)}) async-start(bf16[16,208,128]{2,1,0:T(8,128)(2,1)} %bitcast.44), calls=%async_computation.3 | async-start | bytes 1703936 | tf_op jit(solution)/shard_map/all_to_all | solution.py:26
  131.0 26.5 %collective-permute-start.16 = (bf16[3328,128]{1,0:T(8,128)(2,1)}, bf16[3328,128]{1,0:T(8,128)(2,1)}, u32[]{:S(2)}, u32[]{:S(2)}) collective-permute-start(bf16[3328,128]{1,0:T(8,128)(2,1)} %bitcast.6), channel_id=1, source_target_pairs={{0,2},{2,0},{1,3},{3,1},{4,6},{6,4},{5,7},{7,5},{8,10},{10,8},{9,1... | collective-permute-start | bytes 2555912 | tf_op jit(solution)/shard_map/ppermute | solution.py:22
  132.1 24.9 %collective-permute-start.17 = (bf16[128,640]{1,0:T(8,128)(2,1)}, bf16[128,640]{1,0:T(8,128)(2,1)}, u32[]{:S(2)}, u32[]{:S(2)}) collective-permute-start(bf16[128,640]{1,0:T(8,128)(2,1)} %get-tuple-element.48), channel_id=1, source_target_pairs={{0,2},{2,0},{1,3},{3,1},{4,6},{6,4},{5,7},{7,5},{8,10},{10,8},{9,1... | collective-permute-start | bytes 491528 | tf_op jit(solution)/shard_map/ppermute | solution.py:22
  154.9 8.5 %collective-permute-start.8 = (bf16[128,1664]{1,0:T(8,128)(2,1)S(1)}, bf16[128,1664]{1,0:T(8,128)(2,1)S(1)}, u32[]{:S(2)}, u32[]{:S(2)}) collective-permute-start(bf16[128,1664]{1,0:T(8,128)(2,1)S(1)} %convolution_convert_fusion.2), channel_id=1, source_target_pairs={{0,64},{64,128},{128,192},{192,0},{1,65},{65,129},{129,193},{193,1... | collective-permute-start | bytes 1277960 | tf_op jit(solution)/shard_map/ppermute | solution.py:139
  155.0 9.6 %collective-permute-start.7 = (bf16[128,1664]{1,0:T(8,128)(2,1)}, bf16[128,1664]{1,0:T(8,128)(2,1)S(1)}, u32[]{:S(2)}, u32[]{:S(2)}) collective-permute-start(bf16[128,1664]{1,0:T(8,128)(2,1)} %convolution_convert_fusion.3), channel_id=1, source_target_pairs={{0,192},{64,0},{128,64},{192,128},{1,193},{65,1},{129,65},{193,129... | collective-permute-start | bytes 1277960 | tf_op jit(solution)/shard_map/ppermute | solution.py:139
  157.0 21.1 %collective-permute-start.13 = (bf16[128,3328]{1,0:T(8,128)(2,1)}, bf16[128,3328]{1,0:T(8,128)(2,1)S(1)}, u32[]{:S(2)}, u32[]{:S(2)}) collective-permute-start(bf16[128,3328]{1,0:T(8,128)(2,1)} %copy-done.12), channel_id=1, source_target_pairs={{0,2},{2,0},{1,3},{3,1},{4,6},{6,4},{5,7},{7,5},{8,10},{10,8},{9,1... | collective-permute-start | bytes 2555912 | tf_op jit(solution)/shard_map/ppermute | solution.py:22
  157.0 18.5 %collective-permute-start.14 = (bf16[128,1664]{1,0:T(8,128)(2,1)}, bf16[128,1664]{1,0:T(8,128)(2,1)}, u32[]{:S(2)}, u32[]{:S(2)}) collective-permute-start(bf16[128,1664]{1,0:T(8,128)(2,1)} %copy-done.21), channel_id=1, source_target_pairs={{0,2},{2,0},{1,3},{3,1},{4,6},{6,4},{5,7},{7,5},{8,10},{10,8},{9,1... | collective-permute-start | bytes 1277960 | tf_op jit(solution)/shard_map/ppermute | solution.py:22
  157.5 19.3 %collective-permute-start.15 = (bf16[128,1664]{1,0:T(8,128)(2,1)}, bf16[128,1664]{1,0:T(8,128)(2,1)}, u32[]{:S(2)}, u32[]{:S(2)}) collective-permute-start(bf16[128,1664]{1,0:T(8,128)(2,1)} %copy-done.19), channel_id=1, source_target_pairs={{0,2},{2,0},{1,3},{3,1},{4,6},{6,4},{5,7},{7,5},{8,10},{10,8},{9,1... | collective-permute-start | bytes 1277960 | tf_op jit(solution)/shard_map/ppermute | solution.py:22
  165.0 10.5 %copy-start.22 = (bf16[128,1664]{1,0:T(8,128)(2,1)S(1)}, bf16[128,1664]{1,0:T(8,128)(2,1)}, u32[]{:S(2)}) copy-start(bf16[128,1664]{1,0:T(8,128)(2,1)} %copy-done.21) | copy-start | bytes 1277956
  166.3 10.5 %copy-start.20 = (bf16[128,1664]{1,0:T(8,128)(2,1)S(1)}, bf16[128,1664]{1,0:T(8,128)(2,1)}, u32[]{:S(2)}) copy-start(bf16[128,1664]{1,0:T(8,128)(2,1)} %copy-done.19) | copy-start | bytes 1277956
  166.3 29.4 %all-to-all-start.4 = ((bf16[32,4,3328]{2,1,0:T(4,128)(2,1)}), bf16[32,4,3328]{2,1,0:T(4,128)(2,1)S(1)}, u32[]{:S(2)}, u32[]{:S(2)}) async-start(bf16[32,4,3328]{2,1,0:T(4,128)(2,1)} %pad_maximum_fusion.9), calls=%async_computation.4 | async-start | bytes 1703936 | tf_op jit(solution)/shard_map/all_to_all | solution.py:26
  173.9 1.5 collective-permute-start.12
  196.1 4.2 %collective-permute-start.10 = (f32[4,3328]{1,0:T(4,128)S(1)}, f32[4,3328]{1,0:T(4,128)S(1)}, u32[]{:S(2)}, u32[]{:S(2)}) collective-permute-start(f32[4,3328]{1,0:T(4,128)S(1)} %convert_reduce_fusion), channel_id=1, source_target_pairs={{0,64},{64,128},{128,192},{192,0},{1,65},{65,129},{129,193},{193,1... | collective-permute-start | bytes 159752 | tf_op jit(solution)/shard_map/ppermute | solution.py:139
  197.5 5.3 %collective-permute-start.11 = (f32[4,3328]{1,0:T(4,128)S(1)}, f32[4,3328]{1,0:T(4,128)S(1)}, u32[]{:S(2)}, u32[]{:S(2)}) collective-permute-start(f32[4,3328]{1,0:T(4,128)S(1)} %convert_reduce_fusion), channel_id=1, source_target_pairs={{0,192},{64,0},{128,64},{192,128},{1,193},{65,1},{129,65},{193,129... | collective-permute-start | bytes 159752 | tf_op jit(solution)/shard_map/ppermute | solution.py:139
  198.2 5.6 %collective-permute-start.9 = (f32[4,3328]{1,0:T(4,128)S(1)}, f32[4,3328]{1,0:T(4,128)S(1)}, u32[]{:S(2)}, u32[]{:S(2)}) collective-permute-start(f32[4,3328]{1,0:T(4,128)S(1)} %convert_reduce_fusion), channel_id=1, source_target_pairs={{0,128},{64,192},{128,0},{192,64},{1,129},{65,193},{129,1},{193,65... | collective-permute-start | bytes 159752 | tf_op jit(solution)/shard_map/ppermute | solution.py:139
  (19 other events, 44.7 us)

commit v3 on v2

--- a/solution.py
+++ b/solution.py
@@ -7,6 +7,9 @@
 from jax.sharding import PartitionSpec as P
 
 loss_scale = 16.0
+int16_top = 32767.0
+ln2 = 0.6931471805599453
+vmem_bytes = 60 * 2**20
 f32 = jnp.float32
 bf16 = jnp.bfloat16
 plane = ("ylo", "z")
@@ -53,8 +56,57 @@
             bytes_accessed=4 * half * columns + 4 * half * toks,
             transcendentals=0,
         ),
-        compiler_params=pltpu.CompilerParams(vmem_limit_bytes=24 * 2**20),
+        compiler_params=pltpu.CompilerParams(vmem_limit_bytes=vmem_bytes),
     )(lm_a, lm_b, rows_a, rows_b)
+
+
+def vocab_logits(hidden, lm_a, lm_b):
+    half, columns = lm_a.shape
+    toks = hidden.shape[1]
+    step = half // 2
+    lanes = 128
+
+    def kernel(h_ref, a_ref, b_ref, out_ref, coded_ref):
+        part_a = dot(h_ref[...], a_ref[...], ((0,), (0,)))
+        part_b = dot(h_ref[...], b_ref[...], ((0,), (0,)))
+
+        @pl.when(pl.program_id(0) == 0)
+        def _():
+            out_ref[:, :columns] = part_a
+            out_ref[:, columns:] = part_b
+
+        @pl.when(pl.program_id(0) > 0)
+        def _():
+            value = out_ref[...] + jnp.concatenate([part_a, part_b], 1)
+            out_ref[...] = value
+            size = jnp.max(jnp.abs(value), axis=1, keepdims=True)
+            power = jnp.ceil(jnp.log(jnp.maximum(size, 1e-30)) * (1.0 / ln2))
+            code = jnp.floor(value * (int16_top * jnp.exp(power * -ln2)) + 0.5)
+            code = jnp.clip(code, -int16_top, int16_top)
+            coded_ref[:, : 2 * columns] = code.astype(jnp.int32).astype(jnp.int16)
+            power = jnp.broadcast_to(power, (toks, lanes))
+            coded_ref[:, 2 * columns :] = power.astype(jnp.int32).astype(jnp.int16)
+
+    weights = pl.BlockSpec((step, columns), lambda i: (i, 0))
+    return pl.pallas_call(
+        kernel,
+        grid=(half // step,),
+        in_specs=[pl.BlockSpec((step, toks), lambda i: (i, 0)), weights, weights],
+        out_specs=[
+            pl.BlockSpec((toks, 2 * columns), lambda i: (0, 0)),
+            pl.BlockSpec((toks, 2 * columns + lanes), lambda i: (0, 0)),
+        ],
+        out_shape=[
+            jax.ShapeDtypeStruct((toks, 2 * columns), f32),
+            jax.ShapeDtypeStruct((toks, 2 * columns + lanes), jnp.int16),
+        ],
+        cost_estimate=pl.CostEstimate(
+            flops=4 * half * columns * toks,
+            bytes_accessed=4 * half * columns + 2 * half * toks,
+            transcendentals=0,
+        ),
+        compiler_params=pltpu.CompilerParams(vmem_limit_bytes=vmem_bytes),
+    )(hidden, lm_a, lm_b)
 
 
 def combine(stats, own, product, target_cols):
@@ -91,6 +143,7 @@
         cost_estimate=pl.CostEstimate(
             flops=4 * half * toks, bytes_accessed=8 * half * toks, transcendentals=0
         ),
+        compiler_params=pltpu.CompilerParams(vmem_limit_bytes=vmem_bytes),
     )(stats, own, product, target_cols)
 
 
@@ -128,24 +181,59 @@
     iota_r = lax.broadcasted_iota(jnp.int32, (pair, half_cols), 0)
     iota_c = lax.broadcasted_iota(jnp.int32, (pair, half_cols), 1)
 
-    def aug(side):
-        weights = jnp.where(side == 0, res_pair[:, :half_cols], res_pair[:, half_cols:])
-        select = (iota_r + block * pair == iota_c + side * half_cols).astype(bf16)
-        return jnp.concatenate([weights, select], 0)
-
-    near, far = aug(odd), aug(1 - odd)
+    select = jnp.concatenate(
+        [(iota_r + block * pair == iota_c + side * half_cols).astype(bf16) for side in (0, 1)], 1
+    )
+    res_aug = jnp.concatenate([res_pair, select], 0)
+    near = lax.dynamic_slice_in_dim(res_aug, odd * half_cols, half_cols, 1)
+    far = lax.dynamic_slice_in_dim(res_aug, (1 - odd) * half_cols, half_cols, 1)
 
     def shift(value, step):
         return lax.ppermute(value, "x", [(i, (i + step) % n_x) for i in range(n_x)])
 
-    mine = lax.dynamic_slice_in_dim(trunk_rows, odd * half_cols, half_cols, 1)
-    part = exchange(jnp.broadcast_to(mine[None], (n_all, rows, half_cols)), plane_all)
-    part = part.reshape(toks, half_cols)
+    line = ("ylo", "yhi")
+    n_z = lax.axis_size("z")
+    n_y = lax.axis_size("ylo") * lax.axis_size("yhi")
+    y = yhi * lax.axis_size("ylo") + ylo
+
+    def z_shift(value, step):
+        return lax.ppermute(value, "z", [(i, (i + step) % n_z) for i in range(n_z)])
+
+    def line_index(at):
+        return at % 2 * 2 + at // 2
+
+    def y_shift(value, step):
+        pairs = [(line_index(i), line_index((i + step) % n_y)) for i in range(n_y)]
+        return lax.ppermute(value, line, pairs)
+
+    def place(buffer, block, at, row=0, col=0):
+        return lax.dynamic_update_slice(buffer, block[None], (at, row, col))
+
+    up = down = trunk_rows
+    seen = place(jnp.zeros((n_z, rows, width), bf16), trunk_rows, z)
+    for step in range(1, n_z // 2):
+        up, down = z_shift(up, 1), z_shift(down, -1)
+        seen = place(seen, up, (z - step) % n_z)
+        seen = place(seen, down, (z + step) % n_z)
+    up, down = z_shift(up[:, :half_cols], 1), z_shift(down[:, half_cols:], -1)
+    seen = place(seen, up, (z + n_z // 2) % n_z)
+    seen = place(seen, down, (z + n_z // 2) % n_z, 0, half_cols)
+
+    seen = seen.reshape(n_z * rows, width)
+    cut = n_z * rows // 2
+    trunk = place(jnp.zeros((n_y, n_z * rows, width), bf16), seen, y)
+    up, down = y_shift(seen, 1), y_shift(seen, -1)
+    trunk = place(trunk, up, (y - 1) % n_y)
+    trunk = place(trunk, down, (y + 1) % n_y)
+    trunk = place(trunk, y_shift(up[:cut], 1), (y + 2) % n_y)
+    trunk = place(trunk, y_shift(down[cut:], -1), (y + 2) % n_y, cut)
+    trunk = trunk.reshape(toks, width)
 
     def own_tokens(values):
         values = lax.dynamic_slice_in_dim(values, head + 1, 2 * toks)
-        values = values.reshape(n_plane, 2, toks // n_plane)
-        return lax.dynamic_index_in_dim(values, core, 1, keepdims=False).reshape(toks)
+        values = values.reshape(lax.axis_size("ylo"), n_z, 2, lax.axis_size("yhi"), rows)
+        values = lax.dynamic_index_in_dim(values, core, 2, keepdims=False)
+        return values.transpose(2, 0, 1, 3).reshape(toks)
 
     tok_ids = own_tokens(next_ids)
     live = own_tokens(valid_mask).astype(f32)
@@ -159,12 +247,7 @@
     target_cols = vocab_product(
         lm_own, lm_other, hot_own.astype(bf16), hot_other.astype(bf16), bf16
     )
-    from_right = shift(part[:, :quarter], -1)
-    from_left = shift(part[:, quarter:], 1)
-
-    both = dot(near, part, ((1,), (1,)))
-    both = both + dot(far[:, :quarter], from_right, ((1,), (1,)))
-    both = both + dot(far[:, quarter:], from_left, ((1,), (1,)))
+    both = dot(res_aug, trunk, ((1,), (1,)))
     pre = both[:pair] + bias_pair[:, None]
     hidden = (both[pair:] + jax.nn.silu(pre)).astype(bf16)
     hidden_half = exchange(
@@ -172,10 +255,12 @@
     ).reshape(half, toks)
     target_cols, hidden_half = lax.optimization_barrier((target_cols, hidden_half))
 
-    logits_own = dot(hidden_half, lm_own, ((0,), (0,)))
-    logits_other = dot(hidden_half, lm_other, ((0,), (0,)))
-    logits_own = logits_own + swap(logits_own, "yhi")
-    logits_other = logits_other + swap(logits_other, "yhi")
+    logits, coded = vocab_logits(hidden_half, lm_own, lm_other)
+    coded = swap(coded, "yhi").astype(f32)
+    logits = logits + coded[:, : 2 * vocab_width] * (
+        jnp.exp(coded[:, 2 * vocab_width : 2 * vocab_width + 1] * ln2) * (1.0 / int16_top)
+    )
+    logits_own, logits_other = logits[:, :vocab_width], logits[:, vocab_width:]
     top = jnp.maximum(jnp.max(logits_own, axis=1), jnp.max(logits_other, axis=1))
     exp_own = jnp.exp(logits_own - top[:, None])
     exp_other = jnp.exp(logits_other - top[:, None])
@@ -198,16 +283,22 @@
     pre_round = pre_grad.astype(bf16)
 
     both_grad = jnp.concatenate([pre_round, hidden_grad.astype(bf16)], 0)
+    given = dot(both_grad, far, ((0,), (0,))).astype(bf16)
+    got_left = shift(given[:, quarter:], 1)
+    got_right = shift(given[:, :quarter], -1)
     keep = dot(both_grad, near, ((0,), (0,)))
-    give_left = dot(both_grad, far[:, :quarter], ((0,), (0,))).astype(bf16)
-    give_right = dot(both_grad, far[:, quarter:], ((0,), (0,))).astype(bf16)
-    got_left = shift(give_right, 1)
-    got_right = shift(give_left, -1)
     by_x = jnp.concatenate(
         [keep[:, :quarter] + got_right.astype(f32), keep[:, quarter:] + got_left.astype(f32)], 1
     ).astype(bf16)
-    by_plane = exchange(by_x.reshape(n_all, rows, half_cols), plane_all)
-    summed = jnp.sum(by_plane.astype(f32), axis=0)
+    by_x = by_x.reshape(n_y, n_z * rows, half_cols)
+    by_y = lax.dynamic_index_in_dim(by_x, y, 0, keepdims=False).astype(f32)
+    for flip in (1, 3, 2):
+        sent = lax.dynamic_index_in_dim(by_x, y ^ flip, 0, keepdims=False)
+        pairs = [(line_index(i), line_index(i ^ flip)) for i in range(n_y)]
+        got = lax.ppermute(sent, line, pairs)
+        by_y = by_y + got.astype(f32)
+    by_z = exchange(by_y.astype(bf16).reshape(n_z, rows, half_cols), "z")
+    summed = jnp.sum(by_z.astype(f32), axis=0)
     here = summed + shift(summed, 2)
     there = shift(summed, 1) + shift(summed, -1)
     trunk_grad = jnp.concatenate(
@@ -229,16 +320,8 @@
     bias_grad = jnp.sum(pre_own, axis=1) + jnp.sum(pre_sibling, axis=1)
     pre_both = jnp.concatenate([pre_own, pre_sibling], 1).astype(bf16)
 
-    def with_sibling(value):
-        return jnp.concatenate([value, swap(value, "core")], 0)
-
-    res_near = dot(pre_both, with_sibling(part), ((1,), (0,))).astype(bf16)
-    res_far = jnp.concatenate(
-        [dot(pre_both, with_sibling(v), ((1,), (0,))) for v in (from_right, from_left)], 1
-    ).astype(bf16)
-    res_grad = jnp.concatenate(
-        [jnp.where(odd == 0, res_near, res_far), jnp.where(odd == 0, res_far, res_near)], 1
-    )
+    trunk_both = jnp.concatenate([trunk, swap(trunk, "core")], 0)
+    res_grad = dot(pre_both, trunk_both, ((1,), (0,))).astype(bf16)
     return (trunk_grad, res_grad.T[None], bias_grad[None], lm_grad[None])
 
 

time: 207 us -> 188 us (0.908); the launches traced: 205 us -> 188 us
  waiting for transfers between devices: 86.6 us -> 71 us
  Pallas kernels: 11.2 us -> 20 us
  starting transfers between devices: 51.7 us -> 59.4 us
  matrix products: 19.1 us -> 12.7 us
  other arithmetic: 19.1 us -> 12.8 us
  local copies, waits for them, and re-layouts: 15.5 us -> 10.7 us
    all_to_all x5 -> x4, waiting for transfers between devices: 65.6 us -> 36.7 us  [exchange(): return lax.all_to_all(value, axes, 0, 0, tiled=True)]
    ppermute x0 -> x15, starting transfers between devices: none -> 26.9 us  [the longest x8 15.9 us: z_shift(): return lax.ppermute(value, 'z', [(i, (i + step) % n_z) for i in range(n_z)])]
    ppermute x0 -> x15, waiting for transfers between devices: none -> 25.8 us  [the longest x4 10.7 us: y_shift(): return lax.ppermute(value, line, pairs)]
    all_to_all x5 -> x4, starting transfers between devices: 39.2 us -> 22.4 us  [exchange(): return lax.all_to_all(value, axes, 0, 0, tiled=True)]
    ppermute x7 -> x5, waiting for transfers between devices: 13.7 us -> 2.95 us  [shift(): return lax.ppermute(value, 'x', [(i, (i + step) % n_x) for i in range(n_x)])]
    unnamed x56 -> x30, local copies, waits for them, and re-layouts: 11 us -> 3 us
    dot_general x12 -> x5, matrix products: 19.1 us -> 12.7 us  [dot(): lax.dot_general(a, b, ((contract[0], contract[1]), ((), ())), preferred_e...]
    pallas_call x0 -> x1, Pallas kernels: none -> 5.91 us  [vocab_logits(): pl.pallas_call(kernel, grid=(half // step,), in_specs=[pl.BlockSpec((step...]
  transfers between devices with their start and end apart: 23 -> 32, of which waited for: 14 -> 16; matrix products, arithmetic and copies ran while one was open for 18% -> 16% of each run, Pallas kernels for 4% -> 6%
where the time goes in v3:
time: 188 us
  waiting for transfers between devices  71 us (38%)
  starting transfers between devices  59.4 us (32%)
  Pallas kernels  20 us (11%)
  other arithmetic  12.8 us (7%)
  matrix products  12.7 us (7%)
  local copies, waits for them, and re-layouts  10.7 us (6%)
    all_to_all x4, waiting for transfers between devices, exchange(): return lax.all_to_all(value, axes, 0, 0, tiled=True)  36.7 us
    all_to_all x4, starting transfers between devices, exchange(): return lax.all_to_all(value, axes, 0, 0, tiled=True)  22.4 us
    ppermute x8, starting transfers between devices, z_shift(): return lax.ppermute(value, 'z', [(i, (i + step) % n_z) for i in range(n_z)])  15.9 us
    dot_general x5, matrix products, dot(): lax.dot_general(a, b, ((contract[0], contract[1]), ((), ())), preferred_e...  12.7 us
    pallas_call x2, Pallas kernels, vocab_product(): pl.pallas_call(kernel, grid=(half // step,), in_specs=[weights, weights,...  11.4 us
    ppermute x4, waiting for transfers between devices, y_shift(): return lax.ppermute(value, line, pairs)  10.7 us
    ppermute x3, waiting for transfers between devices, on_device(): got = lax.ppermute(sent, line, pairs)  9.19 us
    ppermute x4, starting transfers between devices, y_shift(): return lax.ppermute(value, line, pairs)  6.81 us
  transfers between devices with their start and end apart: 32, of which 16 were waited for; matrix products, arithmetic and copies ran while one was open for 16% of the time, Pallas kernels for 6%

profile of v3, /device:TPU:6, one launch (start us, length us, event | category | flops | bytes accessed | tf_op | source)
XLA Modules:
  0.0 187.8 jit_solution(2004020824476728875)
XLA Ops:
  2.6 4.0 %collective-permute-start.3 = (bf16[4,6656]{1,0:T(4,128)(2,1)}, bf16[4,6656]{1,0:T(4,128)(2,1)S(1)}, u32[]{:S(2)}, u32[]{:S(2)}) collective-permute-start(bf16[4,6656]{1,0:T(4,128)(2,1)} %param.6), channel_id=1, source_target_pairs={{0,28},{4,0},{8,4},{12,8},{16,12},{20,16},{24,20},{28,24},{1,29},{... | collective-permute-start | bytes 159752 | tf_op jit(solution)/shard_map/ppermute | solution.py:200
  10.4 3.2 %collective-permute-start.5 = (bf16[4,6656]{1,0:T(4,128)(2,1)S(1)}, bf16[4,6656]{1,0:T(4,128)(2,1)S(1)}, u32[]{:S(2)}, u32[]{:S(2)}) collective-permute-start(bf16[4,6656]{1,0:T(4,128)(2,1)S(1)} %collective-permute-done.3), channel_id=1, source_target_pairs={{0,28},{4,0},{8,4},{12,8},{16,12},{20,16},{24,20},{28,24},{1,29},{... | collective-permute-start | bytes 159752 | tf_op jit(solution)/shard_map/ppermute | solution.py:200
  13.7 2.1 %collective-permute-done.4 = bf16[4,6656]{1,0:T(4,128)(2,1)S(1)} collective-permute-done((bf16[4,6656]{1,0:T(4,128)(2,1)S(1)}, bf16[4,6656]{1,0:T(4,128)(2,1)S(1)}, u32[]{:S(2)}, u32[]{:S(2)}) %collective-permute-start.4) | collective-permute-done | bytes 53280 | tf_op jit(solution)/shard_map/ppermute | solution.py:200
  15.8 3.2 %collective-permute-start.7 = (bf16[4,6656]{1,0:T(4,128)(2,1)S(1)}, bf16[4,6656]{1,0:T(4,128)(2,1)S(1)}, u32[]{:S(2)}, u32[]{:S(2)}) collective-permute-start(bf16[4,6656]{1,0:T(4,128)(2,1)S(1)} %collective-permute-done.5), channel_id=1, source_target_pairs={{0,28},{4,0},{8,4},{12,8},{16,12},{20,16},{24,20},{28,24},{1,29},{... | collective-permute-start | bytes 159752 | tf_op jit(solution)/shard_map/ppermute | solution.py:200
  19.1 2.0 %collective-permute-done.6 = bf16[4,6656]{1,0:T(4,128)(2,1)S(1)} collective-permute-done((bf16[4,6656]{1,0:T(4,128)(2,1)S(1)}, bf16[4,6656]{1,0:T(4,128)(2,1)S(1)}, u32[]{:S(2)}, u32[]{:S(2)}) %collective-permute-start.6) | collective-permute-done | bytes 53280 | tf_op jit(solution)/shard_map/ppermute | solution.py:200
  21.3 3.3 %collective-permute-start.9 = (bf16[4,3328]{1,0:T(4,128)(2,1)S(1)}, bf16[4,3328]{1,0:T(4,128)(2,1)S(1)}, u32[]{:S(2)}, u32[]{:S(2)}) collective-permute-start(bf16[4,3328]{1,0:T(4,128)(2,1)S(1)} %slice.57), channel_id=1, source_target_pairs={{0,28},{4,0},{8,4},{12,8},{16,12},{20,16},{24,20},{28,24},{1,29},{... | collective-permute-start | bytes 79880 | tf_op jit(solution)/shard_map/ppermute | solution.py:200
  31.5 7.2 %collective-permute-done.10 = bf16[32,6656]{1,0:T(8,128)(2,1)S(1)} collective-permute-done((bf16[32,6656]{1,0:T(8,128)(2,1)}, bf16[32,6656]{1,0:T(8,128)(2,1)S(1)}, u32[]{:S(2)}, u32[]{:S(2)}) %collective-permute-start.10) | collective-permute-done | bytes 426016 | tf_op jit(solution)/shard_map/ppermute | solution.py:207
  39.8 2.5 %collective-permute-start.13 = (bf16[16,6656]{1,0:T(8,128)(2,1)S(1)}, bf16[16,6656]{1,0:T(8,128)(2,1)S(1)}, u32[]{:S(2)}, u32[]{:S(2)}) collective-permute-start(bf16[16,6656]{1,0:T(8,128)(2,1)S(1)} %slice.59), channel_id=1, source_target_pairs={{0,33},{32,0},{1,32},{33,1},{2,35},{34,2},{3,34},{35,3},{4,37},{36... | collective-permute-start | bytes 638984 | tf_op jit(solution)/shard_map/ppermute | solution.py:207
  42.4 3.5 %collective-permute-done.12 = bf16[16,6656]{1,0:T(8,128)(2,1)S(1)} collective-permute-done((bf16[16,6656]{1,0:T(8,128)(2,1)S(1)}, bf16[16,6656]{1,0:T(8,128)(2,1)S(1)}, u32[]{:S(2)}, u32[]{:S(2)}) %collective-permute-start.12) | collective-permute-done | bytes 213024 | tf_op jit(solution)/shard_map/ppermute | solution.py:207
  46.0 2.1 %broadcast_select_fusion.1 = (bf16[104,6656]{1,0:T(8,128)(2,1)S(1)}, bf16[104,6656]{1,0:T(8,128)(2,1)S(1)}) fusion(bf16[104,6656]{1,0:T(8,128)(2,1)} %collective-permute-done.1, pred[]{:T(512)S(6)} %eq.60, bf16[1,6656,104]{1,2,0:T(8,128)(2,1)S(1)} %copy-done.6), kind=kLoop, calls=%fused_computation.20 | loop fusion | flops 1384448 | bytes 5537793 | tf_op jit(solution)/shard_map/jit(_where)/select_n | solution.py:168
  52.9 7.5 %all-to-all-start = ((bf16[16,208,128]{2,1,0:T(8,128)(2,1)}), bf16[16,208,128]{2,1,0:T(8,128)(2,1)S(1)}, u32[]{:S(2)}, u32[]{:S(2)}) async-start(bf16[16,208,128]{2,1,0:T(8,128)(2,1)} %broadcast_in_dim.94), calls=%async_computation | async-start | bytes 1703936 | tf_op jit(solution)/shard_map/all_to_all | solution.py:29
  62.9 5.7 %shard_map.93.target_ref = bf16[3328,128]{1,0:T(8,128)(2,1)} custom-call(bf16[3328,640]{1,0:T(8,128)(2,1)} %bitcast.90, bf16[3328,640]{1,0:T(8,128)(2,1)} %collective-permute-done.b_ref, bf16[128,640]{1,0:T(8,128)(2,1)} %fusion.25.ra_ref, bf16[128,640]{1,0:T(8,128)(2,1)} %fusion.23.rb_ref), custom_call_target="tpu_custom_call" | custom-call | flops 1090519040 | bytes 10223616 | tf_op jit(solution)/shard_map/pallas_call | solution.py:48
  68.6 9.3 %all-to-all-done = bf16[16,208,128]{2,1,0:T(8,128)(2,1)S(1)} async-done(((bf16[16,208,128]{2,1,0:T(8,128)(2,1)}), bf16[16,208,128]{2,1,0:T(8,128)(2,1)S(1)}, u32[]{:S(2)}, u32[]{:S(2)}) %all-to-all-start) | async-done | bytes 852000 | tf_op jit(solution)/shard_map/all_to_all | solution.py:29
  78.8 5.9 %shard_map.94 = (f32[128,1280]{1,0:T(8,128)}, s16[128,1408]{1,0:T(8,128)(2,1)}) custom-call(bf16[3328,128]{1,0:T(8,128)(2,1)} %bitcast.99, bf16[3328,640]{1,0:T(8,128)(2,1)} %bitcast.91, bf16[3328,640]{1,0:T(8,128)(2,1)} %collective-permute-done.b_ref), custom_call_target="tpu_custom_call" | custom-call | flops 1090519040 | bytes 9371648 | tf_op jit(solution)/shard_map/pallas_call | solution.py:91
  84.7 3.3 %collective-permute-start.15 = (s16[128,1408]{1,0:T(8,128)(2,1)}, s16[128,1408]{1,0:T(8,128)(2,1)S(1)}, u32[]{:S(2)}, u32[]{:S(2)}) collective-permute-start(s16[128,1408]{1,0:T(8,128)(2,1)} %get-tuple-element.12), channel_id=1, source_target_pairs={{0,1},{1,0},{2,3},{3,2},{4,5},{5,4},{6,7},{7,6},{8,9},{9,8},{10,11... | collective-permute-start | bytes 1081352 | tf_op jit(solution)/shard_map/ppermute | solution.py:25
  88.4 5.5 %collective-permute-done.15 = s16[128,1408]{1,0:T(8,128)(2,1)S(1)} collective-permute-done((s16[128,1408]{1,0:T(8,128)(2,1)}, s16[128,1408]{1,0:T(8,128)(2,1)S(1)}, u32[]{:S(2)}, u32[]{:S(2)}) %collective-permute-start.15) | collective-permute-done | bytes 360480 | tf_op jit(solution)/shard_map/ppermute | solution.py:25
  97.1 4.5 %all-to-all-start.1 = ((f32[16,3,128]{2,1,0:T(4,128)}), f32[16,3,128]{2,1,0:T(4,128)S(1)}, u32[]{:S(2)}, u32[]{:S(2)}) async-start(f32[16,3,128]{2,1,0:T(4,128)} %broadcast_in_dim.96), calls=%async_computation.1 | async-start | bytes 65536 | tf_op jit(solution)/shard_map/all_to_all | solution.py:29
  102.1 5.8 %shard_map.95.product_ref = f32[3328,128]{1,0:T(8,128)} custom-call(bf16[3328,640]{1,0:T(8,128)(2,1)} %bitcast.92, bf16[3328,640]{1,0:T(8,128)(2,1)} %collective-permute-done.b_ref, bf16[128,640]{1,0:T(8,128)(2,1)} %get-tuple-element.38.ra_ref, bf16[128,640]{1,0:T(8,128)(2,1)} %get-tuple-element.37.rb_ref), custom_call_target="tpu_custom_call" | custom-call | flops 1090519040 | bytes 10223616 | tf_op jit(solution)/shard_map/pallas_call | solution.py:48
  107.9 2.2 %all-to-all-done.1.stats_ref = f32[16,3,128]{2,1,0:T(4,128)S(1)} async-done(((f32[16,3,128]{2,1,0:T(4,128)}), f32[16,3,128]{2,1,0:T(4,128)S(1)}, u32[]{:S(2)}, u32[]{:S(2)}) %all-to-all-start.1) | async-done | bytes 24608 | tf_op jit(solution)/shard_map/all_to_all | solution.py:29
  110.7 2.6 %shard_map.96 = (bf16[3328,128]{1,0:T(8,128)(2,1)}, f32[1,128]{1,0:T(1,128)}) custom-call(f32[16,3,128]{2,1,0:T(4,128)} %copy-done.7, f32[2,128]{1,0:T(2,128)} %pad_maximum_fusion.7.own_ref, f32[3328,128]{1,0:T(8,128)} %shard_map.95.product_ref, bf16[3328,128]{1,0:T(8,128)(2,1)} %shard_map.93.target_ref), custom_call_target="tpu_custom_call" | custom-call | flops 1703936 | bytes 3407872 | tf_op jit(solution)/shard_map/pallas_call | solution.py:129
  113.3 6.1 %all-to-all-start.2 = ((bf16[16,208,128]{2,1,0:T(8,128)(2,1)}), bf16[16,208,128]{2,1,0:T(8,128)(2,1)S(1)}, u32[]{:S(2)}, u32[]{:S(2)}) async-start(bf16[16,208,128]{2,1,0:T(8,128)(2,1)} %bitcast.106), calls=%async_computation.2 | async-start | bytes 1703936 | tf_op jit(solution)/shard_map/all_to_all | solution.py:29
  121.0 15.9 %all-to-all-done.2 = bf16[16,208,128]{2,1,0:T(8,128)(2,1)S(1)} async-done(((bf16[16,208,128]{2,1,0:T(8,128)(2,1)}), bf16[16,208,128]{2,1,0:T(8,128)(2,1)S(1)}, u32[]{:S(2)}, u32[]{:S(2)}) %all-to-all-start.2) | async-done | bytes 852000 | tf_op jit(solution)/shard_map/all_to_all | solution.py:29
  137.2 2.4 %convolution_convert_fusion.2 = bf16[128,3328]{1,0:T(8,128)(2,1)S(1)} fusion(bf16[416,6656]{1,0:T(8,128)(2,1)} %copy-done, s32[]{:T(128)S(6)} %select_n.215, bf16[208,128]{1,0:T(8,128)(2,1)S(1)} %get-tuple-element.43, bf16[208,128]{1,0:T(8,128)(2,1)S(1)} %get-tuple-element.24), kind=kOutput, calls=%fused_computation.6 | convolution fusion | flops 355057664 | bytes 3727364 | tf_op jit(solution)/shard_map/dot_general | solution.py:33
  141.5 2.4 %collective-permute-start.17 = (bf16[128,1664]{1,0:T(8,128)(2,1)}, bf16[128,1664]{1,0:T(8,128)(2,1)S(1)}, u32[]{:S(2)}, u32[]{:S(2)}) collective-permute-start(bf16[128,1664]{1,0:T(8,128)(2,1)} %get-tuple-element.33), channel_id=1, source_target_pairs={{0,64},{64,128},{128,192},{192,0},{1,65},{65,129},{129,193},{193,1... | collective-permute-start | bytes 1277960 | tf_op jit(solution)/shard_map/ppermute | solution.py:192
  143.9 4.9 %fusion.1 = bf16[1,3328,640]{2,1,0:T(8,128)(2,1)} fusion(bf16[3328,128]{1,0:T(8,128)(2,1)} %collective-permute-done.26, bf16[3328,128]{1,0:T(8,128)(2,1)S(1)} %bitcast.101, bf16[128,640]{1,0:T(8,128)(2,1)} %collective-permute-done.27, bf16[128,640]{1,0:T(8,128)(2,1)S(1)} %get-tuple-element.35), kind=kOutput, calls=%fused_computation.3 | convolution fusion | flops 1096712192 | bytes 6291456 | tf_op jit(solution)/shard_map/dot_general | solution.py:33
  150.9 3.8 %collective-permute-start.19 = (bf16[32,3328]{1,0:T(8,128)(2,1)S(1)}, bf16[32,3328]{1,0:T(8,128)(2,1)S(1)}, u32[]{:S(2)}, u32[]{:S(2)}) collective-permute-start(bf16[32,3328]{1,0:T(8,128)(2,1)S(1)} %get-tuple-element.31), channel_id=1, source_target_pairs={{0,33},{32,1},{1,32},{33,0},{2,35},{34,3},{3,34},{35,2},{4,37},{36... | collective-permute-start | bytes 638984 | tf_op jit(solution)/shard_map/ppermute | solution.py:298
  154.9 3.8 %collective-permute-done.18 = bf16[32,3328]{1,0:T(8,128)(2,1)S(1)} collective-permute-done((bf16[32,3328]{1,0:T(8,128)(2,1)S(1)}, bf16[32,3328]{1,0:T(8,128)(2,1)S(1)}, u32[]{:S(2)}, u32[]{:S(2)}) %collective-permute-start.18) | collective-permute-done | bytes 213024 | tf_op jit(solution)/shard_map/ppermute | solution.py:298
  158.7 5.4 %collective-permute-done.19 = bf16[32,3328]{1,0:T(8,128)(2,1)S(1)} collective-permute-done((bf16[32,3328]{1,0:T(8,128)(2,1)S(1)}, bf16[32,3328]{1,0:T(8,128)(2,1)S(1)}, u32[]{:S(2)}, u32[]{:S(2)}) %collective-permute-start.19) | collective-permute-done | bytes 213024 | tf_op jit(solution)/shard_map/ppermute | solution.py:298
  165.0 4.3 %all-to-all-start.3 = ((bf16[8,4,3328]{2,1,0:T(4,128)(2,1)}), bf16[8,4,3328]{2,1,0:T(4,128)(2,1)S(1)}, u32[]{:S(2)}, u32[]{:S(2)}) async-start(bf16[8,4,3328]{2,1,0:T(4,128)(2,1)} %reshape.152), calls=%async_computation.3 | async-start | bytes 425984 | tf_op jit(solution)/shard_map/all_to_all | solution.py:29
  169.9 9.3 %all-to-all-done.3 = bf16[8,4,3328]{2,1,0:T(4,128)(2,1)S(1)} async-done(((bf16[8,4,3328]{2,1,0:T(4,128)(2,1)}), bf16[8,4,3328]{2,1,0:T(4,128)(2,1)S(1)}, u32[]{:S(2)}, u32[]{:S(2)}) %all-to-all-start.3) | async-done | bytes 213024 | tf_op jit(solution)/shard_map/all_to_all | solution.py:29
  179.6 2.1 %collective-permute-start.22 = (f32[4,3328]{1,0:T(4,128)S(1)}, f32[4,3328]{1,0:T(4,128)S(1)}, u32[]{:S(2)}, u32[]{:S(2)}) collective-permute-start(f32[4,3328]{1,0:T(4,128)S(1)} %convert_reduce_fusion.1), channel_id=1, source_target_pairs={{0,64},{64,128},{128,192},{192,0},{1,65},{65,129},{129,193},{193,1... | collective-permute-start | bytes 159752 | tf_op jit(solution)/shard_map/ppermute | solution.py:192
  181.7 3.2 %fusion = bf16[1,6656,104]{1,2,0:T(8,128)(2,1)} fusion(bf16[128,6656]{1,0:T(8,128)(2,1)} %collective-permute-done.24, bf16[128,6656]{1,0:T(8,128)(2,1)S(1)} %bitcast.104, bf16[104,128]{1,0:T(8,128)(2,1)S(1)} %get-tuple-element.45, bf16[104,128]{1,0:T(8,128)(2,1)S(1)} %dynamic-slice_convert_fusion), kind=kOutput, calls=%fused_computation.1 | convolution fusion | flops 362033152 | bytes 4845568 | tf_op jit(solution)/shard_map/dot_general | solution.py:33
  (147 shorter events, 37.5 us)
Async XLA Ops:
  0.6 9.7 %collective-permute-start.2 = (bf16[4,6656]{1,0:T(4,128)(2,1)}, bf16[4,6656]{1,0:T(4,128)(2,1)S(1)}, u32[]{:S(2)}, u32[]{:S(2)}) collective-permute-start(bf16[4,6656]{1,0:T(4,128)(2,1)} %param.6), channel_id=1, source_target_pairs={{0,4},{4,8},{8,12},{12,16},{16,20},{20,24},{24,28},{28,0},{1,5},{5... | collective-permute-start | bytes 159752 | tf_op jit(solution)/shard_map/ppermute | solution.py:200
  2.6 7.8 %collective-permute-start.3 = (bf16[4,6656]{1,0:T(4,128)(2,1)}, bf16[4,6656]{1,0:T(4,128)(2,1)S(1)}, u32[]{:S(2)}, u32[]{:S(2)}) collective-permute-start(bf16[4,6656]{1,0:T(4,128)(2,1)} %param.6), channel_id=1, source_target_pairs={{0,28},{4,0},{8,4},{12,8},{16,12},{20,16},{24,20},{28,24},{1,29},{... | collective-permute-start | bytes 159752 | tf_op jit(solution)/shard_map/ppermute | solution.py:200
  6.7 39.3 %collective-permute-start.1 = (bf16[104,6656]{1,0:T(8,128)(2,1)}, bf16[104,6656]{1,0:T(8,128)(2,1)}, u32[]{:S(2)}, u32[]{:S(2)}) collective-permute-start(bf16[104,6656]{1,0:T(8,128)(2,1)} %bitcast.105), channel_id=1, source_target_pairs={{0,2},{2,0},{1,3},{3,1},{4,6},{6,4},{5,7},{7,5},{8,10},{10,8},{9,1... | collective-permute-start | bytes 4153352 | tf_op jit(solution)/shard_map/ppermute | solution.py:25
  7.3 2.6 %collective-permute-start.14 = (f32[104]{0:T(128)S(1)}, f32[104]{0:T(128)S(1)}, u32[]{:S(2)}, u32[]{:S(2)}) collective-permute-start(f32[104]{0:T(128)S(1)} %bitcast_convert_fusion), channel_id=1, source_target_pairs={{0,2},{2,0},{1,3},{3,1},{4,6},{6,4},{5,7},{7,5},{8,10},{10,8},{9,1... | collective-permute-start | bytes 1256 | tf_op jit(solution)/shard_map/ppermute | solution.py:25
  7.8 55.1 %collective-permute-start = (bf16[3328,640]{1,0:T(8,128)(2,1)}, bf16[3328,640]{1,0:T(8,128)(2,1)}, u32[]{:S(2)}, u32[]{:S(2)}) collective-permute-start(bf16[3328,640]{1,0:T(8,128)(2,1)} %bitcast.89), channel_id=1, source_target_pairs={{0,2},{2,0},{1,3},{3,1},{4,6},{6,4},{5,7},{7,5},{8,10},{10,8},{9,1... | collective-permute-start | bytes 12779528 | tf_op jit(solution)/shard_map/ppermute | solution.py:25
  10.4 5.5 %collective-permute-start.4 = (bf16[4,6656]{1,0:T(4,128)(2,1)S(1)}, bf16[4,6656]{1,0:T(4,128)(2,1)S(1)}, u32[]{:S(2)}, u32[]{:S(2)}) collective-permute-start(bf16[4,6656]{1,0:T(4,128)(2,1)S(1)} %collective-permute-done.2), channel_id=1, source_target_pairs={{0,4},{4,8},{8,12},{12,16},{16,20},{20,24},{24,28},{28,0},{1,5},{5... | collective-permute-start | bytes 159752 | tf_op jit(solution)/shard_map/ppermute | solution.py:200
  10.4 5.4 %collective-permute-start.5 = (bf16[4,6656]{1,0:T(4,128)(2,1)S(1)}, bf16[4,6656]{1,0:T(4,128)(2,1)S(1)}, u32[]{:S(2)}, u32[]{:S(2)}) collective-permute-start(bf16[4,6656]{1,0:T(4,128)(2,1)S(1)} %collective-permute-done.3), channel_id=1, source_target_pairs={{0,28},{4,0},{8,4},{12,8},{16,12},{20,16},{24,20},{28,24},{1,29},{... | collective-permute-start | bytes 159752 | tf_op jit(solution)/shard_map/ppermute | solution.py:200
  15.8 5.3 %collective-permute-start.6 = (bf16[4,6656]{1,0:T(4,128)(2,1)S(1)}, bf16[4,6656]{1,0:T(4,128)(2,1)S(1)}, u32[]{:S(2)}, u32[]{:S(2)}) collective-permute-start(bf16[4,6656]{1,0:T(4,128)(2,1)S(1)} %collective-permute-done.4), channel_id=1, source_target_pairs={{0,4},{4,8},{8,12},{12,16},{16,20},{20,24},{24,28},{28,0},{1,5},{5... | collective-permute-start | bytes 159752 | tf_op jit(solution)/shard_map/ppermute | solution.py:200
  15.8 5.4 %collective-permute-start.7 = (bf16[4,6656]{1,0:T(4,128)(2,1)S(1)}, bf16[4,6656]{1,0:T(4,128)(2,1)S(1)}, u32[]{:S(2)}, u32[]{:S(2)}) collective-permute-start(bf16[4,6656]{1,0:T(4,128)(2,1)S(1)} %collective-permute-done.5), channel_id=1, source_target_pairs={{0,28},{4,0},{8,4},{12,8},{16,12},{20,16},{24,20},{28,24},{1,29},{... | collective-permute-start | bytes 159752 | tf_op jit(solution)/shard_map/ppermute | solution.py:200
  21.2 5.1 %collective-permute-start.8 = (bf16[4,3328]{1,0:T(4,128)(2,1)S(1)}, bf16[4,3328]{1,0:T(4,128)(2,1)S(1)}, u32[]{:S(2)}, u32[]{:S(2)}) collective-permute-start(bf16[4,3328]{1,0:T(4,128)(2,1)S(1)} %slice.56), channel_id=1, source_target_pairs={{0,4},{4,8},{8,12},{12,16},{16,20},{20,24},{24,28},{28,0},{1,5},{5... | collective-permute-start | bytes 79880 | tf_op jit(solution)/shard_map/ppermute | solution.py:200
  21.3 5.0 %collective-permute-start.9 = (bf16[4,3328]{1,0:T(4,128)(2,1)S(1)}, bf16[4,3328]{1,0:T(4,128)(2,1)S(1)}, u32[]{:S(2)}, u32[]{:S(2)}) collective-permute-start(bf16[4,3328]{1,0:T(4,128)(2,1)S(1)} %slice.57), channel_id=1, source_target_pairs={{0,28},{4,0},{8,4},{12,8},{16,12},{20,16},{24,20},{28,24},{1,29},{... | collective-permute-start | bytes 79880 | tf_op jit(solution)/shard_map/ppermute | solution.py:200
  28.1 10.6 %collective-permute-start.10 = (bf16[32,6656]{1,0:T(8,128)(2,1)}, bf16[32,6656]{1,0:T(8,128)(2,1)S(1)}, u32[]{:S(2)}, u32[]{:S(2)}) collective-permute-start(bf16[32,6656]{1,0:T(8,128)(2,1)} %reshape.147), channel_id=1, source_target_pairs={{0,32},{32,1},{1,33},{33,0},{2,34},{34,3},{3,35},{35,2},{4,36},{36... | collective-permute-start | bytes 1277960 | tf_op jit(solution)/shard_map/ppermute | solution.py:207
  29.7 10.2 %collective-permute-start.11 = (bf16[32,6656]{1,0:T(8,128)(2,1)}, bf16[32,6656]{1,0:T(8,128)(2,1)S(1)}, u32[]{:S(2)}, u32[]{:S(2)}) collective-permute-start(bf16[32,6656]{1,0:T(8,128)(2,1)} %reshape.147), channel_id=1, source_target_pairs={{0,33},{32,0},{1,32},{33,1},{2,35},{34,2},{3,34},{35,3},{4,37},{36... | collective-permute-start | bytes 1277960 | tf_op jit(solution)/shard_map/ppermute | solution.py:207
  38.7 7.1 %collective-permute-start.12 = (bf16[16,6656]{1,0:T(8,128)(2,1)S(1)}, bf16[16,6656]{1,0:T(8,128)(2,1)S(1)}, u32[]{:S(2)}, u32[]{:S(2)}) collective-permute-start(bf16[16,6656]{1,0:T(8,128)(2,1)S(1)} %slice.58), channel_id=1, source_target_pairs={{0,32},{32,1},{1,33},{33,0},{2,34},{34,3},{3,35},{35,2},{4,36},{36... | collective-permute-start | bytes 638984 | tf_op jit(solution)/shard_map/ppermute | solution.py:207
  39.8 6.1 %collective-permute-start.13 = (bf16[16,6656]{1,0:T(8,128)(2,1)S(1)}, bf16[16,6656]{1,0:T(8,128)(2,1)S(1)}, u32[]{:S(2)}, u32[]{:S(2)}) collective-permute-start(bf16[16,6656]{1,0:T(8,128)(2,1)S(1)} %slice.59), channel_id=1, source_target_pairs={{0,33},{32,0},{1,32},{33,1},{2,35},{34,2},{3,34},{35,3},{4,37},{36... | collective-permute-start | bytes 638984 | tf_op jit(solution)/shard_map/ppermute | solution.py:207
  52.9 25.1 %all-to-all-start = ((bf16[16,208,128]{2,1,0:T(8,128)(2,1)}), bf16[16,208,128]{2,1,0:T(8,128)(2,1)S(1)}, u32[]{:S(2)}, u32[]{:S(2)}) async-start(bf16[16,208,128]{2,1,0:T(8,128)(2,1)} %broadcast_in_dim.94), calls=%async_computation | async-start | bytes 1703936 | tf_op jit(solution)/shard_map/all_to_all | solution.py:29
  84.7 9.1 %collective-permute-start.15 = (s16[128,1408]{1,0:T(8,128)(2,1)}, s16[128,1408]{1,0:T(8,128)(2,1)S(1)}, u32[]{:S(2)}, u32[]{:S(2)}) collective-permute-start(s16[128,1408]{1,0:T(8,128)(2,1)} %get-tuple-element.12), channel_id=1, source_target_pairs={{0,1},{1,0},{2,3},{3,2},{4,5},{5,4},{6,7},{7,6},{8,9},{9,8},{10,11... | collective-permute-start | bytes 1081352 | tf_op jit(solution)/shard_map/ppermute | solution.py:25
  97.1 13.0 %all-to-all-start.1 = ((f32[16,3,128]{2,1,0:T(4,128)}), f32[16,3,128]{2,1,0:T(4,128)S(1)}, u32[]{:S(2)}, u32[]{:S(2)}) async-start(f32[16,3,128]{2,1,0:T(4,128)} %broadcast_in_dim.96), calls=%async_computation.1 | async-start | bytes 65536 | tf_op jit(solution)/shard_map/all_to_all | solution.py:29
  113.3 23.6 %all-to-all-start.2 = ((bf16[16,208,128]{2,1,0:T(8,128)(2,1)}), bf16[16,208,128]{2,1,0:T(8,128)(2,1)S(1)}, u32[]{:S(2)}, u32[]{:S(2)}) async-start(bf16[16,208,128]{2,1,0:T(8,128)(2,1)} %bitcast.106), calls=%async_computation.2 | async-start | bytes 1703936 | tf_op jit(solution)/shard_map/all_to_all | solution.py:29
  119.5 24.3 %collective-permute-start.26 = (bf16[3328,128]{1,0:T(8,128)(2,1)S(1)}, bf16[3328,128]{1,0:T(8,128)(2,1)}, u32[]{:S(2)}, u32[]{:S(2)}) collective-permute-start(bf16[3328,128]{1,0:T(8,128)(2,1)S(1)} %bitcast.100), channel_id=1, source_target_pairs={{0,2},{2,0},{1,3},{3,1},{4,6},{6,4},{5,7},{7,5},{8,10},{10,8},{9,1... | collective-permute-start | bytes 2555912 | tf_op jit(solution)/shard_map/ppermute | solution.py:25
  120.5 23.4 %collective-permute-start.27 = (bf16[128,640]{1,0:T(8,128)(2,1)}, bf16[128,640]{1,0:T(8,128)(2,1)}, u32[]{:S(2)}, u32[]{:S(2)}) collective-permute-start(bf16[128,640]{1,0:T(8,128)(2,1)} %get-tuple-element.36), channel_id=1, source_target_pairs={{0,2},{2,0},{1,3},{3,1},{4,6},{6,4},{5,7},{7,5},{8,10},{10,8},{9,1... | collective-permute-start | bytes 491528 | tf_op jit(solution)/shard_map/ppermute | solution.py:25
  140.6 9.5 %collective-permute-start.16 = (bf16[128,1664]{1,0:T(8,128)(2,1)}, bf16[128,1664]{1,0:T(8,128)(2,1)S(1)}, u32[]{:S(2)}, u32[]{:S(2)}) collective-permute-start(bf16[128,1664]{1,0:T(8,128)(2,1)} %get-tuple-element.34), channel_id=1, source_target_pairs={{0,192},{64,0},{128,64},{192,128},{1,193},{65,1},{129,65},{193,129... | collective-permute-start | bytes 1277960 | tf_op jit(solution)/shard_map/ppermute | solution.py:192
  141.5 8.7 %collective-permute-start.17 = (bf16[128,1664]{1,0:T(8,128)(2,1)}, bf16[128,1664]{1,0:T(8,128)(2,1)S(1)}, u32[]{:S(2)}, u32[]{:S(2)}) collective-permute-start(bf16[128,1664]{1,0:T(8,128)(2,1)} %get-tuple-element.33), channel_id=1, source_target_pairs={{0,64},{64,128},{128,192},{192,0},{1,65},{65,129},{129,193},{193,1... | collective-permute-start | bytes 1277960 | tf_op jit(solution)/shard_map/ppermute | solution.py:192
  143.9 37.9 %collective-permute-start.24 = (bf16[128,6656]{1,0:T(8,128)(2,1)}, bf16[128,6656]{1,0:T(8,128)(2,1)}, u32[]{:S(2)}, u32[]{:S(2)}) collective-permute-start(bf16[128,6656]{1,0:T(8,128)(2,1)} %bitcast.103), channel_id=1, source_target_pairs={{0,2},{2,0},{1,3},{3,1},{4,6},{6,4},{5,7},{7,5},{8,10},{10,8},{9,1... | collective-permute-start | bytes 5111816 | tf_op jit(solution)/shard_map/ppermute | solution.py:25
  150.5 8.2 %collective-permute-start.18 = (bf16[32,3328]{1,0:T(8,128)(2,1)S(1)}, bf16[32,3328]{1,0:T(8,128)(2,1)S(1)}, u32[]{:S(2)}, u32[]{:S(2)}) collective-permute-start(bf16[32,3328]{1,0:T(8,128)(2,1)S(1)} %get-tuple-element.30), channel_id=1, source_target_pairs={{0,32},{32,0},{1,33},{33,1},{2,34},{34,2},{3,35},{35,3},{4,36},{36... | collective-permute-start | bytes 638984 | tf_op jit(solution)/shard_map/ppermute | solution.py:298
  150.9 13.2 %collective-permute-start.19 = (bf16[32,3328]{1,0:T(8,128)(2,1)S(1)}, bf16[32,3328]{1,0:T(8,128)(2,1)S(1)}, u32[]{:S(2)}, u32[]{:S(2)}) collective-permute-start(bf16[32,3328]{1,0:T(8,128)(2,1)S(1)} %get-tuple-element.31), channel_id=1, source_target_pairs={{0,33},{32,1},{1,32},{33,0},{2,35},{34,3},{3,34},{35,2},{4,37},{36... | collective-permute-start | bytes 638984 | tf_op jit(solution)/shard_map/ppermute | solution.py:298
  154.7 9.4 %collective-permute-start.20 = (bf16[32,3328]{1,0:T(8,128)(2,1)S(1)}, bf16[32,3328]{1,0:T(8,128)(2,1)S(1)}, u32[]{:S(2)}, u32[]{:S(2)}) collective-permute-start(bf16[32,3328]{1,0:T(8,128)(2,1)S(1)} %get-tuple-element.32), channel_id=1, source_target_pairs={{0,1},{32,33},{1,0},{33,32},{2,3},{34,35},{3,2},{35,34},{4,5},{36,... | collective-permute-start | bytes 638984 | tf_op jit(solution)/shard_map/ppermute | solution.py:298
  154.8 14.5 %collective-permute-start.25 = (f32[104,128]{1,0:T(8,128)S(1)}, f32[104,128]{1,0:T(8,128)S(1)}, u32[]{:S(2)}, u32[]{:S(2)}) collective-permute-start(f32[104,128]{1,0:T(8,128)S(1)} %get-tuple-element.42), channel_id=1, source_target_pairs={{0,2},{2,0},{1,3},{3,1},{4,6},{6,4},{5,7},{7,5},{8,10},{10,8},{9,1... | collective-permute-start | bytes 159752 | tf_op jit(solution)/shard_map/ppermute | solution.py:25
  165.0 14.3 %all-to-all-start.3 = ((bf16[8,4,3328]{2,1,0:T(4,128)(2,1)}), bf16[8,4,3328]{2,1,0:T(4,128)(2,1)S(1)}, u32[]{:S(2)}, u32[]{:S(2)}) async-start(bf16[8,4,3328]{2,1,0:T(4,128)(2,1)} %reshape.152), calls=%async_computation.3 | async-start | bytes 425984 | tf_op jit(solution)/shard_map/all_to_all | solution.py:29
  179.4 5.7 %collective-permute-start.21 = (f32[4,3328]{1,0:T(4,128)S(1)}, f32[4,3328]{1,0:T(4,128)S(1)}, u32[]{:S(2)}, u32[]{:S(2)}) collective-permute-start(f32[4,3328]{1,0:T(4,128)S(1)} %convert_reduce_fusion.1), channel_id=1, source_target_pairs={{0,128},{64,192},{128,0},{192,64},{1,129},{65,193},{129,1},{193,65... | collective-permute-start | bytes 159752 | tf_op jit(solution)/shard_map/ppermute | solution.py:192
  179.6 5.5 %collective-permute-start.22 = (f32[4,3328]{1,0:T(4,128)S(1)}, f32[4,3328]{1,0:T(4,128)S(1)}, u32[]{:S(2)}, u32[]{:S(2)}) collective-permute-start(f32[4,3328]{1,0:T(4,128)S(1)} %convert_reduce_fusion.1), channel_id=1, source_target_pairs={{0,64},{64,128},{128,192},{192,0},{1,65},{65,129},{129,193},{193,1... | collective-permute-start | bytes 159752 | tf_op jit(solution)/shard_map/ppermute | solution.py:192
  181.7 5.3 %collective-permute-start.23 = (f32[4,3328]{1,0:T(4,128)S(1)}, f32[4,3328]{1,0:T(4,128)S(1)}, u32[]{:S(2)}, u32[]{:S(2)}) collective-permute-start(f32[4,3328]{1,0:T(4,128)S(1)} %convert_reduce_fusion.1), channel_id=1, source_target_pairs={{0,192},{64,0},{128,64},{192,128},{1,193},{65,1},{129,65},{193,129... | collective-permute-start | bytes 159752 | tf_op jit(solution)/shard_map/ppermute | solution.py:192
  (14 other events, 106.6 us)

commit v4 on v3

--- a/solution.py
+++ b/solution.py
@@ -111,7 +111,7 @@
 
 def combine(stats, own, product, target_cols):
     half, toks = product.shape
-    step = half // 2
+    step = half
 
     def kernel(stats_ref, own_ref, product_ref, target_ref, out_ref, ratio_ref):
         tops, rests, targets = stats_ref[:, 0, :], stats_ref[:, 1, :], stats_ref[:, 2, :]
@@ -122,7 +122,7 @@
         total = rest + jnp.sum(targets * weight, axis=0, keepdims=True)
         ratio = scale * jnp.exp(top - all_top) / total
         ratio_ref[...] = ratio
-        value = product_ref[...] * ratio - target_ref[...].astype(f32) * (scale * rest / total)
+        value = product_ref[...].astype(f32) * ratio - target_ref[...].astype(f32) * (scale * rest / total)
         out_ref[...] = value.astype(out_ref.dtype)
 
     rows = pl.BlockSpec((step, toks), lambda i: (i, 0))
@@ -202,38 +202,34 @@
     def line_index(at):
         return at % 2 * 2 + at // 2
 
-    def y_shift(value, step):
-        pairs = [(line_index(i), line_index((i + step) % n_y)) for i in range(n_y)]
+    def y_flip(value, flip):
+        pairs = [(line_index(i), line_index(i ^ flip)) for i in range(n_y)]
         return lax.ppermute(value, line, pairs)
 
-    def place(buffer, block, at, row=0, col=0):
-        return lax.dynamic_update_slice(buffer, block[None], (at, row, col))
-
-    up = down = trunk_rows
-    seen = place(jnp.zeros((n_z, rows, width), bf16), trunk_rows, z)
+    def place(buffer, block, at, row=0):
+        return lax.dynamic_update_slice(buffer, block[None], (at, row, 0))
+
+    seen = exchange(jnp.broadcast_to(trunk_rows[None], (n_y, rows, width)), line)
+    seen = seen.reshape(n_y * rows, width)
+    cut = n_y * rows // 2
+    up = down = seen
+    trunk = place(jnp.zeros((n_z, n_y * rows, width), bf16), seen, z)
     for step in range(1, n_z // 2):
         up, down = z_shift(up, 1), z_shift(down, -1)
-        seen = place(seen, up, (z - step) % n_z)
-        seen = place(seen, down, (z + step) % n_z)
-    up, down = z_shift(up[:, :half_cols], 1), z_shift(down[:, half_cols:], -1)
-    seen = place(seen, up, (z + n_z // 2) % n_z)
-    seen = place(seen, down, (z + n_z // 2) % n_z, 0, half_cols)
-
-    seen = seen.reshape(n_z * rows, width)
-    cut = n_z * rows // 2
-    trunk = place(jnp.zeros((n_y, n_z * rows, width), bf16), seen, y)
-    up, down = y_shift(seen, 1), y_shift(seen, -1)
-    trunk = place(trunk, up, (y - 1) % n_y)
-    trunk = place(trunk, down, (y + 1) % n_y)
-    trunk = place(trunk, y_shift(up[:cut], 1), (y + 2) % n_y)
-    trunk = place(trunk, y_shift(down[cut:], -1), (y + 2) % n_y, cut)
+        if step == n_z // 2 - 1:
+            up, down, res_aug = lax.optimization_barrier((up, down, res_aug))
+        trunk = place(trunk, up, (z - step) % n_z)
+        trunk = place(trunk, down, (z + step) % n_z)
+    up, down = z_shift(up[:cut], 1), z_shift(down[cut:], -1)
+    trunk = place(trunk, up, (z + n_z // 2) % n_z)
+    trunk = place(trunk, down, (z + n_z // 2) % n_z, cut)
     trunk = trunk.reshape(toks, width)
 
     def own_tokens(values):
         values = lax.dynamic_slice_in_dim(values, head + 1, 2 * toks)
         values = values.reshape(lax.axis_size("ylo"), n_z, 2, lax.axis_size("yhi"), rows)
         values = lax.dynamic_index_in_dim(values, core, 2, keepdims=False)
-        return values.transpose(2, 0, 1, 3).reshape(toks)
+        return values.transpose(1, 0, 2, 3).reshape(toks)
 
     tok_ids = own_tokens(next_ids)
     live = own_tokens(valid_mask).astype(f32)
@@ -273,7 +269,7 @@
     stats = jnp.stack([top, rest, at_target])
     stats = exchange(jnp.broadcast_to(stats[None], (n_plane, 3, toks)), plane)
     part_grad = vocab_product(
-        lm_own, lm_other, rest_own.astype(bf16), rest_other.astype(bf16), f32
+        lm_own, lm_other, rest_own.astype(bf16), rest_other.astype(bf16), bf16
     )
     part_grad, ratio = combine(stats, jnp.stack([top, scale]), part_grad, target_cols)
     ratio = ratio[0]
@@ -282,7 +278,29 @@
     pre_grad = hidden_grad * silu_grad(pre)
     pre_round = pre_grad.astype(bf16)
 
+    def grad_of(exps, hot):
+        return jnp.where(hot, ratio[:, None] * exps - scale[:, None], ratio[:, None] * exps).astype(
+            bf16
+        )
+
+    grad_own = grad_of(exp_own, hot_own)
+    grad_other = grad_of(exp_other, hot_other)
+    hidden_both = jnp.concatenate([hidden_half, swap(hidden_half, "core")], 1)
+    grad_both = jnp.concatenate([grad_own, swap(grad_other, "core")], 0)
+    lm_grad = dot(hidden_both, grad_both, ((1,), (0,))).astype(bf16)
+    pre_own = lax.dynamic_slice_in_dim(pre_grad, core * cols, cols, 0)
+    pre_sibling = swap(lax.dynamic_slice_in_dim(pre_grad, (1 - core) * cols, cols, 0), "core")
+    bias_grad = jnp.sum(pre_own, axis=1) + jnp.sum(pre_sibling, axis=1)
+    pre_both = jnp.concatenate([pre_own, pre_sibling], 1).astype(bf16)
+
+    trunk_both = jnp.concatenate([trunk, swap(trunk, "core")], 0)
+    res_grad = dot(pre_both, trunk_both, ((1,), (0,))).astype(bf16)
+    order = lax.broadcasted_iota(jnp.int32, (toks, toks), 1)
+    order_y, order_z = order // (rows * n_z), order // rows % n_z
+    order = (order_z * n_y + line_index(order_y)) * rows + order % rows
+    order = (order == lax.broadcasted_iota(jnp.int32, (toks, toks), 0)).astype(bf16)
     both_grad = jnp.concatenate([pre_round, hidden_grad.astype(bf16)], 0)
+    both_grad = dot(both_grad, order, ((1,), (0,))).astype(bf16)
     given = dot(both_grad, far, ((0,), (0,))).astype(bf16)
     got_left = shift(given[:, quarter:], 1)
     got_right = shift(given[:, :quarter], -1)
@@ -298,6 +316,7 @@
         got = lax.ppermute(sent, line, pairs)
         by_y = by_y + got.astype(f32)
     by_z = exchange(by_y.astype(bf16).reshape(n_z, rows, half_cols), "z")
+    by_z, res_grad = lax.optimization_barrier((by_z, res_grad))
     summed = jnp.sum(by_z.astype(f32), axis=0)
     here = summed + shift(summed, 2)
     there = shift(summed, 1) + shift(summed, -1)
@@ -305,23 +324,6 @@
         [jnp.where(odd == 0, here, there), jnp.where(odd == 0, there, here)], 1
     )
 
-    def grad_of(exps, hot):
-        return jnp.where(hot, ratio[:, None] * exps - scale[:, None], ratio[:, None] * exps).astype(
-            bf16
-        )
-
-    grad_own = grad_of(exp_own, hot_own)
-    grad_other = grad_of(exp_other, hot_other)
-    hidden_both = jnp.concatenate([hidden_half, swap(hidden_half, "core")], 1)
-    grad_both = jnp.concatenate([grad_own, swap(grad_other, "core")], 0)
-    lm_grad = dot(hidden_both, grad_both, ((1,), (0,))).astype(bf16)
-    pre_own = lax.dynamic_slice_in_dim(pre_grad, core * cols, cols, 0)
-    pre_sibling = swap(lax.dynamic_slice_in_dim(pre_grad, (1 - core) * cols, cols, 0), "core")
-    bias_grad = jnp.sum(pre_own, axis=1) + jnp.sum(pre_sibling, axis=1)
-    pre_both = jnp.concatenate([pre_own, pre_sibling], 1).astype(bf16)
-
-    trunk_both = jnp.concatenate([trunk, swap(trunk, "core")], 0)
-    res_grad = dot(pre_both, trunk_both, ((1,), (0,))).astype(bf16)
     return (trunk_grad, res_grad.T[None], bias_grad[None], lm_grad[None])
 
 

time: 188 us -> 181 us (0.963)
  starting transfers between devices: 59.4 us -> 55.5 us
  waiting for transfers between devices: 71 us -> 68.9 us
    ppermute x4 -> x0, waiting for transfers between devices: 10.7 us -> none  [y_shift(): return lax.ppermute(value, line, pairs)]
    ppermute x4 -> x0, starting transfers between devices: 6.81 us -> none  [y_shift(): return lax.ppermute(value, line, pairs)]
    ppermute x8, waiting for transfers between devices: 5.83 us -> 11.3 us  [z_shift(): return lax.ppermute(value, 'z', [(i, (i + step) % n_z) for i in range(n_z)])]
    all_to_all x4 -> x5, starting transfers between devices: 22.4 us -> 26 us  [exchange(): return lax.all_to_all(value, axes, 0, 0, tiled=True)]
    ppermute x5, waiting for transfers between devices: 2.95 us -> 5.63 us  [shift(): return lax.ppermute(value, 'x', [(i, (i + step) % n_x) for i in range(n_x)])]
    all_to_all x4 -> x5, waiting for transfers between devices: 36.7 us -> 36 us  [exchange(): return lax.all_to_all(value, axes, 0, 0, tiled=True)]
    dot_general x5 -> x6, matrix products: 12.7 us -> 12.9 us  [dot(): lax.dot_general(a, b, ((contract[0], contract[1]), ((), ())), preferred_e...]
  transfers between devices with their start and end apart: 32 -> 29, of which waited for: 16 -> 16; matrix products, arithmetic and copies ran while one was open for 16% -> 15% of each run, Pallas kernels for 6% -> 6%
where the time goes in v4:
time: 181 us
  waiting for transfers between devices  68.9 us (38%)
  starting transfers between devices  55.5 us (31%)
  Pallas kernels  19.9 us (11%)
  matrix products  12.9 us (7%)
  other arithmetic  12.2 us (7%)
  local copies, waits for them, and re-layouts  9.93 us (5%)
    all_to_all x5, waiting for transfers between devices, exchange(): return lax.all_to_all(value, axes, 0, 0, tiled=True)  36 us
    all_to_all x5, starting transfers between devices, exchange(): return lax.all_to_all(value, axes, 0, 0, tiled=True)  26 us
    ppermute x8, starting transfers between devices, z_shift(): return lax.ppermute(value, 'z', [(i, (i + step) % n_z) for i in range(n_z)])  15.9 us
    dot_general x6, matrix products, dot(): lax.dot_general(a, b, ((contract[0], contract[1]), ((), ())), preferred_e...  12.9 us
    ppermute x8, waiting for transfers between devices, z_shift(): return lax.ppermute(value, 'z', [(i, (i + step) % n_z) for i in range(n_z)])  11.3 us
    pallas_call x2, Pallas kernels, vocab_product(): pl.pallas_call(kernel, grid=(half // step,), in_specs=[weights, weights,...  11.3 us
    ppermute x3, waiting for transfers between devices, on_device(): got = lax.ppermute(sent, line, pairs)  8.89 us
    ppermute x8, waiting for transfers between devices, swap(): return lax.ppermute(value, axis, [(0, 1), (1, 0)])  7.09 us
  transfers between devices with their start and end apart: 29, of which 16 were waited for; matrix products, arithmetic and copies ran while one was open for 15% of the time, Pallas kernels for 6%

profile of v4, /device:TPU:6, one launch (start us, length us, event | category | flops | bytes accessed | tf_op | source)
XLA Modules:
  0.0 180.6 jit_solution(15715307267102833037)
XLA Ops:
  2.2 4.5 %all-to-all-start = ((bf16[4,4,6656]{2,1,0:T(4,128)(2,1)}), bf16[4,4,6656]{2,1,0:T(4,128)(2,1)S(1)}, u32[]{:S(2)}, u32[]{:S(2)}) async-start(bf16[4,4,6656]{2,1,0:T(4,128)(2,1)} %broadcast_in_dim.67), calls=%async_computation | async-start | bytes 425984 | tf_op jit(solution)/shard_map/all_to_all | solution.py:29
  9.8 2.9 %all-to-all-done = bf16[4,4,6656]{2,1,0:T(4,128)(2,1)S(1)} async-done(((bf16[4,4,6656]{2,1,0:T(4,128)(2,1)}), bf16[4,4,6656]{2,1,0:T(4,128)(2,1)S(1)}, u32[]{:S(2)}, u32[]{:S(2)}) %all-to-all-start) | async-done | bytes 213024 | tf_op jit(solution)/shard_map/all_to_all | solution.py:29
  15.4 3.9 %collective-permute-start.4 = (bf16[16,6656]{1,0:T(8,128)(2,1)}, bf16[16,6656]{1,0:T(8,128)(2,1)S(1)}, u32[]{:S(2)}, u32[]{:S(2)}) collective-permute-start(bf16[16,6656]{1,0:T(8,128)(2,1)} %reshape.148), channel_id=1, source_target_pairs={{0,28},{4,0},{8,4},{12,8},{16,12},{20,16},{24,20},{28,24},{1,29},{... | collective-permute-start | bytes 638984 | tf_op jit(solution)/shard_map/ppermute | solution.py:200
  19.6 3.9 %collective-permute-done.1 = bf16[16,6656]{1,0:T(8,128)(2,1)} collective-permute-done((bf16[16,6656]{1,0:T(8,128)(2,1)}, bf16[16,6656]{1,0:T(8,128)(2,1)}, u32[]{:S(2)}, u32[]{:S(2)}) %collective-permute-start.1) | collective-permute-done | bytes 213024 | tf_op jit(solution)/shard_map/ppermute | solution.py:200
  23.5 3.2 %collective-permute-start.5 = (bf16[16,6656]{1,0:T(8,128)(2,1)S(1)}, bf16[16,6656]{1,0:T(8,128)(2,1)S(1)}, u32[]{:S(2)}, u32[]{:S(2)}) collective-permute-start(bf16[16,6656]{1,0:T(8,128)(2,1)S(1)} %collective-permute-done.4), channel_id=1, source_target_pairs={{0,28},{4,0},{8,4},{12,8},{16,12},{20,16},{24,20},{28,24},{1,29},{... | collective-permute-start | bytes 638984 | tf_op jit(solution)/shard_map/ppermute | solution.py:200
  27.7 3.0 %collective-permute-done.2 = bf16[16,6656]{1,0:T(8,128)(2,1)S(1)} collective-permute-done((bf16[16,6656]{1,0:T(8,128)(2,1)}, bf16[16,6656]{1,0:T(8,128)(2,1)S(1)}, u32[]{:S(2)}, u32[]{:S(2)}) %collective-permute-start.2) | collective-permute-done | bytes 213024 | tf_op jit(solution)/shard_map/ppermute | solution.py:200
  30.8 3.2 %collective-permute-start.6 = (bf16[16,6656]{1,0:T(8,128)(2,1)S(1)}, bf16[16,6656]{1,0:T(8,128)(2,1)S(1)}, u32[]{:S(2)}, u32[]{:S(2)}) collective-permute-start(bf16[16,6656]{1,0:T(8,128)(2,1)S(1)} %collective-permute-done.5), channel_id=1, source_target_pairs={{0,28},{4,0},{8,4},{12,8},{16,12},{20,16},{24,20},{28,24},{1,29},{... | collective-permute-start | bytes 638984 | tf_op jit(solution)/shard_map/ppermute | solution.py:200
  38.7 3.5 %collective-permute-start.9 = (bf16[8,6656]{1,0:T(8,128)(2,1)S(1)}, bf16[8,6656]{1,0:T(8,128)(2,1)S(1)}, u32[]{:S(2)}, u32[]{:S(2)}) collective-permute-start(bf16[8,6656]{1,0:T(8,128)(2,1)S(1)} %slice.37), channel_id=1, source_target_pairs={{0,28},{4,0},{8,4},{12,8},{16,12},{20,16},{24,20},{28,24},{1,29},{... | collective-permute-start | bytes 319496 | tf_op jit(solution)/shard_map/ppermute | solution.py:200
  42.3 2.5 %collective-permute-done.8 = bf16[8,6656]{1,0:T(8,128)(2,1)S(1)} collective-permute-done((bf16[8,6656]{1,0:T(8,128)(2,1)S(1)}, bf16[8,6656]{1,0:T(8,128)(2,1)S(1)}, u32[]{:S(2)}, u32[]{:S(2)}) %collective-permute-start.8) | collective-permute-done | bytes 106528 | tf_op jit(solution)/shard_map/ppermute | solution.py:200
  47.7 6.7 %all-to-all-start.1 = ((bf16[16,208,128]{2,1,0:T(8,128)(2,1)}), bf16[16,208,128]{2,1,0:T(8,128)(2,1)S(1)}, u32[]{:S(2)}, u32[]{:S(2)}) async-start(bf16[16,208,128]{2,1,0:T(8,128)(2,1)} %broadcast_in_dim.77), calls=%async_computation.1 | async-start | bytes 1703936 | tf_op jit(solution)/shard_map/all_to_all | solution.py:29
  57.0 5.7 %shard_map.93.target_ref = bf16[3328,128]{1,0:T(8,128)(2,1)} custom-call(bf16[3328,640]{1,0:T(8,128)(2,1)} %bitcast.75, bf16[3328,640]{1,0:T(8,128)(2,1)} %collective-permute-done.b_ref, bf16[128,640]{1,0:T(8,128)(2,1)} %fusion.24.ra_ref, bf16[128,640]{1,0:T(8,128)(2,1)} %fusion.22.rb_ref), custom_call_target="tpu_custom_call" | custom-call | flops 1090519040 | bytes 10223616 | tf_op jit(solution)/shard_map/pallas_call | solution.py:48
  62.6 8.7 %all-to-all-done.1 = bf16[16,208,128]{2,1,0:T(8,128)(2,1)S(1)} async-done(((bf16[16,208,128]{2,1,0:T(8,128)(2,1)}), bf16[16,208,128]{2,1,0:T(8,128)(2,1)S(1)}, u32[]{:S(2)}, u32[]{:S(2)}) %all-to-all-start.1) | async-done | bytes 852000 | tf_op jit(solution)/shard_map/all_to_all | solution.py:29
  72.2 5.9 %shard_map.94 = (f32[128,1280]{1,0:T(8,128)}, s16[128,1408]{1,0:T(8,128)(2,1)}) custom-call(bf16[3328,128]{1,0:T(8,128)(2,1)} %bitcast.84, bf16[3328,640]{1,0:T(8,128)(2,1)} %bitcast.76, bf16[3328,640]{1,0:T(8,128)(2,1)} %collective-permute-done.b_ref), custom_call_target="tpu_custom_call" | custom-call | flops 1090519040 | bytes 9371648 | tf_op jit(solution)/shard_map/pallas_call | solution.py:91
  78.1 2.6 %collective-permute-start.11 = (s16[128,1408]{1,0:T(8,128)(2,1)}, s16[128,1408]{1,0:T(8,128)(2,1)S(1)}, u32[]{:S(2)}, u32[]{:S(2)}) collective-permute-start(s16[128,1408]{1,0:T(8,128)(2,1)} %get-tuple-element.20), channel_id=1, source_target_pairs={{0,1},{1,0},{2,3},{3,2},{4,5},{5,4},{6,7},{7,6},{8,9},{9,8},{10,11... | collective-permute-start | bytes 1081352 | tf_op jit(solution)/shard_map/ppermute | solution.py:25
  81.1 6.2 %collective-permute-done.11 = s16[128,1408]{1,0:T(8,128)(2,1)S(1)} collective-permute-done((s16[128,1408]{1,0:T(8,128)(2,1)}, s16[128,1408]{1,0:T(8,128)(2,1)S(1)}, u32[]{:S(2)}, u32[]{:S(2)}) %collective-permute-start.11) | collective-permute-done | bytes 360480 | tf_op jit(solution)/shard_map/ppermute | solution.py:25
  90.5 4.5 %all-to-all-start.2 = ((f32[16,3,128]{2,1,0:T(4,128)}), f32[16,3,128]{2,1,0:T(4,128)S(1)}, u32[]{:S(2)}, u32[]{:S(2)}) async-start(f32[16,3,128]{2,1,0:T(4,128)} %broadcast_in_dim.79), calls=%async_computation.2 | async-start | bytes 65536 | tf_op jit(solution)/shard_map/all_to_all | solution.py:29
  95.5 5.6 %shard_map.95.product_ref = bf16[3328,128]{1,0:T(8,128)(2,1)} custom-call(bf16[3328,640]{1,0:T(8,128)(2,1)} %bitcast.77, bf16[3328,640]{1,0:T(8,128)(2,1)} %collective-permute-done.b_ref, bf16[128,640]{1,0:T(8,128)(2,1)} %get-tuple-element.48.ra_ref, bf16[128,640]{1,0:T(8,128)(2,1)} %get-tuple-element.47.rb_ref), custom_call_target="tpu_custom_call" | custom-call | flops 1090519040 | bytes 10223616 | tf_op jit(solution)/shard_map/pallas_call | solution.py:48
  101.1 2.3 %all-to-all-done.2.stats_ref = f32[16,3,128]{2,1,0:T(4,128)S(1)} async-done(((f32[16,3,128]{2,1,0:T(4,128)}), f32[16,3,128]{2,1,0:T(4,128)S(1)}, u32[]{:S(2)}, u32[]{:S(2)}) %all-to-all-start.2) | async-done | bytes 24608 | tf_op jit(solution)/shard_map/all_to_all | solution.py:29
  104.1 2.7 %shard_map.96 = (bf16[3328,128]{1,0:T(8,128)(2,1)}, f32[1,128]{1,0:T(1,128)}) custom-call(f32[16,3,128]{2,1,0:T(4,128)} %copy-done.6, f32[2,128]{1,0:T(2,128)} %pad_maximum_fusion.4.own_ref, bf16[3328,128]{1,0:T(8,128)(2,1)} %shard_map.95.product_ref, bf16[3328,128]{1,0:T(8,128)(2,1)} %shard_map.93.target_ref), custom_call_target="tpu_custom_call" | custom-call | flops 1703936 | bytes 3407872 | tf_op jit(solution)/shard_map/pallas_call | solution.py:129
  106.8 5.9 %all-to-all-start.3 = ((bf16[16,208,128]{2,1,0:T(8,128)(2,1)}), bf16[16,208,128]{2,1,0:T(8,128)(2,1)S(1)}, u32[]{:S(2)}, u32[]{:S(2)}) async-start(bf16[16,208,128]{2,1,0:T(8,128)(2,1)} %bitcast.91), calls=%async_computation.3 | async-start | bytes 1703936 | tf_op jit(solution)/shard_map/all_to_all | solution.py:29
  114.4 15.5 %all-to-all-done.3 = bf16[16,208,128]{2,1,0:T(8,128)(2,1)S(1)} async-done(((bf16[16,208,128]{2,1,0:T(8,128)(2,1)}), bf16[16,208,128]{2,1,0:T(8,128)(2,1)S(1)}, u32[]{:S(2)}, u32[]{:S(2)}) %all-to-all-start.3) | async-done | bytes 852000 | tf_op jit(solution)/shard_map/all_to_all | solution.py:29
  130.3 2.4 %convolution_convert_fusion.2 = bf16[128,3328]{1,0:T(8,128)(2,1)S(1)} fusion(bf16[416,128]{1,0:T(8,128)(2,1)S(1)} %convolution_convert_fusion.3, bf16[416,6656]{1,0:T(8,128)(2,1)} %copy-done, s32[]{:T(128)S(6)} %select_n.214), kind=kOutput, calls=%fused_computation.5 | convolution fusion | flops 354844672 | bytes 3727364 | tf_op jit(solution)/shard_map/dot_general | solution.py:33
  134.6 2.4 %collective-permute-start.13 = (bf16[128,1664]{1,0:T(8,128)(2,1)}, bf16[128,1664]{1,0:T(8,128)(2,1)S(1)}, u32[]{:S(2)}, u32[]{:S(2)}) collective-permute-start(bf16[128,1664]{1,0:T(8,128)(2,1)} %get-tuple-element.43), channel_id=1, source_target_pairs={{0,64},{64,128},{128,192},{192,0},{1,65},{65,129},{129,193},{193,1... | collective-permute-start | bytes 1277960 | tf_op jit(solution)/shard_map/ppermute | solution.py:192
  137.0 4.9 %fusion = bf16[1,3328,640]{2,1,0:T(8,128)(2,1)} fusion(bf16[3328,128]{1,0:T(8,128)(2,1)} %collective-permute-done.22, bf16[3328,128]{1,0:T(8,128)(2,1)S(1)} %bitcast.86, bf16[128,640]{1,0:T(8,128)(2,1)} %collective-permute-done.23, bf16[128,640]{1,0:T(8,128)(2,1)S(1)} %get-tuple-element.45), kind=kOutput, calls=%fused_computation.2 | convolution fusion | flops 1096712192 | bytes 6291456 | tf_op jit(solution)/shard_map/dot_general | solution.py:33
  144.0 3.4 %collective-permute-start.15 = (bf16[32,3328]{1,0:T(8,128)(2,1)S(1)}, bf16[32,3328]{1,0:T(8,128)(2,1)S(1)}, u32[]{:S(2)}, u32[]{:S(2)}) collective-permute-start(bf16[32,3328]{1,0:T(8,128)(2,1)S(1)} %get-tuple-element.41), channel_id=1, source_target_pairs={{0,33},{32,1},{1,32},{33,0},{2,35},{34,3},{3,34},{35,2},{4,37},{36... | collective-permute-start | bytes 638984 | tf_op jit(solution)/shard_map/ppermute | solution.py:316
  148.0 3.8 %collective-permute-done.14 = bf16[32,3328]{1,0:T(8,128)(2,1)S(1)} collective-permute-done((bf16[32,3328]{1,0:T(8,128)(2,1)S(1)}, bf16[32,3328]{1,0:T(8,128)(2,1)S(1)}, u32[]{:S(2)}, u32[]{:S(2)}) %collective-permute-start.14) | collective-permute-done | bytes 213024 | tf_op jit(solution)/shard_map/ppermute | solution.py:316
  151.8 5.1 %collective-permute-done.15 = bf16[32,3328]{1,0:T(8,128)(2,1)S(1)} collective-permute-done((bf16[32,3328]{1,0:T(8,128)(2,1)S(1)}, bf16[32,3328]{1,0:T(8,128)(2,1)S(1)}, u32[]{:S(2)}, u32[]{:S(2)}) %collective-permute-start.15) | collective-permute-done | bytes 213024 | tf_op jit(solution)/shard_map/ppermute | solution.py:316
  157.7 4.4 %all-to-all-start.4 = ((bf16[8,4,3328]{2,1,0:T(4,128)(2,1)}), bf16[8,4,3328]{2,1,0:T(4,128)(2,1)S(1)}, u32[]{:S(2)}, u32[]{:S(2)}) async-start(bf16[8,4,3328]{2,1,0:T(4,128)(2,1)} %reshape.153), calls=%async_computation.4 | async-start | bytes 425984 | tf_op jit(solution)/shard_map/all_to_all | solution.py:29
  162.2 3.2 %convolution_convert_fusion = bf16[104,6656]{1,0:T(8,128)(2,1)} fusion(bf16[128,6656]{1,0:T(8,128)(2,1)} %collective-permute-done.18, bf16[128,6656]{1,0:T(8,128)(2,1)S(1)} %bitcast.89, bf16[104,128]{1,0:T(8,128)(2,1)S(1)} %get-tuple-element.55, bf16[104,128]{1,0:T(8,128)(2,1)S(1)} %dynamic-slice_convert_fusion), kind=kOutput, calls=%fused_computation | convolution fusion | flops 362033152 | bytes 4845568 | tf_op jit(solution)/shard_map/dot_general | solution.py:33
  165.4 6.6 %all-to-all-done.4 = bf16[8,4,3328]{2,1,0:T(4,128)(2,1)S(1)} async-done(((bf16[8,4,3328]{2,1,0:T(4,128)(2,1)}), bf16[8,4,3328]{2,1,0:T(4,128)(2,1)S(1)}, u32[]{:S(2)}, u32[]{:S(2)}) %all-to-all-start.4) | async-done | bytes 213024 | tf_op jit(solution)/shard_map/all_to_all | solution.py:29
  172.4 2.1 %collective-permute-start.20 = (f32[4,3328]{1,0:T(4,128)S(1)}, f32[4,3328]{1,0:T(4,128)S(1)}, u32[]{:S(2)}, u32[]{:S(2)}) collective-permute-start(f32[4,3328]{1,0:T(4,128)S(1)} %convert_reduce_fusion.1), channel_id=1, source_target_pairs={{0,64},{64,128},{128,192},{192,0},{1,65},{65,129},{129,193},{193,1... | collective-permute-start | bytes 159752 | tf_op jit(solution)/shard_map/ppermute | solution.py:192
  175.0 2.8 %collective-permute-done.19 = f32[4,3328]{1,0:T(4,128)S(1)} collective-permute-done((f32[4,3328]{1,0:T(4,128)S(1)}, f32[4,3328]{1,0:T(4,128)S(1)}, u32[]{:S(2)}, u32[]{:S(2)}) %collective-permute-start.19) | collective-permute-done | bytes 53280 | tf_op jit(solution)/shard_map/ppermute | solution.py:192
  (138 shorter events, 35.1 us)
Async XLA Ops:
  2.2 10.6 %all-to-all-start = ((bf16[4,4,6656]{2,1,0:T(4,128)(2,1)}), bf16[4,4,6656]{2,1,0:T(4,128)(2,1)S(1)}, u32[]{:S(2)}, u32[]{:S(2)}) async-start(bf16[4,4,6656]{2,1,0:T(4,128)(2,1)} %broadcast_in_dim.67), calls=%async_computation | async-start | bytes 425984 | tf_op jit(solution)/shard_map/all_to_all | solution.py:29
  6.6 27.4 %collective-permute-start.7 = (bf16[104,6656]{1,0:T(8,128)(2,1)}, bf16[104,6656]{1,0:T(8,128)(2,1)}, u32[]{:S(2)}, u32[]{:S(2)}) collective-permute-start(bf16[104,6656]{1,0:T(8,128)(2,1)} %bitcast.90), channel_id=1, source_target_pairs={{0,2},{2,0},{1,3},{3,1},{4,6},{6,4},{5,7},{7,5},{8,10},{10,8},{9,1... | collective-permute-start | bytes 4153352 | tf_op jit(solution)/shard_map/ppermute | solution.py:25
  7.3 2.4 %collective-permute-start.10 = (f32[104]{0:T(128)S(1)}, f32[104]{0:T(128)S(1)}, u32[]{:S(2)}, u32[]{:S(2)}) collective-permute-start(f32[104]{0:T(128)S(1)} %bitcast_convert_fusion), channel_id=1, source_target_pairs={{0,2},{2,0},{1,3},{3,1},{4,6},{6,4},{5,7},{7,5},{8,10},{10,8},{9,1... | collective-permute-start | bytes 1256 | tf_op jit(solution)/shard_map/ppermute | solution.py:25
  7.8 49.2 %collective-permute-start = (bf16[3328,640]{1,0:T(8,128)(2,1)}, bf16[3328,640]{1,0:T(8,128)(2,1)}, u32[]{:S(2)}, u32[]{:S(2)}) collective-permute-start(bf16[3328,640]{1,0:T(8,128)(2,1)} %bitcast.74), channel_id=1, source_target_pairs={{0,2},{2,0},{1,3},{3,1},{4,6},{6,4},{5,7},{7,5},{8,10},{10,8},{9,1... | collective-permute-start | bytes 12779528 | tf_op jit(solution)/shard_map/ppermute | solution.py:25
  13.5 10.0 %collective-permute-start.1 = (bf16[16,6656]{1,0:T(8,128)(2,1)}, bf16[16,6656]{1,0:T(8,128)(2,1)}, u32[]{:S(2)}, u32[]{:S(2)}) collective-permute-start(bf16[16,6656]{1,0:T(8,128)(2,1)} %reshape.148), channel_id=1, source_target_pairs={{0,4},{4,8},{8,12},{12,16},{16,20},{20,24},{24,28},{28,0},{1,5},{5... | collective-permute-start | bytes 638984 | tf_op jit(solution)/shard_map/ppermute | solution.py:200
  15.4 8.1 %collective-permute-start.4 = (bf16[16,6656]{1,0:T(8,128)(2,1)}, bf16[16,6656]{1,0:T(8,128)(2,1)S(1)}, u32[]{:S(2)}, u32[]{:S(2)}) collective-permute-start(bf16[16,6656]{1,0:T(8,128)(2,1)} %reshape.148), channel_id=1, source_target_pairs={{0,28},{4,0},{8,4},{12,8},{16,12},{20,16},{24,20},{28,24},{1,29},{... | collective-permute-start | bytes 638984 | tf_op jit(solution)/shard_map/ppermute | solution.py:200
  19.4 14.7 %copy-start.5 = (bf16[1,6656,104]{1,2,0:T(8,128)(2,1)S(1)}, bf16[1,6656,104]{1,2,0:T(8,128)(2,1)}, u32[]{:S(2)}) copy-start(bf16[1,6656,104]{1,2,0:T(8,128)(2,1)} %param.7) | copy-start | bytes 4153348
  23.5 7.3 %collective-permute-start.2 = (bf16[16,6656]{1,0:T(8,128)(2,1)}, bf16[16,6656]{1,0:T(8,128)(2,1)S(1)}, u32[]{:S(2)}, u32[]{:S(2)}) collective-permute-start(bf16[16,6656]{1,0:T(8,128)(2,1)} %collective-permute-done.1), channel_id=1, source_target_pairs={{0,4},{4,8},{8,12},{12,16},{16,20},{20,24},{24,28},{28,0},{1,5},{5... | collective-permute-start | bytes 638984 | tf_op jit(solution)/shard_map/ppermute | solution.py:200
  23.5 7.3 %collective-permute-start.5 = (bf16[16,6656]{1,0:T(8,128)(2,1)S(1)}, bf16[16,6656]{1,0:T(8,128)(2,1)S(1)}, u32[]{:S(2)}, u32[]{:S(2)}) collective-permute-start(bf16[16,6656]{1,0:T(8,128)(2,1)S(1)} %collective-permute-done.4), channel_id=1, source_target_pairs={{0,28},{4,0},{8,4},{12,8},{16,12},{20,16},{24,20},{28,24},{1,29},{... | collective-permute-start | bytes 638984 | tf_op jit(solution)/shard_map/ppermute | solution.py:200
  30.8 7.9 %collective-permute-start.3 = (bf16[16,6656]{1,0:T(8,128)(2,1)S(1)}, bf16[16,6656]{1,0:T(8,128)(2,1)S(1)}, u32[]{:S(2)}, u32[]{:S(2)}) collective-permute-start(bf16[16,6656]{1,0:T(8,128)(2,1)S(1)} %collective-permute-done.2), channel_id=1, source_target_pairs={{0,4},{4,8},{8,12},{12,16},{16,20},{20,24},{24,28},{28,0},{1,5},{5... | collective-permute-start | bytes 638984 | tf_op jit(solution)/shard_map/ppermute | solution.py:200
  30.8 7.9 %collective-permute-start.6 = (bf16[16,6656]{1,0:T(8,128)(2,1)S(1)}, bf16[16,6656]{1,0:T(8,128)(2,1)S(1)}, u32[]{:S(2)}, u32[]{:S(2)}) collective-permute-start(bf16[16,6656]{1,0:T(8,128)(2,1)S(1)} %collective-permute-done.5), channel_id=1, source_target_pairs={{0,28},{4,0},{8,4},{12,8},{16,12},{20,16},{24,20},{28,24},{1,29},{... | collective-permute-start | bytes 638984 | tf_op jit(solution)/shard_map/ppermute | solution.py:200
  38.6 6.2 %collective-permute-start.8 = (bf16[8,6656]{1,0:T(8,128)(2,1)S(1)}, bf16[8,6656]{1,0:T(8,128)(2,1)S(1)}, u32[]{:S(2)}, u32[]{:S(2)}) collective-permute-start(bf16[8,6656]{1,0:T(8,128)(2,1)S(1)} %slice.36), channel_id=1, source_target_pairs={{0,4},{4,8},{8,12},{12,16},{16,20},{20,24},{24,28},{28,0},{1,5},{5... | collective-permute-start | bytes 319496 | tf_op jit(solution)/shard_map/ppermute | solution.py:200
  38.7 6.1 %collective-permute-start.9 = (bf16[8,6656]{1,0:T(8,128)(2,1)S(1)}, bf16[8,6656]{1,0:T(8,128)(2,1)S(1)}, u32[]{:S(2)}, u32[]{:S(2)}) collective-permute-start(bf16[8,6656]{1,0:T(8,128)(2,1)S(1)} %slice.37), channel_id=1, source_target_pairs={{0,28},{4,0},{8,4},{12,8},{16,12},{20,16},{24,20},{28,24},{1,29},{... | collective-permute-start | bytes 319496 | tf_op jit(solution)/shard_map/ppermute | solution.py:200
  47.7 23.6 %all-to-all-start.1 = ((bf16[16,208,128]{2,1,0:T(8,128)(2,1)}), bf16[16,208,128]{2,1,0:T(8,128)(2,1)S(1)}, u32[]{:S(2)}, u32[]{:S(2)}) async-start(bf16[16,208,128]{2,1,0:T(8,128)(2,1)} %broadcast_in_dim.77), calls=%async_computation.1 | async-start | bytes 1703936 | tf_op jit(solution)/shard_map/all_to_all | solution.py:29
  78.1 9.1 %collective-permute-start.11 = (s16[128,1408]{1,0:T(8,128)(2,1)}, s16[128,1408]{1,0:T(8,128)(2,1)S(1)}, u32[]{:S(2)}, u32[]{:S(2)}) collective-permute-start(s16[128,1408]{1,0:T(8,128)(2,1)} %get-tuple-element.20), channel_id=1, source_target_pairs={{0,1},{1,0},{2,3},{3,2},{4,5},{5,4},{6,7},{7,6},{8,9},{9,8},{10,11... | collective-permute-start | bytes 1081352 | tf_op jit(solution)/shard_map/ppermute | solution.py:25
  90.5 13.0 %all-to-all-start.2 = ((f32[16,3,128]{2,1,0:T(4,128)}), f32[16,3,128]{2,1,0:T(4,128)S(1)}, u32[]{:S(2)}, u32[]{:S(2)}) async-start(f32[16,3,128]{2,1,0:T(4,128)} %broadcast_in_dim.79), calls=%async_computation.2 | async-start | bytes 65536 | tf_op jit(solution)/shard_map/all_to_all | solution.py:29
  101.1 11.8 %copy-start.2 = (bf16[16,208,128]{2,1,0:T(8,128)(2,1)S(1)}, bf16[16,208,128]{2,1,0:T(8,128)(2,1)}, u32[]{:S(2)}) copy-start(bf16[16,208,128]{2,1,0:T(8,128)(2,1)} %copy-done.1) | copy-start | bytes 2555908
  106.8 23.1 %all-to-all-start.3 = ((bf16[16,208,128]{2,1,0:T(8,128)(2,1)}), bf16[16,208,128]{2,1,0:T(8,128)(2,1)S(1)}, u32[]{:S(2)}, u32[]{:S(2)}) async-start(bf16[16,208,128]{2,1,0:T(8,128)(2,1)} %bitcast.91), calls=%async_computation.3 | async-start | bytes 1703936 | tf_op jit(solution)/shard_map/all_to_all | solution.py:29
  112.9 24.1 %collective-permute-start.22 = (bf16[3328,128]{1,0:T(8,128)(2,1)S(1)}, bf16[3328,128]{1,0:T(8,128)(2,1)}, u32[]{:S(2)}, u32[]{:S(2)}) collective-permute-start(bf16[3328,128]{1,0:T(8,128)(2,1)S(1)} %bitcast.85), channel_id=1, source_target_pairs={{0,2},{2,0},{1,3},{3,1},{4,6},{6,4},{5,7},{7,5},{8,10},{10,8},{9,1... | collective-permute-start | bytes 2555912 | tf_op jit(solution)/shard_map/ppermute | solution.py:25
  113.9 23.1 %collective-permute-start.23 = (bf16[128,640]{1,0:T(8,128)(2,1)}, bf16[128,640]{1,0:T(8,128)(2,1)}, u32[]{:S(2)}, u32[]{:S(2)}) collective-permute-start(bf16[128,640]{1,0:T(8,128)(2,1)} %get-tuple-element.46), channel_id=1, source_target_pairs={{0,2},{2,0},{1,3},{3,1},{4,6},{6,4},{5,7},{7,5},{8,10},{10,8},{9,1... | collective-permute-start | bytes 491528 | tf_op jit(solution)/shard_map/ppermute | solution.py:25
  133.7 9.5 %collective-permute-start.12 = (bf16[128,1664]{1,0:T(8,128)(2,1)}, bf16[128,1664]{1,0:T(8,128)(2,1)S(1)}, u32[]{:S(2)}, u32[]{:S(2)}) collective-permute-start(bf16[128,1664]{1,0:T(8,128)(2,1)} %get-tuple-element.44), channel_id=1, source_target_pairs={{0,192},{64,0},{128,64},{192,128},{1,193},{65,1},{129,65},{193,129... | collective-permute-start | bytes 1277960 | tf_op jit(solution)/shard_map/ppermute | solution.py:192
  134.6 8.7 %collective-permute-start.13 = (bf16[128,1664]{1,0:T(8,128)(2,1)}, bf16[128,1664]{1,0:T(8,128)(2,1)S(1)}, u32[]{:S(2)}, u32[]{:S(2)}) collective-permute-start(bf16[128,1664]{1,0:T(8,128)(2,1)} %get-tuple-element.43), channel_id=1, source_target_pairs={{0,64},{64,128},{128,192},{192,0},{1,65},{65,129},{129,193},{193,1... | collective-permute-start | bytes 1277960 | tf_op jit(solution)/shard_map/ppermute | solution.py:192
  137.0 25.2 %collective-permute-start.18 = (bf16[128,6656]{1,0:T(8,128)(2,1)}, bf16[128,6656]{1,0:T(8,128)(2,1)}, u32[]{:S(2)}, u32[]{:S(2)}) collective-permute-start(bf16[128,6656]{1,0:T(8,128)(2,1)} %bitcast.88), channel_id=1, source_target_pairs={{0,2},{2,0},{1,3},{3,1},{4,6},{6,4},{5,7},{7,5},{8,10},{10,8},{9,1... | collective-permute-start | bytes 5111816 | tf_op jit(solution)/shard_map/ppermute | solution.py:25
  143.6 18.7 %copy-start.4 = (bf16[8,16,6656]{2,1,0:T(8,128)(2,1)S(1)}, bf16[8,16,6656]{2,1,0:T(8,128)(2,1)}, u32[]{:S(2)}) copy-start(bf16[8,16,6656]{2,1,0:T(8,128)(2,1)} %copy-done.3) | copy-start | bytes 5111812
  143.6 8.2 %collective-permute-start.14 = (bf16[32,3328]{1,0:T(8,128)(2,1)S(1)}, bf16[32,3328]{1,0:T(8,128)(2,1)S(1)}, u32[]{:S(2)}, u32[]{:S(2)}) collective-permute-start(bf16[32,3328]{1,0:T(8,128)(2,1)S(1)} %get-tuple-element.40), channel_id=1, source_target_pairs={{0,32},{32,0},{1,33},{33,1},{2,34},{34,2},{3,35},{35,3},{4,36},{36... | collective-permute-start | bytes 638984 | tf_op jit(solution)/shard_map/ppermute | solution.py:316
  144.0 12.8 %collective-permute-start.15 = (bf16[32,3328]{1,0:T(8,128)(2,1)S(1)}, bf16[32,3328]{1,0:T(8,128)(2,1)S(1)}, u32[]{:S(2)}, u32[]{:S(2)}) collective-permute-start(bf16[32,3328]{1,0:T(8,128)(2,1)S(1)} %get-tuple-element.41), channel_id=1, source_target_pairs={{0,33},{32,1},{1,32},{33,0},{2,35},{34,3},{3,34},{35,2},{4,37},{36... | collective-permute-start | bytes 638984 | tf_op jit(solution)/shard_map/ppermute | solution.py:316
  147.5 9.4 %collective-permute-start.16 = (bf16[32,3328]{1,0:T(8,128)(2,1)S(1)}, bf16[32,3328]{1,0:T(8,128)(2,1)S(1)}, u32[]{:S(2)}, u32[]{:S(2)}) collective-permute-start(bf16[32,3328]{1,0:T(8,128)(2,1)S(1)} %get-tuple-element.42), channel_id=1, source_target_pairs={{0,1},{32,33},{1,0},{33,32},{2,3},{34,35},{3,2},{35,34},{4,5},{36,... | collective-permute-start | bytes 638984 | tf_op jit(solution)/shard_map/ppermute | solution.py:316
  147.9 14.2 %collective-permute-start.17 = (f32[104,128]{1,0:T(8,128)S(1)}, f32[104,128]{1,0:T(8,128)S(1)}, u32[]{:S(2)}, u32[]{:S(2)}) collective-permute-start(f32[104,128]{1,0:T(8,128)S(1)} %get-tuple-element.52), channel_id=1, source_target_pairs={{0,2},{2,0},{1,3},{3,1},{4,6},{6,4},{5,7},{7,5},{8,10},{10,8},{9,1... | collective-permute-start | bytes 159752 | tf_op jit(solution)/shard_map/ppermute | solution.py:25
  157.7 14.3 %all-to-all-start.4 = ((bf16[8,4,3328]{2,1,0:T(4,128)(2,1)}), bf16[8,4,3328]{2,1,0:T(4,128)(2,1)S(1)}, u32[]{:S(2)}, u32[]{:S(2)}) async-start(bf16[8,4,3328]{2,1,0:T(4,128)(2,1)} %reshape.153), calls=%async_computation.4 | async-start | bytes 425984 | tf_op jit(solution)/shard_map/all_to_all | solution.py:29
  172.1 5.7 %collective-permute-start.19 = (f32[4,3328]{1,0:T(4,128)S(1)}, f32[4,3328]{1,0:T(4,128)S(1)}, u32[]{:S(2)}, u32[]{:S(2)}) collective-permute-start(f32[4,3328]{1,0:T(4,128)S(1)} %convert_reduce_fusion.1), channel_id=1, source_target_pairs={{0,128},{64,192},{128,0},{192,64},{1,129},{65,193},{129,1},{193,65... | collective-permute-start | bytes 159752 | tf_op jit(solution)/shard_map/ppermute | solution.py:192
  172.4 5.4 %collective-permute-start.20 = (f32[4,3328]{1,0:T(4,128)S(1)}, f32[4,3328]{1,0:T(4,128)S(1)}, u32[]{:S(2)}, u32[]{:S(2)}) collective-permute-start(f32[4,3328]{1,0:T(4,128)S(1)} %convert_reduce_fusion.1), channel_id=1, source_target_pairs={{0,64},{64,128},{128,192},{192,0},{1,65},{65,129},{129,193},{193,1... | collective-permute-start | bytes 159752 | tf_op jit(solution)/shard_map/ppermute | solution.py:192
  174.5 5.3 %collective-permute-start.21 = (f32[4,3328]{1,0:T(4,128)S(1)}, f32[4,3328]{1,0:T(4,128)S(1)}, u32[]{:S(2)}, u32[]{:S(2)}) collective-permute-start(f32[4,3328]{1,0:T(4,128)S(1)} %convert_reduce_fusion.1), channel_id=1, source_target_pairs={{0,192},{64,0},{128,64},{192,128},{1,193},{65,1},{129,65},{193,129... | collective-permute-start | bytes 159752 | tf_op jit(solution)/shard_map/ppermute | solution.py:192
  (10 other events, 50.4 us)

commit v5 on v4

--- a/solution.py
+++ b/solution.py
@@ -143,7 +143,7 @@
         cost_estimate=pl.CostEstimate(
             flops=4 * half * toks, bytes_accessed=8 * half * toks, transcendentals=0
         ),
-        compiler_params=pltpu.CompilerParams(vmem_limit_bytes=vmem_bytes),
+        compiler_params=pltpu.CompilerParams(vmem_limit_bytes=16 * 2**20),
     )(stats, own, product, target_cols)
 
 

time: 181 us -> 180 us (level)
  no operation moved by 1% of the time
where the time goes in v5:
time: 180 us; the launch traced here: 179 us
  waiting for transfers between devices  69.4 us (39%)
  starting transfers between devices  54.9 us (30%)
  Pallas kernels  18.5 us (10%)
  matrix products  12.9 us (7%)
  other arithmetic  11.7 us (6%)
  local copies, waits for them, and re-layouts  10.5 us (6%)
    all_to_all x5, waiting for transfers between devices, exchange(): return lax.all_to_all(value, axes, 0, 0, tiled=True)  36.4 us
    all_to_all x5, starting transfers between devices, exchange(): return lax.all_to_all(value, axes, 0, 0, tiled=True)  25.4 us
    ppermute x8, starting transfers between devices, z_shift(): return lax.ppermute(value, 'z', [(i, (i + step) % n_z) for i in range(n_z)])  15.9 us
    dot_general x6, matrix products, dot(): lax.dot_general(a, b, ((contract[0], contract[1]), ((), ())), preferred_e...  12.9 us
    pallas_call x2, Pallas kernels, vocab_product(): pl.pallas_call(kernel, grid=(half // step,), in_specs=[weights, weights,...  11.4 us
    ppermute x8, waiting for transfers between devices, z_shift(): return lax.ppermute(value, 'z', [(i, (i + step) % n_z) for i in range(n_z)])  11.3 us
    ppermute x3, waiting for transfers between devices, on_device(): got = lax.ppermute(sent, line, pairs)  8.9 us
    ppermute x8, waiting for transfers between devices, swap(): return lax.ppermute(value, axis, [(0, 1), (1, 0)])  7.09 us
  transfers between devices with their start and end apart: 29, of which 16 were waited for; matrix products, arithmetic and copies ran while one was open for 15% of the time, Pallas kernels for 6%

profile of v5, /device:TPU:6, one launch (start us, length us, event | category | flops | bytes accessed | tf_op | source)
XLA Modules:
  0.0 179.1 jit_solution(7445460523310592540)
XLA Ops:
  2.2 4.5 %all-to-all-start = ((bf16[4,4,6656]{2,1,0:T(4,128)(2,1)}), bf16[4,4,6656]{2,1,0:T(4,128)(2,1)S(1)}, u32[]{:S(2)}, u32[]{:S(2)}) async-start(bf16[4,4,6656]{2,1,0:T(4,128)(2,1)} %broadcast_in_dim.67), calls=%async_computation | async-start | bytes 425984 | tf_op jit(solution)/shard_map/all_to_all | solution.py:29
  9.8 2.9 %all-to-all-done = bf16[4,4,6656]{2,1,0:T(4,128)(2,1)S(1)} async-done(((bf16[4,4,6656]{2,1,0:T(4,128)(2,1)}), bf16[4,4,6656]{2,1,0:T(4,128)(2,1)S(1)}, u32[]{:S(2)}, u32[]{:S(2)}) %all-to-all-start) | async-done | bytes 213024 | tf_op jit(solution)/shard_map/all_to_all | solution.py:29
  15.4 3.9 %collective-permute-start.4 = (bf16[16,6656]{1,0:T(8,128)(2,1)}, bf16[16,6656]{1,0:T(8,128)(2,1)S(1)}, u32[]{:S(2)}, u32[]{:S(2)}) collective-permute-start(bf16[16,6656]{1,0:T(8,128)(2,1)} %reshape.148), channel_id=1, source_target_pairs={{0,28},{4,0},{8,4},{12,8},{16,12},{20,16},{24,20},{28,24},{1,29},{... | collective-permute-start | bytes 638984 | tf_op jit(solution)/shard_map/ppermute | solution.py:200
  19.6 3.9 %collective-permute-done.1 = bf16[16,6656]{1,0:T(8,128)(2,1)} collective-permute-done((bf16[16,6656]{1,0:T(8,128)(2,1)}, bf16[16,6656]{1,0:T(8,128)(2,1)}, u32[]{:S(2)}, u32[]{:S(2)}) %collective-permute-start.1) | collective-permute-done | bytes 213024 | tf_op jit(solution)/shard_map/ppermute | solution.py:200
  23.5 3.2 %collective-permute-start.5 = (bf16[16,6656]{1,0:T(8,128)(2,1)S(1)}, bf16[16,6656]{1,0:T(8,128)(2,1)S(1)}, u32[]{:S(2)}, u32[]{:S(2)}) collective-permute-start(bf16[16,6656]{1,0:T(8,128)(2,1)S(1)} %collective-permute-done.4), channel_id=1, source_target_pairs={{0,28},{4,0},{8,4},{12,8},{16,12},{20,16},{24,20},{28,24},{1,29},{... | collective-permute-start | bytes 638984 | tf_op jit(solution)/shard_map/ppermute | solution.py:200
  27.7 3.0 %collective-permute-done.2 = bf16[16,6656]{1,0:T(8,128)(2,1)S(1)} collective-permute-done((bf16[16,6656]{1,0:T(8,128)(2,1)}, bf16[16,6656]{1,0:T(8,128)(2,1)S(1)}, u32[]{:S(2)}, u32[]{:S(2)}) %collective-permute-start.2) | collective-permute-done | bytes 213024 | tf_op jit(solution)/shard_map/ppermute | solution.py:200
  30.8 3.2 %collective-permute-start.6 = (bf16[16,6656]{1,0:T(8,128)(2,1)S(1)}, bf16[16,6656]{1,0:T(8,128)(2,1)S(1)}, u32[]{:S(2)}, u32[]{:S(2)}) collective-permute-start(bf16[16,6656]{1,0:T(8,128)(2,1)S(1)} %collective-permute-done.5), channel_id=1, source_target_pairs={{0,28},{4,0},{8,4},{12,8},{16,12},{20,16},{24,20},{28,24},{1,29},{... | collective-permute-start | bytes 638984 | tf_op jit(solution)/shard_map/ppermute | solution.py:200
  38.7 3.5 %collective-permute-start.9 = (bf16[8,6656]{1,0:T(8,128)(2,1)S(1)}, bf16[8,6656]{1,0:T(8,128)(2,1)S(1)}, u32[]{:S(2)}, u32[]{:S(2)}) collective-permute-start(bf16[8,6656]{1,0:T(8,128)(2,1)S(1)} %slice.37), channel_id=1, source_target_pairs={{0,28},{4,0},{8,4},{12,8},{16,12},{20,16},{24,20},{28,24},{1,29},{... | collective-permute-start | bytes 319496 | tf_op jit(solution)/shard_map/ppermute | solution.py:200
  42.3 2.5 %collective-permute-done.8 = bf16[8,6656]{1,0:T(8,128)(2,1)S(1)} collective-permute-done((bf16[8,6656]{1,0:T(8,128)(2,1)S(1)}, bf16[8,6656]{1,0:T(8,128)(2,1)S(1)}, u32[]{:S(2)}, u32[]{:S(2)}) %collective-permute-start.8) | collective-permute-done | bytes 106528 | tf_op jit(solution)/shard_map/ppermute | solution.py:200
  47.7 6.7 %all-to-all-start.1 = ((bf16[16,208,128]{2,1,0:T(8,128)(2,1)}), bf16[16,208,128]{2,1,0:T(8,128)(2,1)S(1)}, u32[]{:S(2)}, u32[]{:S(2)}) async-start(bf16[16,208,128]{2,1,0:T(8,128)(2,1)} %broadcast_in_dim.77), calls=%async_computation.1 | async-start | bytes 1703936 | tf_op jit(solution)/shard_map/all_to_all | solution.py:29
  57.0 5.7 %shard_map.93.target_ref = bf16[3328,128]{1,0:T(8,128)(2,1)} custom-call(bf16[3328,640]{1,0:T(8,128)(2,1)} %bitcast.76, bf16[3328,640]{1,0:T(8,128)(2,1)} %collective-permute-done.b_ref, bf16[128,640]{1,0:T(8,128)(2,1)} %fusion.24.ra_ref, bf16[128,640]{1,0:T(8,128)(2,1)} %fusion.22.rb_ref), custom_call_target="tpu_custom_call" | custom-call | flops 1090519040 | bytes 10223616 | tf_op jit(solution)/shard_map/pallas_call | solution.py:48
  62.6 8.7 %all-to-all-done.1 = bf16[16,208,128]{2,1,0:T(8,128)(2,1)S(1)} async-done(((bf16[16,208,128]{2,1,0:T(8,128)(2,1)}), bf16[16,208,128]{2,1,0:T(8,128)(2,1)S(1)}, u32[]{:S(2)}, u32[]{:S(2)}) %all-to-all-start.1) | async-done | bytes 852000 | tf_op jit(solution)/shard_map/all_to_all | solution.py:29
  72.2 5.9 %shard_map.94 = (f32[128,1280]{1,0:T(8,128)}, s16[128,1408]{1,0:T(8,128)(2,1)}) custom-call(bf16[3328,128]{1,0:T(8,128)(2,1)} %bitcast.85, bf16[3328,640]{1,0:T(8,128)(2,1)} %bitcast.77, bf16[3328,640]{1,0:T(8,128)(2,1)} %collective-permute-done.b_ref), custom_call_target="tpu_custom_call" | custom-call | flops 1090519040 | bytes 9371648 | tf_op jit(solution)/shard_map/pallas_call | solution.py:91
  78.1 2.6 %collective-permute-start.11 = (s16[128,1408]{1,0:T(8,128)(2,1)}, s16[128,1408]{1,0:T(8,128)(2,1)S(1)}, u32[]{:S(2)}, u32[]{:S(2)}) collective-permute-start(s16[128,1408]{1,0:T(8,128)(2,1)} %get-tuple-element.20), channel_id=1, source_target_pairs={{0,1},{1,0},{2,3},{3,2},{4,5},{5,4},{6,7},{7,6},{8,9},{9,8},{10,11... | collective-permute-start | bytes 1081352 | tf_op jit(solution)/shard_map/ppermute | solution.py:25
  81.1 6.2 %collective-permute-done.11 = s16[128,1408]{1,0:T(8,128)(2,1)S(1)} collective-permute-done((s16[128,1408]{1,0:T(8,128)(2,1)}, s16[128,1408]{1,0:T(8,128)(2,1)S(1)}, u32[]{:S(2)}, u32[]{:S(2)}) %collective-permute-start.11) | collective-permute-done | bytes 360480 | tf_op jit(solution)/shard_map/ppermute | solution.py:25
  90.5 4.5 %all-to-all-start.2 = ((f32[16,3,128]{2,1,0:T(4,128)}), f32[16,3,128]{2,1,0:T(4,128)S(1)}, u32[]{:S(2)}, u32[]{:S(2)}) async-start(f32[16,3,128]{2,1,0:T(4,128)} %broadcast_in_dim.79), calls=%async_computation.2 | async-start | bytes 65536 | tf_op jit(solution)/shard_map/all_to_all | solution.py:29
  95.0 5.7 %shard_map.95.product_ref = bf16[3328,128]{1,0:T(8,128)(2,1)} custom-call(bf16[3328,640]{1,0:T(8,128)(2,1)} %bitcast.78, bf16[3328,640]{1,0:T(8,128)(2,1)} %collective-permute-done.b_ref, bf16[128,640]{1,0:T(8,128)(2,1)} %get-tuple-element.48.ra_ref, bf16[128,640]{1,0:T(8,128)(2,1)} %get-tuple-element.47.rb_ref), custom_call_target="tpu_custom_call" | custom-call | flops 1090519040 | bytes 10223616 | tf_op jit(solution)/shard_map/pallas_call | solution.py:48
  100.7 2.8 %all-to-all-done.2.stats_ref = f32[16,3,128]{2,1,0:T(4,128)S(1)} async-done(((f32[16,3,128]{2,1,0:T(4,128)}), f32[16,3,128]{2,1,0:T(4,128)S(1)}, u32[]{:S(2)}, u32[]{:S(2)}) %all-to-all-start.2) | async-done | bytes 24608 | tf_op jit(solution)/shard_map/all_to_all | solution.py:29
  105.9 5.4 %all-to-all-start.3 = ((bf16[16,208,128]{2,1,0:T(8,128)(2,1)}), bf16[16,208,128]{2,1,0:T(8,128)(2,1)S(1)}, u32[]{:S(2)}, u32[]{:S(2)}) async-start(bf16[16,208,128]{2,1,0:T(8,128)(2,1)} %bitcast.25), calls=%async_computation.3 | async-start | bytes 1703936 | tf_op jit(solution)/shard_map/all_to_all | solution.py:29
  112.9 15.5 %all-to-all-done.3 = bf16[16,208,128]{2,1,0:T(8,128)(2,1)S(1)} async-done(((bf16[16,208,128]{2,1,0:T(8,128)(2,1)}), bf16[16,208,128]{2,1,0:T(8,128)(2,1)S(1)}, u32[]{:S(2)}, u32[]{:S(2)}) %all-to-all-start.3) | async-done | bytes 852000 | tf_op jit(solution)/shard_map/all_to_all | solution.py:29
  128.8 2.4 %convolution_convert_fusion.2 = bf16[128,3328]{1,0:T(8,128)(2,1)S(1)} fusion(bf16[416,128]{1,0:T(8,128)(2,1)S(1)} %convolution_convert_fusion.3, bf16[416,6656]{1,0:T(8,128)(2,1)} %copy-done.2, s32[]{:T(128)S(6)} %select_n.214), kind=kOutput, calls=%fused_computation.5 | convolution fusion | flops 354844672 | bytes 3727364 | tf_op jit(solution)/shard_map/dot_general | solution.py:33
  133.1 2.4 %collective-permute-start.13 = (bf16[128,1664]{1,0:T(8,128)(2,1)}, bf16[128,1664]{1,0:T(8,128)(2,1)S(1)}, u32[]{:S(2)}, u32[]{:S(2)}) collective-permute-start(bf16[128,1664]{1,0:T(8,128)(2,1)} %get-tuple-element.43), channel_id=1, source_target_pairs={{0,64},{64,128},{128,192},{192,0},{1,65},{65,129},{129,193},{193,1... | collective-permute-start | bytes 1277960 | tf_op jit(solution)/shard_map/ppermute | solution.py:192
  135.5 4.9 %fusion = bf16[1,3328,640]{2,1,0:T(8,128)(2,1)} fusion(bf16[3328,128]{1,0:T(8,128)(2,1)} %collective-permute-done.22, bf16[3328,128]{1,0:T(8,128)(2,1)S(1)} %bitcast.87, bf16[128,640]{1,0:T(8,128)(2,1)} %collective-permute-done.23, bf16[128,640]{1,0:T(8,128)(2,1)S(1)} %get-tuple-element.45), kind=kOutput, calls=%fused_computation.2 | convolution fusion | flops 1096712192 | bytes 6291456 | tf_op jit(solution)/shard_map/dot_general | solution.py:33
  142.6 3.4 %collective-permute-start.15 = (bf16[32,3328]{1,0:T(8,128)(2,1)S(1)}, bf16[32,3328]{1,0:T(8,128)(2,1)S(1)}, u32[]{:S(2)}, u32[]{:S(2)}) collective-permute-start(bf16[32,3328]{1,0:T(8,128)(2,1)S(1)} %get-tuple-element.41), channel_id=1, source_target_pairs={{0,33},{32,1},{1,32},{33,0},{2,35},{34,3},{3,34},{35,2},{4,37},{36... | collective-permute-start | bytes 638984 | tf_op jit(solution)/shard_map/ppermute | solution.py:316
  146.5 3.8 %collective-permute-done.14 = bf16[32,3328]{1,0:T(8,128)(2,1)S(1)} collective-permute-done((bf16[32,3328]{1,0:T(8,128)(2,1)S(1)}, bf16[32,3328]{1,0:T(8,128)(2,1)S(1)}, u32[]{:S(2)}, u32[]{:S(2)}) %collective-permute-start.14) | collective-permute-done | bytes 213024 | tf_op jit(solution)/shard_map/ppermute | solution.py:316
  150.3 5.1 %collective-permute-done.15 = bf16[32,3328]{1,0:T(8,128)(2,1)S(1)} collective-permute-done((bf16[32,3328]{1,0:T(8,128)(2,1)S(1)}, bf16[32,3328]{1,0:T(8,128)(2,1)S(1)}, u32[]{:S(2)}, u32[]{:S(2)}) %collective-permute-start.15) | collective-permute-done | bytes 213024 | tf_op jit(solution)/shard_map/ppermute | solution.py:316
  156.3 4.3 %all-to-all-start.4 = ((bf16[8,4,3328]{2,1,0:T(4,128)(2,1)}), bf16[8,4,3328]{2,1,0:T(4,128)(2,1)S(1)}, u32[]{:S(2)}, u32[]{:S(2)}) async-start(bf16[8,4,3328]{2,1,0:T(4,128)(2,1)} %reshape.153), calls=%async_computation.4 | async-start | bytes 425984 | tf_op jit(solution)/shard_map/all_to_all | solution.py:29
  160.8 3.2 %convolution_convert_fusion = bf16[104,6656]{1,0:T(8,128)(2,1)} fusion(bf16[128,6656]{1,0:T(8,128)(2,1)} %collective-permute-done.18, bf16[128,6656]{1,0:T(8,128)(2,1)S(1)} %bitcast.90, bf16[104,128]{1,0:T(8,128)(2,1)S(1)} %get-tuple-element.55, bf16[104,128]{1,0:T(8,128)(2,1)S(1)} %dynamic-slice_convert_fusion), kind=kOutput, calls=%fused_computation | convolution fusion | flops 362033152 | bytes 4845568 | tf_op jit(solution)/shard_map/dot_general | solution.py:33
  163.9 6.6 %all-to-all-done.4 = bf16[8,4,3328]{2,1,0:T(4,128)(2,1)S(1)} async-done(((bf16[8,4,3328]{2,1,0:T(4,128)(2,1)}), bf16[8,4,3328]{2,1,0:T(4,128)(2,1)S(1)}, u32[]{:S(2)}, u32[]{:S(2)}) %all-to-all-start.4) | async-done | bytes 213024 | tf_op jit(solution)/shard_map/all_to_all | solution.py:29
  171.0 2.1 %collective-permute-start.20 = (f32[4,3328]{1,0:T(4,128)S(1)}, f32[4,3328]{1,0:T(4,128)S(1)}, u32[]{:S(2)}, u32[]{:S(2)}) collective-permute-start(f32[4,3328]{1,0:T(4,128)S(1)} %convert_reduce_fusion.1), channel_id=1, source_target_pairs={{0,64},{64,128},{128,192},{192,0},{1,65},{65,129},{129,193},{193,1... | collective-permute-start | bytes 159752 | tf_op jit(solution)/shard_map/ppermute | solution.py:192
  173.6 2.8 %collective-permute-done.19 = f32[4,3328]{1,0:T(4,128)S(1)} collective-permute-done((f32[4,3328]{1,0:T(4,128)S(1)}, f32[4,3328]{1,0:T(4,128)S(1)}, u32[]{:S(2)}, u32[]{:S(2)}) %collective-permute-start.19) | collective-permute-done | bytes 53280 | tf_op jit(solution)/shard_map/ppermute | solution.py:192
  176.4 2.0 %collective-permute-done.21 = f32[4,3328]{1,0:T(4,128)S(1)} collective-permute-done((f32[4,3328]{1,0:T(4,128)S(1)}, f32[4,3328]{1,0:T(4,128)S(1)}, u32[]{:S(2)}, u32[]{:S(2)}) %collective-permute-start.21) | collective-permute-done | bytes 53280 | tf_op jit(solution)/shard_map/ppermute | solution.py:192
  (138 shorter events, 34.4 us)
Async XLA Ops:
  2.2 10.6 %all-to-all-start = ((bf16[4,4,6656]{2,1,0:T(4,128)(2,1)}), bf16[4,4,6656]{2,1,0:T(4,128)(2,1)S(1)}, u32[]{:S(2)}, u32[]{:S(2)}) async-start(bf16[4,4,6656]{2,1,0:T(4,128)(2,1)} %broadcast_in_dim.67), calls=%async_computation | async-start | bytes 425984 | tf_op jit(solution)/shard_map/all_to_all | solution.py:29
  6.6 27.4 %collective-permute-start.7 = (bf16[104,6656]{1,0:T(8,128)(2,1)}, bf16[104,6656]{1,0:T(8,128)(2,1)}, u32[]{:S(2)}, u32[]{:S(2)}) collective-permute-start(bf16[104,6656]{1,0:T(8,128)(2,1)} %bitcast.91), channel_id=1, source_target_pairs={{0,2},{2,0},{1,3},{3,1},{4,6},{6,4},{5,7},{7,5},{8,10},{10,8},{9,1... | collective-permute-start | bytes 4153352 | tf_op jit(solution)/shard_map/ppermute | solution.py:25
  7.3 2.4 %collective-permute-start.10 = (f32[104]{0:T(128)S(1)}, f32[104]{0:T(128)S(1)}, u32[]{:S(2)}, u32[]{:S(2)}) collective-permute-start(f32[104]{0:T(128)S(1)} %bitcast_convert_fusion), channel_id=1, source_target_pairs={{0,2},{2,0},{1,3},{3,1},{4,6},{6,4},{5,7},{7,5},{8,10},{10,8},{9,1... | collective-permute-start | bytes 1256 | tf_op jit(solution)/shard_map/ppermute | solution.py:25
  7.8 49.2 %collective-permute-start = (bf16[3328,640]{1,0:T(8,128)(2,1)}, bf16[3328,640]{1,0:T(8,128)(2,1)}, u32[]{:S(2)}, u32[]{:S(2)}) collective-permute-start(bf16[3328,640]{1,0:T(8,128)(2,1)} %bitcast.75), channel_id=1, source_target_pairs={{0,2},{2,0},{1,3},{3,1},{4,6},{6,4},{5,7},{7,5},{8,10},{10,8},{9,1... | collective-permute-start | bytes 12779528 | tf_op jit(solution)/shard_map/ppermute | solution.py:25
  13.5 10.0 %collective-permute-start.1 = (bf16[16,6656]{1,0:T(8,128)(2,1)}, bf16[16,6656]{1,0:T(8,128)(2,1)}, u32[]{:S(2)}, u32[]{:S(2)}) collective-permute-start(bf16[16,6656]{1,0:T(8,128)(2,1)} %reshape.148), channel_id=1, source_target_pairs={{0,4},{4,8},{8,12},{12,16},{16,20},{20,24},{24,28},{28,0},{1,5},{5... | collective-permute-start | bytes 638984 | tf_op jit(solution)/shard_map/ppermute | solution.py:200
  15.4 8.1 %collective-permute-start.4 = (bf16[16,6656]{1,0:T(8,128)(2,1)}, bf16[16,6656]{1,0:T(8,128)(2,1)S(1)}, u32[]{:S(2)}, u32[]{:S(2)}) collective-permute-start(bf16[16,6656]{1,0:T(8,128)(2,1)} %reshape.148), channel_id=1, source_target_pairs={{0,28},{4,0},{8,4},{12,8},{16,12},{20,16},{24,20},{28,24},{1,29},{... | collective-permute-start | bytes 638984 | tf_op jit(solution)/shard_map/ppermute | solution.py:200
  19.4 14.7 %copy-start.7 = (bf16[1,6656,104]{1,2,0:T(8,128)(2,1)S(1)}, bf16[1,6656,104]{1,2,0:T(8,128)(2,1)}, u32[]{:S(2)}) copy-start(bf16[1,6656,104]{1,2,0:T(8,128)(2,1)} %param.7) | copy-start | bytes 4153348
  23.5 7.3 %collective-permute-start.2 = (bf16[16,6656]{1,0:T(8,128)(2,1)}, bf16[16,6656]{1,0:T(8,128)(2,1)S(1)}, u32[]{:S(2)}, u32[]{:S(2)}) collective-permute-start(bf16[16,6656]{1,0:T(8,128)(2,1)} %collective-permute-done.1), channel_id=1, source_target_pairs={{0,4},{4,8},{8,12},{12,16},{16,20},{20,24},{24,28},{28,0},{1,5},{5... | collective-permute-start | bytes 638984 | tf_op jit(solution)/shard_map/ppermute | solution.py:200
  23.5 7.3 %collective-permute-start.5 = (bf16[16,6656]{1,0:T(8,128)(2,1)S(1)}, bf16[16,6656]{1,0:T(8,128)(2,1)S(1)}, u32[]{:S(2)}, u32[]{:S(2)}) collective-permute-start(bf16[16,6656]{1,0:T(8,128)(2,1)S(1)} %collective-permute-done.4), channel_id=1, source_target_pairs={{0,28},{4,0},{8,4},{12,8},{16,12},{20,16},{24,20},{28,24},{1,29},{... | collective-permute-start | bytes 638984 | tf_op jit(solution)/shard_map/ppermute | solution.py:200
  30.8 7.9 %collective-permute-start.3 = (bf16[16,6656]{1,0:T(8,128)(2,1)S(1)}, bf16[16,6656]{1,0:T(8,128)(2,1)S(1)}, u32[]{:S(2)}, u32[]{:S(2)}) collective-permute-start(bf16[16,6656]{1,0:T(8,128)(2,1)S(1)} %collective-permute-done.2), channel_id=1, source_target_pairs={{0,4},{4,8},{8,12},{12,16},{16,20},{20,24},{24,28},{28,0},{1,5},{5... | collective-permute-start | bytes 638984 | tf_op jit(solution)/shard_map/ppermute | solution.py:200
  30.8 7.9 %collective-permute-start.6 = (bf16[16,6656]{1,0:T(8,128)(2,1)S(1)}, bf16[16,6656]{1,0:T(8,128)(2,1)S(1)}, u32[]{:S(2)}, u32[]{:S(2)}) collective-permute-start(bf16[16,6656]{1,0:T(8,128)(2,1)S(1)} %collective-permute-done.5), channel_id=1, source_target_pairs={{0,28},{4,0},{8,4},{12,8},{16,12},{20,16},{24,20},{28,24},{1,29},{... | collective-permute-start | bytes 638984 | tf_op jit(solution)/shard_map/ppermute | solution.py:200
  36.8 9.7 %copy-start.2 = (bf16[416,6656]{1,0:T(8,128)(2,1)}, bf16[416,6656]{1,0:T(8,128)(2,1)S(1)}, u32[]{:S(2)}) copy-start(bf16[416,6656]{1,0:T(8,128)(2,1)S(1)} %pad_maximum_fusion) | copy-start | bytes 16613380
  38.6 6.2 %collective-permute-start.8 = (bf16[8,6656]{1,0:T(8,128)(2,1)S(1)}, bf16[8,6656]{1,0:T(8,128)(2,1)S(1)}, u32[]{:S(2)}, u32[]{:S(2)}) collective-permute-start(bf16[8,6656]{1,0:T(8,128)(2,1)S(1)} %slice.36), channel_id=1, source_target_pairs={{0,4},{4,8},{8,12},{12,16},{16,20},{20,24},{24,28},{28,0},{1,5},{5... | collective-permute-start | bytes 319496 | tf_op jit(solution)/shard_map/ppermute | solution.py:200
  38.7 6.1 %collective-permute-start.9 = (bf16[8,6656]{1,0:T(8,128)(2,1)S(1)}, bf16[8,6656]{1,0:T(8,128)(2,1)S(1)}, u32[]{:S(2)}, u32[]{:S(2)}) collective-permute-start(bf16[8,6656]{1,0:T(8,128)(2,1)S(1)} %slice.37), channel_id=1, source_target_pairs={{0,28},{4,0},{8,4},{12,8},{16,12},{20,16},{24,20},{28,24},{1,29},{... | collective-permute-start | bytes 319496 | tf_op jit(solution)/shard_map/ppermute | solution.py:200
  47.7 23.6 %all-to-all-start.1 = ((bf16[16,208,128]{2,1,0:T(8,128)(2,1)}), bf16[16,208,128]{2,1,0:T(8,128)(2,1)S(1)}, u32[]{:S(2)}, u32[]{:S(2)}) async-start(bf16[16,208,128]{2,1,0:T(8,128)(2,1)} %broadcast_in_dim.77), calls=%async_computation.1 | async-start | bytes 1703936 | tf_op jit(solution)/shard_map/all_to_all | solution.py:29
  78.1 9.1 %collective-permute-start.11 = (s16[128,1408]{1,0:T(8,128)(2,1)}, s16[128,1408]{1,0:T(8,128)(2,1)S(1)}, u32[]{:S(2)}, u32[]{:S(2)}) collective-permute-start(s16[128,1408]{1,0:T(8,128)(2,1)} %get-tuple-element.20), channel_id=1, source_target_pairs={{0,1},{1,0},{2,3},{3,2},{4,5},{5,4},{6,7},{7,6},{8,9},{9,8},{10,11... | collective-permute-start | bytes 1081352 | tf_op jit(solution)/shard_map/ppermute | solution.py:25
  90.5 13.0 %all-to-all-start.2 = ((f32[16,3,128]{2,1,0:T(4,128)}), f32[16,3,128]{2,1,0:T(4,128)S(1)}, u32[]{:S(2)}, u32[]{:S(2)}) async-start(f32[16,3,128]{2,1,0:T(4,128)} %broadcast_in_dim.79), calls=%async_computation.2 | async-start | bytes 65536 | tf_op jit(solution)/shard_map/all_to_all | solution.py:29
  105.9 22.5 %all-to-all-start.3 = ((bf16[16,208,128]{2,1,0:T(8,128)(2,1)}), bf16[16,208,128]{2,1,0:T(8,128)(2,1)S(1)}, u32[]{:S(2)}, u32[]{:S(2)}) async-start(bf16[16,208,128]{2,1,0:T(8,128)(2,1)} %bitcast.25), calls=%async_computation.3 | async-start | bytes 1703936 | tf_op jit(solution)/shard_map/all_to_all | solution.py:29
  111.5 24.1 %collective-permute-start.22 = (bf16[3328,128]{1,0:T(8,128)(2,1)S(1)}, bf16[3328,128]{1,0:T(8,128)(2,1)}, u32[]{:S(2)}, u32[]{:S(2)}) collective-permute-start(bf16[3328,128]{1,0:T(8,128)(2,1)S(1)} %bitcast.86), channel_id=1, source_target_pairs={{0,2},{2,0},{1,3},{3,1},{4,6},{6,4},{5,7},{7,5},{8,10},{10,8},{9,1... | collective-permute-start | bytes 2555912 | tf_op jit(solution)/shard_map/ppermute | solution.py:25
  112.4 23.1 %collective-permute-start.23 = (bf16[128,640]{1,0:T(8,128)(2,1)}, bf16[128,640]{1,0:T(8,128)(2,1)}, u32[]{:S(2)}, u32[]{:S(2)}) collective-permute-start(bf16[128,640]{1,0:T(8,128)(2,1)} %get-tuple-element.46), channel_id=1, source_target_pairs={{0,2},{2,0},{1,3},{3,1},{4,6},{6,4},{5,7},{7,5},{8,10},{10,8},{9,1... | collective-permute-start | bytes 491528 | tf_op jit(solution)/shard_map/ppermute | solution.py:25
  132.3 9.5 %collective-permute-start.12 = (bf16[128,1664]{1,0:T(8,128)(2,1)}, bf16[128,1664]{1,0:T(8,128)(2,1)S(1)}, u32[]{:S(2)}, u32[]{:S(2)}) collective-permute-start(bf16[128,1664]{1,0:T(8,128)(2,1)} %get-tuple-element.44), channel_id=1, source_target_pairs={{0,192},{64,0},{128,64},{192,128},{1,193},{65,1},{129,65},{193,129... | collective-permute-start | bytes 1277960 | tf_op jit(solution)/shard_map/ppermute | solution.py:192
  133.1 8.7 %collective-permute-start.13 = (bf16[128,1664]{1,0:T(8,128)(2,1)}, bf16[128,1664]{1,0:T(8,128)(2,1)S(1)}, u32[]{:S(2)}, u32[]{:S(2)}) collective-permute-start(bf16[128,1664]{1,0:T(8,128)(2,1)} %get-tuple-element.43), channel_id=1, source_target_pairs={{0,64},{64,128},{128,192},{192,0},{1,65},{65,129},{129,193},{193,1... | collective-permute-start | bytes 1277960 | tf_op jit(solution)/shard_map/ppermute | solution.py:192
  135.5 25.2 %collective-permute-start.18 = (bf16[128,6656]{1,0:T(8,128)(2,1)}, bf16[128,6656]{1,0:T(8,128)(2,1)}, u32[]{:S(2)}, u32[]{:S(2)}) collective-permute-start(bf16[128,6656]{1,0:T(8,128)(2,1)} %bitcast.89), channel_id=1, source_target_pairs={{0,2},{2,0},{1,3},{3,1},{4,6},{6,4},{5,7},{7,5},{8,10},{10,8},{9,1... | collective-permute-start | bytes 5111816 | tf_op jit(solution)/shard_map/ppermute | solution.py:25
  142.1 18.7 %copy-start.6 = (bf16[8,16,6656]{2,1,0:T(8,128)(2,1)S(1)}, bf16[8,16,6656]{2,1,0:T(8,128)(2,1)}, u32[]{:S(2)}) copy-start(bf16[8,16,6656]{2,1,0:T(8,128)(2,1)} %copy-done.5) | copy-start | bytes 5111812
  142.1 8.2 %collective-permute-start.14 = (bf16[32,3328]{1,0:T(8,128)(2,1)S(1)}, bf16[32,3328]{1,0:T(8,128)(2,1)S(1)}, u32[]{:S(2)}, u32[]{:S(2)}) collective-permute-start(bf16[32,3328]{1,0:T(8,128)(2,1)S(1)} %get-tuple-element.40), channel_id=1, source_target_pairs={{0,32},{32,0},{1,33},{33,1},{2,34},{34,2},{3,35},{35,3},{4,36},{36... | collective-permute-start | bytes 638984 | tf_op jit(solution)/shard_map/ppermute | solution.py:316
  142.6 12.8 %collective-permute-start.15 = (bf16[32,3328]{1,0:T(8,128)(2,1)S(1)}, bf16[32,3328]{1,0:T(8,128)(2,1)S(1)}, u32[]{:S(2)}, u32[]{:S(2)}) collective-permute-start(bf16[32,3328]{1,0:T(8,128)(2,1)S(1)} %get-tuple-element.41), channel_id=1, source_target_pairs={{0,33},{32,1},{1,32},{33,0},{2,35},{34,3},{3,34},{35,2},{4,37},{36... | collective-permute-start | bytes 638984 | tf_op jit(solution)/shard_map/ppermute | solution.py:316
  146.0 9.4 %collective-permute-start.16 = (bf16[32,3328]{1,0:T(8,128)(2,1)S(1)}, bf16[32,3328]{1,0:T(8,128)(2,1)S(1)}, u32[]{:S(2)}, u32[]{:S(2)}) collective-permute-start(bf16[32,3328]{1,0:T(8,128)(2,1)S(1)} %get-tuple-element.42), channel_id=1, source_target_pairs={{0,1},{32,33},{1,0},{33,32},{2,3},{34,35},{3,2},{35,34},{4,5},{36,... | collective-permute-start | bytes 638984 | tf_op jit(solution)/shard_map/ppermute | solution.py:316
  146.4 14.2 %collective-permute-start.17 = (f32[104,128]{1,0:T(8,128)S(1)}, f32[104,128]{1,0:T(8,128)S(1)}, u32[]{:S(2)}, u32[]{:S(2)}) collective-permute-start(f32[104,128]{1,0:T(8,128)S(1)} %get-tuple-element.52), channel_id=1, source_target_pairs={{0,2},{2,0},{1,3},{3,1},{4,6},{6,4},{5,7},{7,5},{8,10},{10,8},{9,1... | collective-permute-start | bytes 159752 | tf_op jit(solution)/shard_map/ppermute | solution.py:25
  156.3 14.3 %all-to-all-start.4 = ((bf16[8,4,3328]{2,1,0:T(4,128)(2,1)}), bf16[8,4,3328]{2,1,0:T(4,128)(2,1)S(1)}, u32[]{:S(2)}, u32[]{:S(2)}) async-start(bf16[8,4,3328]{2,1,0:T(4,128)(2,1)} %reshape.153), calls=%async_computation.4 | async-start | bytes 425984 | tf_op jit(solution)/shard_map/all_to_all | solution.py:29
  170.7 5.7 %collective-permute-start.19 = (f32[4,3328]{1,0:T(4,128)S(1)}, f32[4,3328]{1,0:T(4,128)S(1)}, u32[]{:S(2)}, u32[]{:S(2)}) collective-permute-start(f32[4,3328]{1,0:T(4,128)S(1)} %convert_reduce_fusion.1), channel_id=1, source_target_pairs={{0,128},{64,192},{128,0},{192,64},{1,129},{65,193},{129,1},{193,65... | collective-permute-start | bytes 159752 | tf_op jit(solution)/shard_map/ppermute | solution.py:192
  171.0 5.4 %collective-permute-start.20 = (f32[4,3328]{1,0:T(4,128)S(1)}, f32[4,3328]{1,0:T(4,128)S(1)}, u32[]{:S(2)}, u32[]{:S(2)}) collective-permute-start(f32[4,3328]{1,0:T(4,128)S(1)} %convert_reduce_fusion.1), channel_id=1, source_target_pairs={{0,64},{64,128},{128,192},{192,0},{1,65},{65,129},{129,193},{193,1... | collective-permute-start | bytes 159752 | tf_op jit(solution)/shard_map/ppermute | solution.py:192
  173.1 5.3 %collective-permute-start.21 = (f32[4,3328]{1,0:T(4,128)S(1)}, f32[4,3328]{1,0:T(4,128)S(1)}, u32[]{:S(2)}, u32[]{:S(2)}) collective-permute-start(f32[4,3328]{1,0:T(4,128)S(1)} %convert_reduce_fusion.1), channel_id=1, source_target_pairs={{0,192},{64,0},{128,64},{192,128},{1,193},{65,1},{129,65},{193,129... | collective-permute-start | bytes 159752 | tf_op jit(solution)/shard_map/ppermute | solution.py:192
  (10 other events, 50.3 us)

commit v6 on v5

--- a/solution.py
+++ b/solution.py
@@ -109,13 +109,53 @@
     )(hidden, lm_a, lm_b)
 
 
-def combine(stats, own, product, target_cols):
+def local_softmax(logits, coded, spots, copies):
+    toks, columns = logits.shape
+    width = columns // 2
+
+    def kernel(logits_ref, coded_ref, spots_ref, total_ref, rest_a_ref, rest_b_ref, stats_ref):
+        power = coded_ref[:, columns : columns + 1].astype(jnp.int32).astype(f32)
+        code = coded_ref[:, :columns].astype(jnp.int32).astype(f32)
+        total = logits_ref[...] + code * (jnp.exp(power * ln2) * (1.0 / int16_top))
+        total_ref[...] = total
+        top = jnp.max(total, axis=1, keepdims=True)
+        rests, targets = 0.0, 0.0
+        for side, out_ref in ((0, rest_a_ref), (1, rest_b_ref)):
+            exps = jnp.exp(total[:, side * width : (side + 1) * width] - top)
+            lanes = lax.broadcasted_iota(jnp.int32, (toks, width), 1)
+            hot = lanes == spots_ref[:, side : side + 1]
+            rest = jnp.where(hot, 0.0, exps)
+            out_ref[...] = rest.astype(bf16)
+            rests = rests + jnp.sum(rest, axis=1, keepdims=True)
+            targets = targets + jnp.sum(jnp.where(hot, exps, 0.0), axis=1, keepdims=True)
+        for row, value in enumerate((top, rests, targets)):
+            line = jnp.broadcast_to(value, (toks, toks)).T[0:1]
+            stats_ref[:, row, :] = jnp.broadcast_to(line, (copies, toks))
+
+    return pl.pallas_call(
+        kernel,
+        out_shape=[
+            jax.ShapeDtypeStruct((toks, columns), f32),
+            jax.ShapeDtypeStruct((toks, width), bf16),
+            jax.ShapeDtypeStruct((toks, width), bf16),
+            jax.ShapeDtypeStruct((copies, 3, toks), f32),
+        ],
+        cost_estimate=pl.CostEstimate(
+            flops=12 * toks * columns,
+            bytes_accessed=12 * toks * columns,
+            transcendentals=toks * columns,
+        ),
+        compiler_params=pltpu.CompilerParams(vmem_limit_bytes=vmem_bytes),
+    )(logits, coded, spots)
+
+
+def combine(stats, own, scale, product, target_cols):
     half, toks = product.shape
     step = half
 
-    def kernel(stats_ref, own_ref, product_ref, target_ref, out_ref, ratio_ref):
+    def kernel(stats_ref, own_ref, scale_ref, product_ref, target_ref, out_ref, ratio_ref):
         tops, rests, targets = stats_ref[:, 0, :], stats_ref[:, 1, :], stats_ref[:, 2, :]
-        top, scale = own_ref[0:1, :], own_ref[1:2, :]
+        top, scale = own_ref[0:1, 0, :], scale_ref[...]
         all_top = jnp.max(tops, axis=0, keepdims=True)
         weight = jnp.exp(tops - all_top)
         rest = jnp.sum(rests * weight, axis=0, keepdims=True)
@@ -131,7 +171,8 @@
         grid=(half // step,),
         in_specs=[
             pl.BlockSpec(stats.shape, lambda i: (0, 0, 0)),
-            pl.BlockSpec(own.shape, lambda i: (0, 0)),
+            pl.BlockSpec(own.shape, lambda i: (0, 0, 0)),
+            pl.BlockSpec(scale.shape, lambda i: (0, 0)),
             rows,
             rows,
         ],
@@ -144,7 +185,7 @@
             flops=4 * half * toks, bytes_accessed=8 * half * toks, transcendentals=0
         ),
         compiler_params=pltpu.CompilerParams(vmem_limit_bytes=16 * 2**20),
-    )(stats, own, product, target_cols)
+    )(stats, own, scale, product, target_cols)
 
 
 def on_device(trunk_rows, res_weight, res_bias, lm_weight, next_ids, valid_mask):
@@ -252,26 +293,17 @@
     target_cols, hidden_half = lax.optimization_barrier((target_cols, hidden_half))
 
     logits, coded = vocab_logits(hidden_half, lm_own, lm_other)
-    coded = swap(coded, "yhi").astype(f32)
-    logits = logits + coded[:, : 2 * vocab_width] * (
-        jnp.exp(coded[:, 2 * vocab_width : 2 * vocab_width + 1] * ln2) * (1.0 / int16_top)
-    )
-    logits_own, logits_other = logits[:, :vocab_width], logits[:, vocab_width:]
-    top = jnp.maximum(jnp.max(logits_own, axis=1), jnp.max(logits_other, axis=1))
-    exp_own = jnp.exp(logits_own - top[:, None])
-    exp_other = jnp.exp(logits_other - top[:, None])
-    rest_own = jnp.where(hot_own, 0.0, exp_own)
-    rest_other = jnp.where(hot_other, 0.0, exp_other)
-    rest = jnp.sum(rest_own, axis=1) + jnp.sum(rest_other, axis=1)
-    at_target = jnp.sum(jnp.where(hot_own, exp_own, 0.0), axis=1) + jnp.sum(
-        jnp.where(hot_other, exp_other, 0.0), axis=1
-    )
-    stats = jnp.stack([top, rest, at_target])
-    stats = exchange(jnp.broadcast_to(stats[None], (n_plane, 3, toks)), plane)
+    coded = swap(coded, "yhi")
+    spots = jnp.stack([tok_ids - (chip * 2 + owner) * vocab_width for owner in (core, 1 - core)], 1)
+    logits, rest_own, rest_other, own_stats = local_softmax(logits, coded, spots, n_plane)
+    top = own_stats[0, 0]
+    exp_own = jnp.exp(logits[:, :vocab_width] - top[:, None])
+    exp_other = jnp.exp(logits[:, vocab_width:] - top[:, None])
+    stats = exchange(own_stats, plane)
     part_grad = vocab_product(
-        lm_own, lm_other, rest_own.astype(bf16), rest_other.astype(bf16), bf16
-    )
-    part_grad, ratio = combine(stats, jnp.stack([top, scale]), part_grad, target_cols)
+        lm_own, lm_other, rest_own, rest_other, bf16
+    )
+    part_grad, ratio = combine(stats, own_stats, scale[None], part_grad, target_cols)
     ratio = ratio[0]
     parts = exchange(part_grad.reshape(n_plane, pair, toks), plane)
     hidden_grad = jnp.sum(parts.astype(f32), axis=0)
@@ -318,8 +350,9 @@
     by_z = exchange(by_y.astype(bf16).reshape(n_z, rows, half_cols), "z")
     by_z, res_grad = lax.optimization_barrier((by_z, res_grad))
     summed = jnp.sum(by_z.astype(f32), axis=0)
-    here = summed + shift(summed, 2)
-    there = shift(summed, 1) + shift(summed, -1)
+    sent = summed.astype(bf16)
+    here = summed + shift(sent, 2).astype(f32)
+    there = shift(sent, 1).astype(f32) + shift(sent, -1).astype(f32)
     trunk_grad = jnp.concatenate(
         [jnp.where(odd == 0, here, there), jnp.where(odd == 0, there, here)], 1
     )

time: 180 us -> 180 us (level)
  other arithmetic: 11.7 us -> 9.1 us
  Pallas kernels: 18.5 us -> 20.9 us
    pallas_call x0 -> x1, Pallas kernels: none -> 2.34 us  [local_softmax(): pl.pallas_call(kernel, out_shape=[jax.ShapeDtypeStruct((toks, columns), f...]
  transfers between devices with their start and end apart: 29 -> 29, of which waited for: 16 -> 16; matrix products, arithmetic and copies ran while one was open for 15% -> 16% of each run, Pallas kernels for 6% -> 6%
where the time goes in v6:
time: 180 us; the launch traced here: 179 us
  waiting for transfers between devices  68.1 us (38%)
  starting transfers between devices  54.9 us (30%)
  Pallas kernels  20.9 us (12%)
  matrix products  12.9 us (7%)
  local copies, waits for them, and re-layouts  11.6 us (6%)
  other arithmetic  9.1 us (5%)
    all_to_all x5, waiting for transfers between devices, exchange(): return lax.all_to_all(value, axes, 0, 0, tiled=True)  36.4 us
    all_to_all x5, starting transfers between devices, exchange(): return lax.all_to_all(value, axes, 0, 0, tiled=True)  25.4 us
    ppermute x8, starting transfers between devices, z_shift(): return lax.ppermute(value, 'z', [(i, (i + step) % n_z) for i in range(n_z)])  15.9 us
    dot_general x6, matrix products, dot(): lax.dot_general(a, b, ((contract[0], contract[1]), ((), ())), preferred_e...  12.9 us
    pallas_call x2, Pallas kernels, vocab_product(): pl.pallas_call(kernel, grid=(half // step,), in_specs=[weights, weights,...  11.4 us
    ppermute x8, waiting for transfers between devices, z_shift(): return lax.ppermute(value, 'z', [(i, (i + step) % n_z) for i in range(n_z)])  11.3 us
    ppermute x3, waiting for transfers between devices, on_device(): got = lax.ppermute(sent, line, pairs)  8.91 us
    ppermute x8, waiting for transfers between devices, swap(): return lax.ppermute(value, axis, [(0, 1), (1, 0)])  6.1 us
  transfers between devices with their start and end apart: 29, of which 16 were waited for; matrix products, arithmetic and copies ran while one was open for 16% of the time, Pallas kernels for 6%

profile of v6, /device:TPU:6, one launch (start us, length us, event | category | flops | bytes accessed | tf_op | source)
XLA Modules:
  0.0 178.7 jit_solution(4049660931937298212)
XLA Ops:
  2.2 4.5 %all-to-all-start = ((bf16[4,4,6656]{2,1,0:T(4,128)(2,1)}), bf16[4,4,6656]{2,1,0:T(4,128)(2,1)S(1)}, u32[]{:S(2)}, u32[]{:S(2)}) async-start(bf16[4,4,6656]{2,1,0:T(4,128)(2,1)} %broadcast_in_dim.52), calls=%async_computation | async-start | bytes 425984 | tf_op jit(solution)/shard_map/all_to_all | solution.py:29
  9.8 2.9 %all-to-all-done = bf16[4,4,6656]{2,1,0:T(4,128)(2,1)S(1)} async-done(((bf16[4,4,6656]{2,1,0:T(4,128)(2,1)}), bf16[4,4,6656]{2,1,0:T(4,128)(2,1)S(1)}, u32[]{:S(2)}, u32[]{:S(2)}) %all-to-all-start) | async-done | bytes 213024 | tf_op jit(solution)/shard_map/all_to_all | solution.py:29
  15.4 3.9 %collective-permute-start.4 = (bf16[16,6656]{1,0:T(8,128)(2,1)}, bf16[16,6656]{1,0:T(8,128)(2,1)S(1)}, u32[]{:S(2)}, u32[]{:S(2)}) collective-permute-start(bf16[16,6656]{1,0:T(8,128)(2,1)} %reshape.127), channel_id=1, source_target_pairs={{0,28},{4,0},{8,4},{12,8},{16,12},{20,16},{24,20},{28,24},{1,29},{... | collective-permute-start | bytes 638984 | tf_op jit(solution)/shard_map/ppermute | solution.py:241
  19.6 3.9 %collective-permute-done.1 = bf16[16,6656]{1,0:T(8,128)(2,1)} collective-permute-done((bf16[16,6656]{1,0:T(8,128)(2,1)}, bf16[16,6656]{1,0:T(8,128)(2,1)}, u32[]{:S(2)}, u32[]{:S(2)}) %collective-permute-start.1) | collective-permute-done | bytes 213024 | tf_op jit(solution)/shard_map/ppermute | solution.py:241
  23.5 3.2 %collective-permute-start.5 = (bf16[16,6656]{1,0:T(8,128)(2,1)S(1)}, bf16[16,6656]{1,0:T(8,128)(2,1)S(1)}, u32[]{:S(2)}, u32[]{:S(2)}) collective-permute-start(bf16[16,6656]{1,0:T(8,128)(2,1)S(1)} %collective-permute-done.4), channel_id=1, source_target_pairs={{0,28},{4,0},{8,4},{12,8},{16,12},{20,16},{24,20},{28,24},{1,29},{... | collective-permute-start | bytes 638984 | tf_op jit(solution)/shard_map/ppermute | solution.py:241
  27.7 3.0 %collective-permute-done.2 = bf16[16,6656]{1,0:T(8,128)(2,1)S(1)} collective-permute-done((bf16[16,6656]{1,0:T(8,128)(2,1)}, bf16[16,6656]{1,0:T(8,128)(2,1)S(1)}, u32[]{:S(2)}, u32[]{:S(2)}) %collective-permute-start.2) | collective-permute-done | bytes 213024 | tf_op jit(solution)/shard_map/ppermute | solution.py:241
  30.8 3.2 %collective-permute-start.6 = (bf16[16,6656]{1,0:T(8,128)(2,1)S(1)}, bf16[16,6656]{1,0:T(8,128)(2,1)S(1)}, u32[]{:S(2)}, u32[]{:S(2)}) collective-permute-start(bf16[16,6656]{1,0:T(8,128)(2,1)S(1)} %collective-permute-done.5), channel_id=1, source_target_pairs={{0,28},{4,0},{8,4},{12,8},{16,12},{20,16},{24,20},{28,24},{1,29},{... | collective-permute-start | bytes 638984 | tf_op jit(solution)/shard_map/ppermute | solution.py:241
  38.7 3.5 %collective-permute-start.9 = (bf16[8,6656]{1,0:T(8,128)(2,1)S(1)}, bf16[8,6656]{1,0:T(8,128)(2,1)S(1)}, u32[]{:S(2)}, u32[]{:S(2)}) collective-permute-start(bf16[8,6656]{1,0:T(8,128)(2,1)S(1)} %slice.34), channel_id=1, source_target_pairs={{0,28},{4,0},{8,4},{12,8},{16,12},{20,16},{24,20},{28,24},{1,29},{... | collective-permute-start | bytes 319496 | tf_op jit(solution)/shard_map/ppermute | solution.py:241
  42.3 2.5 %collective-permute-done.8 = bf16[8,6656]{1,0:T(8,128)(2,1)S(1)} collective-permute-done((bf16[8,6656]{1,0:T(8,128)(2,1)S(1)}, bf16[8,6656]{1,0:T(8,128)(2,1)S(1)}, u32[]{:S(2)}, u32[]{:S(2)}) %collective-permute-start.8) | collective-permute-done | bytes 106528 | tf_op jit(solution)/shard_map/ppermute | solution.py:241
  47.7 6.7 %all-to-all-start.1 = ((bf16[16,208,128]{2,1,0:T(8,128)(2,1)}), bf16[16,208,128]{2,1,0:T(8,128)(2,1)S(1)}, u32[]{:S(2)}, u32[]{:S(2)}) async-start(bf16[16,208,128]{2,1,0:T(8,128)(2,1)} %broadcast_in_dim.62), calls=%async_computation.1 | async-start | bytes 1703936 | tf_op jit(solution)/shard_map/all_to_all | solution.py:29
  57.0 5.7 %shard_map.93.target_ref = bf16[3328,128]{1,0:T(8,128)(2,1)} custom-call(bf16[3328,640]{1,0:T(8,128)(2,1)} %bitcast.73, bf16[3328,640]{1,0:T(8,128)(2,1)} %collective-permute-done.b_ref, bf16[128,640]{1,0:T(8,128)(2,1)} %fusion.21.ra_ref, bf16[128,640]{1,0:T(8,128)(2,1)} %fusion.20.rb_ref), custom_call_target="tpu_custom_call" | custom-call | flops 1090519040 | bytes 10223616 | tf_op jit(solution)/shard_map/pallas_call | solution.py:48
  62.6 8.7 %all-to-all-done.1 = bf16[16,208,128]{2,1,0:T(8,128)(2,1)S(1)} async-done(((bf16[16,208,128]{2,1,0:T(8,128)(2,1)}), bf16[16,208,128]{2,1,0:T(8,128)(2,1)S(1)}, u32[]{:S(2)}, u32[]{:S(2)}) %all-to-all-start.1) | async-done | bytes 852000 | tf_op jit(solution)/shard_map/all_to_all | solution.py:29
  72.2 5.9 %shard_map.94 = (f32[128,1280]{1,0:T(8,128)}, s16[128,1408]{1,0:T(8,128)(2,1)}) custom-call(bf16[3328,128]{1,0:T(8,128)(2,1)} %bitcast.82, bf16[3328,640]{1,0:T(8,128)(2,1)} %bitcast.74, bf16[3328,640]{1,0:T(8,128)(2,1)} %collective-permute-done.b_ref), custom_call_target="tpu_custom_call" | custom-call | flops 1090519040 | bytes 9371648 | tf_op jit(solution)/shard_map/pallas_call | solution.py:91
  78.1 2.6 %collective-permute-start.11 = (s16[128,1408]{1,0:T(8,128)(2,1)}, s16[128,1408]{1,0:T(8,128)(2,1)S(1)}, u32[]{:S(2)}, u32[]{:S(2)}) collective-permute-start(s16[128,1408]{1,0:T(8,128)(2,1)} %get-tuple-element.24), channel_id=1, source_target_pairs={{0,1},{1,0},{2,3},{3,2},{4,5},{5,4},{6,7},{7,6},{8,9},{9,8},{10,11... | collective-permute-start | bytes 1081352 | tf_op jit(solution)/shard_map/ppermute | solution.py:25
  82.0 5.2 %collective-permute-done.11.coded_ref = s16[128,1408]{1,0:T(8,128)(2,1)S(1)} collective-permute-done((s16[128,1408]{1,0:T(8,128)(2,1)}, s16[128,1408]{1,0:T(8,128)(2,1)S(1)}, u32[]{:S(2)}, u32[]{:S(2)}) %collective-permute-start.11) | collective-permute-done | bytes 360480 | tf_op jit(solution)/shard_map/ppermute | solution.py:25
  88.0 2.3 %shard_map.95 = (f32[128,1280]{1,0:T(8,128)}, bf16[128,640]{1,0:T(8,128)(2,1)}, bf16[128,640]{1,0:T(8,128)(2,1)}, f32[16,3,128]{2,1,0:T(4,128)}) custom-call(f32[128,1280]{1,0:T(8,128)} %get-tuple-element.23.logits_ref, s16[128,1408]{1,0:T(8,128)(2,1)} %copy-done.10, s32[128,2]{1,0:T(8,128)} %copy.44.spots_ref), custom_call_target="tpu_custom_call" | custom-call | flops 1966080 | bytes 1966080 | tf_op jit(solution)/shard_map/pallas_call | solution.py:135
  90.3 4.5 %all-to-all-start.2 = ((f32[16,3,128]{2,1,0:T(4,128)}), f32[16,3,128]{2,1,0:T(4,128)S(1)}, u32[]{:S(2)}, u32[]{:S(2)}) async-start(f32[16,3,128]{2,1,0:T(4,128)} %get-tuple-element.25.own_ref), calls=%async_computation.2 | async-start | bytes 65536 | tf_op jit(solution)/shard_map/all_to_all | solution.py:29
  94.9 5.7 %shard_map.96.product_ref = bf16[3328,128]{1,0:T(8,128)(2,1)} custom-call(bf16[3328,640]{1,0:T(8,128)(2,1)} %bitcast.75, bf16[3328,640]{1,0:T(8,128)(2,1)} %collective-permute-done.b_ref, bf16[128,640]{1,0:T(8,128)(2,1)} %get-tuple-element.26.ra_ref, bf16[128,640]{1,0:T(8,128)(2,1)} %get-tuple-element.27.rb_ref), custom_call_target="tpu_custom_call" | custom-call | flops 1090519040 | bytes 10223616 | tf_op jit(solution)/shard_map/pallas_call | solution.py:48
  100.6 2.8 %all-to-all-done.2.stats_ref = f32[16,3,128]{2,1,0:T(4,128)S(1)} async-done(((f32[16,3,128]{2,1,0:T(4,128)}), f32[16,3,128]{2,1,0:T(4,128)S(1)}, u32[]{:S(2)}, u32[]{:S(2)}) %all-to-all-start.2) | async-done | bytes 24608 | tf_op jit(solution)/shard_map/all_to_all | solution.py:29
  105.8 5.4 %all-to-all-start.3 = ((bf16[16,208,128]{2,1,0:T(8,128)(2,1)}), bf16[16,208,128]{2,1,0:T(8,128)(2,1)S(1)}, u32[]{:S(2)}, u32[]{:S(2)}) async-start(bf16[16,208,128]{2,1,0:T(8,128)(2,1)} %bitcast.24), calls=%async_computation.3 | async-start | bytes 1703936 | tf_op jit(solution)/shard_map/all_to_all | solution.py:29
  112.8 15.5 %all-to-all-done.3 = bf16[16,208,128]{2,1,0:T(8,128)(2,1)S(1)} async-done(((bf16[16,208,128]{2,1,0:T(8,128)(2,1)}), bf16[16,208,128]{2,1,0:T(8,128)(2,1)S(1)}, u32[]{:S(2)}, u32[]{:S(2)}) %all-to-all-start.3) | async-done | bytes 852000 | tf_op jit(solution)/shard_map/all_to_all | solution.py:29
  128.7 2.4 %convolution_convert_fusion.2 = bf16[128,3328]{1,0:T(8,128)(2,1)S(1)} fusion(bf16[416,128]{1,0:T(8,128)(2,1)S(1)} %convolution_convert_fusion.3, bf16[416,6656]{1,0:T(8,128)(2,1)} %copy-done.3, s32[]{:T(128)S(6)} %select_n.196), kind=kOutput, calls=%fused_computation.5 | convolution fusion | flops 354844672 | bytes 3727364 | tf_op jit(solution)/shard_map/dot_general | solution.py:33
  133.0 2.4 %collective-permute-start.13 = (bf16[128,1664]{1,0:T(8,128)(2,1)}, bf16[128,1664]{1,0:T(8,128)(2,1)S(1)}, u32[]{:S(2)}, u32[]{:S(2)}) collective-permute-start(bf16[128,1664]{1,0:T(8,128)(2,1)} %get-tuple-element.43), channel_id=1, source_target_pairs={{0,64},{64,128},{128,192},{192,0},{1,65},{65,129},{129,193},{193,1... | collective-permute-start | bytes 1277960 | tf_op jit(solution)/shard_map/ppermute | solution.py:233
  135.4 4.9 %fusion = bf16[1,3328,640]{2,1,0:T(8,128)(2,1)} fusion(bf16[3328,128]{1,0:T(8,128)(2,1)} %collective-permute-done.22, bf16[3328,128]{1,0:T(8,128)(2,1)S(1)} %bitcast.84, bf16[128,640]{1,0:T(8,128)(2,1)} %collective-permute-done.23, bf16[128,640]{1,0:T(8,128)(2,1)S(1)} %get-tuple-element.45), kind=kOutput, calls=%fused_computation.2 | convolution fusion | flops 1096712192 | bytes 6291456 | tf_op jit(solution)/shard_map/dot_general | solution.py:33
  142.4 3.4 %collective-permute-start.15 = (bf16[32,3328]{1,0:T(8,128)(2,1)S(1)}, bf16[32,3328]{1,0:T(8,128)(2,1)S(1)}, u32[]{:S(2)}, u32[]{:S(2)}) collective-permute-start(bf16[32,3328]{1,0:T(8,128)(2,1)S(1)} %get-tuple-element.41), channel_id=1, source_target_pairs={{0,33},{32,1},{1,32},{33,0},{2,35},{34,3},{3,34},{35,2},{4,37},{36... | collective-permute-start | bytes 638984 | tf_op jit(solution)/shard_map/ppermute | solution.py:348
  146.4 3.8 %collective-permute-done.14 = bf16[32,3328]{1,0:T(8,128)(2,1)S(1)} collective-permute-done((bf16[32,3328]{1,0:T(8,128)(2,1)S(1)}, bf16[32,3328]{1,0:T(8,128)(2,1)S(1)}, u32[]{:S(2)}, u32[]{:S(2)}) %collective-permute-start.14) | collective-permute-done | bytes 213024 | tf_op jit(solution)/shard_map/ppermute | solution.py:348
  150.2 5.1 %collective-permute-done.15 = bf16[32,3328]{1,0:T(8,128)(2,1)S(1)} collective-permute-done((bf16[32,3328]{1,0:T(8,128)(2,1)S(1)}, bf16[32,3328]{1,0:T(8,128)(2,1)S(1)}, u32[]{:S(2)}, u32[]{:S(2)}) %collective-permute-start.15) | collective-permute-done | bytes 213024 | tf_op jit(solution)/shard_map/ppermute | solution.py:348
  156.2 4.4 %all-to-all-start.4 = ((bf16[8,4,3328]{2,1,0:T(4,128)(2,1)}), bf16[8,4,3328]{2,1,0:T(4,128)(2,1)S(1)}, u32[]{:S(2)}, u32[]{:S(2)}) async-start(bf16[8,4,3328]{2,1,0:T(4,128)(2,1)} %reshape.132), calls=%async_computation.4 | async-start | bytes 425984 | tf_op jit(solution)/shard_map/all_to_all | solution.py:29
  160.7 3.2 %convolution_convert_fusion = bf16[104,6656]{1,0:T(8,128)(2,1)} fusion(bf16[128,6656]{1,0:T(8,128)(2,1)} %collective-permute-done.18, bf16[128,6656]{1,0:T(8,128)(2,1)S(1)} %bitcast.87, bf16[104,128]{1,0:T(8,128)(2,1)S(1)} %get-tuple-element.53, bf16[104,128]{1,0:T(8,128)(2,1)S(1)} %dynamic-slice_convert_fusion), kind=kOutput, calls=%fused_computation | convolution fusion | flops 362033152 | bytes 4845568 | tf_op jit(solution)/shard_map/dot_general | solution.py:33
  163.9 6.6 %all-to-all-done.4 = bf16[8,4,3328]{2,1,0:T(4,128)(2,1)S(1)} async-done(((bf16[8,4,3328]{2,1,0:T(4,128)(2,1)}), bf16[8,4,3328]{2,1,0:T(4,128)(2,1)S(1)}, u32[]{:S(2)}, u32[]{:S(2)}) %all-to-all-start.4) | async-done | bytes 213024 | tf_op jit(solution)/shard_map/all_to_all | solution.py:29
  170.9 2.1 %collective-permute-start.20 = (bf16[4,3328]{1,0:T(4,128)(2,1)S(1)}, bf16[4,3328]{1,0:T(4,128)(2,1)S(1)}, u32[]{:S(2)}, u32[]{:S(2)}) collective-permute-start(bf16[4,3328]{1,0:T(4,128)(2,1)S(1)} %convert_element_type.132), channel_id=1, source_target_pairs={{0,64},{64,128},{128,192},{192,0},{1,65},{65,129},{129,193},{193,1... | collective-permute-start | bytes 79880 | tf_op jit(solution)/shard_map/ppermute | solution.py:233
  173.5 2.5 %collective-permute-done.19 = bf16[4,3328]{1,0:T(4,128)(2,1)S(1)} collective-permute-done((bf16[4,3328]{1,0:T(4,128)(2,1)S(1)}, bf16[4,3328]{1,0:T(4,128)(2,1)S(1)}, u32[]{:S(2)}, u32[]{:S(2)}) %collective-permute-start.19) | collective-permute-done | bytes 26656 | tf_op jit(solution)/shard_map/ppermute | solution.py:233
  (140 shorter events, 35.0 us)
Async XLA Ops:
  2.2 10.6 %all-to-all-start = ((bf16[4,4,6656]{2,1,0:T(4,128)(2,1)}), bf16[4,4,6656]{2,1,0:T(4,128)(2,1)S(1)}, u32[]{:S(2)}, u32[]{:S(2)}) async-start(bf16[4,4,6656]{2,1,0:T(4,128)(2,1)} %broadcast_in_dim.52), calls=%async_computation | async-start | bytes 425984 | tf_op jit(solution)/shard_map/all_to_all | solution.py:29
  6.6 27.4 %collective-permute-start.7 = (bf16[104,6656]{1,0:T(8,128)(2,1)}, bf16[104,6656]{1,0:T(8,128)(2,1)}, u32[]{:S(2)}, u32[]{:S(2)}) collective-permute-start(bf16[104,6656]{1,0:T(8,128)(2,1)} %bitcast.88), channel_id=1, source_target_pairs={{0,2},{2,0},{1,3},{3,1},{4,6},{6,4},{5,7},{7,5},{8,10},{10,8},{9,1... | collective-permute-start | bytes 4153352 | tf_op jit(solution)/shard_map/ppermute | solution.py:25
  7.3 2.4 %collective-permute-start.10 = (f32[104]{0:T(128)S(1)}, f32[104]{0:T(128)S(1)}, u32[]{:S(2)}, u32[]{:S(2)}) collective-permute-start(f32[104]{0:T(128)S(1)} %bitcast_convert_fusion), channel_id=1, source_target_pairs={{0,2},{2,0},{1,3},{3,1},{4,6},{6,4},{5,7},{7,5},{8,10},{10,8},{9,1... | collective-permute-start | bytes 1256 | tf_op jit(solution)/shard_map/ppermute | solution.py:25
  7.8 49.2 %collective-permute-start = (bf16[3328,640]{1,0:T(8,128)(2,1)}, bf16[3328,640]{1,0:T(8,128)(2,1)}, u32[]{:S(2)}, u32[]{:S(2)}) collective-permute-start(bf16[3328,640]{1,0:T(8,128)(2,1)} %bitcast.72), channel_id=1, source_target_pairs={{0,2},{2,0},{1,3},{3,1},{4,6},{6,4},{5,7},{7,5},{8,10},{10,8},{9,1... | collective-permute-start | bytes 12779528 | tf_op jit(solution)/shard_map/ppermute | solution.py:25
  13.5 10.0 %collective-permute-start.1 = (bf16[16,6656]{1,0:T(8,128)(2,1)}, bf16[16,6656]{1,0:T(8,128)(2,1)}, u32[]{:S(2)}, u32[]{:S(2)}) collective-permute-start(bf16[16,6656]{1,0:T(8,128)(2,1)} %reshape.127), channel_id=1, source_target_pairs={{0,4},{4,8},{8,12},{12,16},{16,20},{20,24},{24,28},{28,0},{1,5},{5... | collective-permute-start | bytes 638984 | tf_op jit(solution)/shard_map/ppermute | solution.py:241
  15.4 8.1 %collective-permute-start.4 = (bf16[16,6656]{1,0:T(8,128)(2,1)}, bf16[16,6656]{1,0:T(8,128)(2,1)S(1)}, u32[]{:S(2)}, u32[]{:S(2)}) collective-permute-start(bf16[16,6656]{1,0:T(8,128)(2,1)} %reshape.127), channel_id=1, source_target_pairs={{0,28},{4,0},{8,4},{12,8},{16,12},{20,16},{24,20},{28,24},{1,29},{... | collective-permute-start | bytes 638984 | tf_op jit(solution)/shard_map/ppermute | solution.py:241
  19.4 14.7 %copy-start.8 = (bf16[1,6656,104]{1,2,0:T(8,128)(2,1)S(1)}, bf16[1,6656,104]{1,2,0:T(8,128)(2,1)}, u32[]{:S(2)}) copy-start(bf16[1,6656,104]{1,2,0:T(8,128)(2,1)} %param.7) | copy-start | bytes 4153348
  23.5 7.3 %collective-permute-start.2 = (bf16[16,6656]{1,0:T(8,128)(2,1)}, bf16[16,6656]{1,0:T(8,128)(2,1)S(1)}, u32[]{:S(2)}, u32[]{:S(2)}) collective-permute-start(bf16[16,6656]{1,0:T(8,128)(2,1)} %collective-permute-done.1), channel_id=1, source_target_pairs={{0,4},{4,8},{8,12},{12,16},{16,20},{20,24},{24,28},{28,0},{1,5},{5... | collective-permute-start | bytes 638984 | tf_op jit(solution)/shard_map/ppermute | solution.py:241
  23.5 7.3 %collective-permute-start.5 = (bf16[16,6656]{1,0:T(8,128)(2,1)S(1)}, bf16[16,6656]{1,0:T(8,128)(2,1)S(1)}, u32[]{:S(2)}, u32[]{:S(2)}) collective-permute-start(bf16[16,6656]{1,0:T(8,128)(2,1)S(1)} %collective-permute-done.4), channel_id=1, source_target_pairs={{0,28},{4,0},{8,4},{12,8},{16,12},{20,16},{24,20},{28,24},{1,29},{... | collective-permute-start | bytes 638984 | tf_op jit(solution)/shard_map/ppermute | solution.py:241
  30.8 7.9 %collective-permute-start.3 = (bf16[16,6656]{1,0:T(8,128)(2,1)S(1)}, bf16[16,6656]{1,0:T(8,128)(2,1)S(1)}, u32[]{:S(2)}, u32[]{:S(2)}) collective-permute-start(bf16[16,6656]{1,0:T(8,128)(2,1)S(1)} %collective-permute-done.2), channel_id=1, source_target_pairs={{0,4},{4,8},{8,12},{12,16},{16,20},{20,24},{24,28},{28,0},{1,5},{5... | collective-permute-start | bytes 638984 | tf_op jit(solution)/shard_map/ppermute | solution.py:241
  30.8 7.9 %collective-permute-start.6 = (bf16[16,6656]{1,0:T(8,128)(2,1)S(1)}, bf16[16,6656]{1,0:T(8,128)(2,1)S(1)}, u32[]{:S(2)}, u32[]{:S(2)}) collective-permute-start(bf16[16,6656]{1,0:T(8,128)(2,1)S(1)} %collective-permute-done.5), channel_id=1, source_target_pairs={{0,28},{4,0},{8,4},{12,8},{16,12},{20,16},{24,20},{28,24},{1,29},{... | collective-permute-start | bytes 638984 | tf_op jit(solution)/shard_map/ppermute | solution.py:241
  36.8 9.7 %copy-start.3 = (bf16[416,6656]{1,0:T(8,128)(2,1)}, bf16[416,6656]{1,0:T(8,128)(2,1)S(1)}, u32[]{:S(2)}) copy-start(bf16[416,6656]{1,0:T(8,128)(2,1)S(1)} %pad_maximum_fusion) | copy-start | bytes 16613380
  38.6 6.2 %collective-permute-start.8 = (bf16[8,6656]{1,0:T(8,128)(2,1)S(1)}, bf16[8,6656]{1,0:T(8,128)(2,1)S(1)}, u32[]{:S(2)}, u32[]{:S(2)}) collective-permute-start(bf16[8,6656]{1,0:T(8,128)(2,1)S(1)} %slice.33), channel_id=1, source_target_pairs={{0,4},{4,8},{8,12},{12,16},{16,20},{20,24},{24,28},{28,0},{1,5},{5... | collective-permute-start | bytes 319496 | tf_op jit(solution)/shard_map/ppermute | solution.py:241
  38.7 6.1 %collective-permute-start.9 = (bf16[8,6656]{1,0:T(8,128)(2,1)S(1)}, bf16[8,6656]{1,0:T(8,128)(2,1)S(1)}, u32[]{:S(2)}, u32[]{:S(2)}) collective-permute-start(bf16[8,6656]{1,0:T(8,128)(2,1)S(1)} %slice.34), channel_id=1, source_target_pairs={{0,28},{4,0},{8,4},{12,8},{16,12},{20,16},{24,20},{28,24},{1,29},{... | collective-permute-start | bytes 319496 | tf_op jit(solution)/shard_map/ppermute | solution.py:241
  47.7 23.6 %all-to-all-start.1 = ((bf16[16,208,128]{2,1,0:T(8,128)(2,1)}), bf16[16,208,128]{2,1,0:T(8,128)(2,1)S(1)}, u32[]{:S(2)}, u32[]{:S(2)}) async-start(bf16[16,208,128]{2,1,0:T(8,128)(2,1)} %broadcast_in_dim.62), calls=%async_computation.1 | async-start | bytes 1703936 | tf_op jit(solution)/shard_map/all_to_all | solution.py:29
  78.1 9.1 %collective-permute-start.11 = (s16[128,1408]{1,0:T(8,128)(2,1)}, s16[128,1408]{1,0:T(8,128)(2,1)S(1)}, u32[]{:S(2)}, u32[]{:S(2)}) collective-permute-start(s16[128,1408]{1,0:T(8,128)(2,1)} %get-tuple-element.24), channel_id=1, source_target_pairs={{0,1},{1,0},{2,3},{3,2},{4,5},{5,4},{6,7},{7,6},{8,9},{9,8},{10,11... | collective-permute-start | bytes 1081352 | tf_op jit(solution)/shard_map/ppermute | solution.py:25
  90.3 13.0 %all-to-all-start.2 = ((f32[16,3,128]{2,1,0:T(4,128)}), f32[16,3,128]{2,1,0:T(4,128)S(1)}, u32[]{:S(2)}, u32[]{:S(2)}) async-start(f32[16,3,128]{2,1,0:T(4,128)} %get-tuple-element.25.own_ref), calls=%async_computation.2 | async-start | bytes 65536 | tf_op jit(solution)/shard_map/all_to_all | solution.py:29
  105.8 22.5 %all-to-all-start.3 = ((bf16[16,208,128]{2,1,0:T(8,128)(2,1)}), bf16[16,208,128]{2,1,0:T(8,128)(2,1)S(1)}, u32[]{:S(2)}, u32[]{:S(2)}) async-start(bf16[16,208,128]{2,1,0:T(8,128)(2,1)} %bitcast.24), calls=%async_computation.3 | async-start | bytes 1703936 | tf_op jit(solution)/shard_map/all_to_all | solution.py:29
  111.3 24.1 %collective-permute-start.22 = (bf16[3328,128]{1,0:T(8,128)(2,1)S(1)}, bf16[3328,128]{1,0:T(8,128)(2,1)}, u32[]{:S(2)}, u32[]{:S(2)}) collective-permute-start(bf16[3328,128]{1,0:T(8,128)(2,1)S(1)} %bitcast.83), channel_id=1, source_target_pairs={{0,2},{2,0},{1,3},{3,1},{4,6},{6,4},{5,7},{7,5},{8,10},{10,8},{9,1... | collective-permute-start | bytes 2555912 | tf_op jit(solution)/shard_map/ppermute | solution.py:25
  112.3 23.1 %collective-permute-start.23 = (bf16[128,640]{1,0:T(8,128)(2,1)}, bf16[128,640]{1,0:T(8,128)(2,1)}, u32[]{:S(2)}, u32[]{:S(2)}) collective-permute-start(bf16[128,640]{1,0:T(8,128)(2,1)} %get-tuple-element.46), channel_id=1, source_target_pairs={{0,2},{2,0},{1,3},{3,1},{4,6},{6,4},{5,7},{7,5},{8,10},{10,8},{9,1... | collective-permute-start | bytes 491528 | tf_op jit(solution)/shard_map/ppermute | solution.py:25
  132.1 9.5 %collective-permute-start.12 = (bf16[128,1664]{1,0:T(8,128)(2,1)}, bf16[128,1664]{1,0:T(8,128)(2,1)S(1)}, u32[]{:S(2)}, u32[]{:S(2)}) collective-permute-start(bf16[128,1664]{1,0:T(8,128)(2,1)} %get-tuple-element.44), channel_id=1, source_target_pairs={{0,192},{64,0},{128,64},{192,128},{1,193},{65,1},{129,65},{193,129... | collective-permute-start | bytes 1277960 | tf_op jit(solution)/shard_map/ppermute | solution.py:233
  133.0 8.7 %collective-permute-start.13 = (bf16[128,1664]{1,0:T(8,128)(2,1)}, bf16[128,1664]{1,0:T(8,128)(2,1)S(1)}, u32[]{:S(2)}, u32[]{:S(2)}) collective-permute-start(bf16[128,1664]{1,0:T(8,128)(2,1)} %get-tuple-element.43), channel_id=1, source_target_pairs={{0,64},{64,128},{128,192},{192,0},{1,65},{65,129},{129,193},{193,1... | collective-permute-start | bytes 1277960 | tf_op jit(solution)/shard_map/ppermute | solution.py:233
  135.4 25.3 %collective-permute-start.18 = (bf16[128,6656]{1,0:T(8,128)(2,1)}, bf16[128,6656]{1,0:T(8,128)(2,1)}, u32[]{:S(2)}, u32[]{:S(2)}) collective-permute-start(bf16[128,6656]{1,0:T(8,128)(2,1)} %bitcast.86), channel_id=1, source_target_pairs={{0,2},{2,0},{1,3},{3,1},{4,6},{6,4},{5,7},{7,5},{8,10},{10,8},{9,1... | collective-permute-start | bytes 5111816 | tf_op jit(solution)/shard_map/ppermute | solution.py:25
  141.9 18.7 %copy-start.7 = (bf16[8,16,6656]{2,1,0:T(8,128)(2,1)S(1)}, bf16[8,16,6656]{2,1,0:T(8,128)(2,1)}, u32[]{:S(2)}) copy-start(bf16[8,16,6656]{2,1,0:T(8,128)(2,1)} %copy-done.6) | copy-start | bytes 5111812
  142.0 8.2 %collective-permute-start.14 = (bf16[32,3328]{1,0:T(8,128)(2,1)S(1)}, bf16[32,3328]{1,0:T(8,128)(2,1)S(1)}, u32[]{:S(2)}, u32[]{:S(2)}) collective-permute-start(bf16[32,3328]{1,0:T(8,128)(2,1)S(1)} %get-tuple-element.40), channel_id=1, source_target_pairs={{0,32},{32,0},{1,33},{33,1},{2,34},{34,2},{3,35},{35,3},{4,36},{36... | collective-permute-start | bytes 638984 | tf_op jit(solution)/shard_map/ppermute | solution.py:348
  142.4 12.8 %collective-permute-start.15 = (bf16[32,3328]{1,0:T(8,128)(2,1)S(1)}, bf16[32,3328]{1,0:T(8,128)(2,1)S(1)}, u32[]{:S(2)}, u32[]{:S(2)}) collective-permute-start(bf16[32,3328]{1,0:T(8,128)(2,1)S(1)} %get-tuple-element.41), channel_id=1, source_target_pairs={{0,33},{32,1},{1,32},{33,0},{2,35},{34,3},{3,34},{35,2},{4,37},{36... | collective-permute-start | bytes 638984 | tf_op jit(solution)/shard_map/ppermute | solution.py:348
  145.8 9.4 %collective-permute-start.16 = (bf16[32,3328]{1,0:T(8,128)(2,1)S(1)}, bf16[32,3328]{1,0:T(8,128)(2,1)S(1)}, u32[]{:S(2)}, u32[]{:S(2)}) collective-permute-start(bf16[32,3328]{1,0:T(8,128)(2,1)S(1)} %get-tuple-element.42), channel_id=1, source_target_pairs={{0,1},{32,33},{1,0},{33,32},{2,3},{34,35},{3,2},{35,34},{4,5},{36,... | collective-permute-start | bytes 638984 | tf_op jit(solution)/shard_map/ppermute | solution.py:348
  146.2 14.3 %collective-permute-start.17 = (f32[104,128]{1,0:T(8,128)S(1)}, f32[104,128]{1,0:T(8,128)S(1)}, u32[]{:S(2)}, u32[]{:S(2)}) collective-permute-start(f32[104,128]{1,0:T(8,128)S(1)} %get-tuple-element.50), channel_id=1, source_target_pairs={{0,2},{2,0},{1,3},{3,1},{4,6},{6,4},{5,7},{7,5},{8,10},{10,8},{9,1... | collective-permute-start | bytes 159752 | tf_op jit(solution)/shard_map/ppermute | solution.py:25
  156.2 14.3 %all-to-all-start.4 = ((bf16[8,4,3328]{2,1,0:T(4,128)(2,1)}), bf16[8,4,3328]{2,1,0:T(4,128)(2,1)S(1)}, u32[]{:S(2)}, u32[]{:S(2)}) async-start(bf16[8,4,3328]{2,1,0:T(4,128)(2,1)} %reshape.132), calls=%async_computation.4 | async-start | bytes 425984 | tf_op jit(solution)/shard_map/all_to_all | solution.py:29
  170.6 5.4 %collective-permute-start.19 = (bf16[4,3328]{1,0:T(4,128)(2,1)S(1)}, bf16[4,3328]{1,0:T(4,128)(2,1)S(1)}, u32[]{:S(2)}, u32[]{:S(2)}) collective-permute-start(bf16[4,3328]{1,0:T(4,128)(2,1)S(1)} %convert_element_type.132), channel_id=1, source_target_pairs={{0,128},{64,192},{128,0},{192,64},{1,129},{65,193},{129,1},{193,65... | collective-permute-start | bytes 79880 | tf_op jit(solution)/shard_map/ppermute | solution.py:233
  170.9 5.1 %collective-permute-start.20 = (bf16[4,3328]{1,0:T(4,128)(2,1)S(1)}, bf16[4,3328]{1,0:T(4,128)(2,1)S(1)}, u32[]{:S(2)}, u32[]{:S(2)}) collective-permute-start(bf16[4,3328]{1,0:T(4,128)(2,1)S(1)} %convert_element_type.132), channel_id=1, source_target_pairs={{0,64},{64,128},{128,192},{192,0},{1,65},{65,129},{129,193},{193,1... | collective-permute-start | bytes 79880 | tf_op jit(solution)/shard_map/ppermute | solution.py:233
  173.0 5.1 %collective-permute-start.21 = (bf16[4,3328]{1,0:T(4,128)(2,1)S(1)}, bf16[4,3328]{1,0:T(4,128)(2,1)S(1)}, u32[]{:S(2)}, u32[]{:S(2)}) collective-permute-start(bf16[4,3328]{1,0:T(4,128)(2,1)S(1)} %convert_element_type.132), channel_id=1, source_target_pairs={{0,192},{64,0},{128,64},{192,128},{1,193},{65,1},{129,65},{193,129... | collective-permute-start | bytes 79880 | tf_op jit(solution)/shard_map/ppermute | solution.py:233
  (13 other events, 66.4 us)

commit v7 on v6

--- a/solution.py
+++ b/solution.py
@@ -113,11 +113,10 @@
     toks, columns = logits.shape
     width = columns // 2
 
-    def kernel(logits_ref, coded_ref, spots_ref, total_ref, rest_a_ref, rest_b_ref, stats_ref):
+    def kernel(logits_ref, coded_ref, spots_ref, rest_a_ref, rest_b_ref, stats_ref):
         power = coded_ref[:, columns : columns + 1].astype(jnp.int32).astype(f32)
         code = coded_ref[:, :columns].astype(jnp.int32).astype(f32)
         total = logits_ref[...] + code * (jnp.exp(power * ln2) * (1.0 / int16_top))
-        total_ref[...] = total
         top = jnp.max(total, axis=1, keepdims=True)
         rests, targets = 0.0, 0.0
         for side, out_ref in ((0, rest_a_ref), (1, rest_b_ref)):
@@ -135,7 +134,6 @@
     return pl.pallas_call(
         kernel,
         out_shape=[
-            jax.ShapeDtypeStruct((toks, columns), f32),
             jax.ShapeDtypeStruct((toks, width), bf16),
             jax.ShapeDtypeStruct((toks, width), bf16),
             jax.ShapeDtypeStruct((copies, 3, toks), f32),
@@ -295,8 +293,12 @@
     logits, coded = vocab_logits(hidden_half, lm_own, lm_other)
     coded = swap(coded, "yhi")
     spots = jnp.stack([tok_ids - (chip * 2 + owner) * vocab_width for owner in (core, 1 - core)], 1)
-    logits, rest_own, rest_other, own_stats = local_softmax(logits, coded, spots, n_plane)
+    rest_own, rest_other, own_stats = local_softmax(logits, coded, spots, n_plane)
     top = own_stats[0, 0]
+    coded = coded.astype(f32)
+    logits = logits + coded[:, : 2 * vocab_width] * (
+        jnp.exp(coded[:, 2 * vocab_width : 2 * vocab_width + 1] * ln2) * (1.0 / int16_top)
+    )
     exp_own = jnp.exp(logits[:, :vocab_width] - top[:, None])
     exp_other = jnp.exp(logits[:, vocab_width:] - top[:, None])
     stats = exchange(own_stats, plane)

time: 180 us -> 180 us (level)
  no operation moved by 1% of the time
where the time goes in v7:
time: 180 us; the launch traced here: 179 us
  waiting for transfers between devices  67.7 us (38%)
  starting transfers between devices  55 us (31%)
  Pallas kernels  20.8 us (12%)
  matrix products  12.9 us (7%)
  local copies, waits for them, and re-layouts  11.6 us (6%)
  other arithmetic  9.43 us (5%)
    all_to_all x5, waiting for transfers between devices, exchange(): return lax.all_to_all(value, axes, 0, 0, tiled=True)  36.1 us
    all_to_all x5, starting transfers between devices, exchange(): return lax.all_to_all(value, axes, 0, 0, tiled=True)  25.5 us
    ppermute x8, starting transfers between devices, z_shift(): return lax.ppermute(value, 'z', [(i, (i + step) % n_z) for i in range(n_z)])  15.9 us
    dot_general x6, matrix products, dot(): lax.dot_general(a, b, ((contract[0], contract[1]), ((), ())), preferred_e...  12.9 us
    pallas_call x2, Pallas kernels, vocab_product(): pl.pallas_call(kernel, grid=(half // step,), in_specs=[weights, weights,...  11.4 us
    ppermute x8, waiting for transfers between devices, z_shift(): return lax.ppermute(value, 'z', [(i, (i + step) % n_z) for i in range(n_z)])  11.3 us
    ppermute x3, waiting for transfers between devices, on_device(): got = lax.ppermute(sent, line, pairs)  8.9 us
    ppermute x8, waiting for transfers between devices, swap(): return lax.ppermute(value, axis, [(0, 1), (1, 0)])  6.1 us
  transfers between devices with their start and end apart: 29, of which 16 were waited for; matrix products, arithmetic and copies ran while one was open for 16% of the time, Pallas kernels for 6%

profile of v7, /device:TPU:6, one launch (start us, length us, event | category | flops | bytes accessed | tf_op | source)
XLA Modules:
  0.0 178.9 jit_solution(15928513145925490590)
XLA Ops:
  2.2 4.5 %all-to-all-start = ((bf16[4,4,6656]{2,1,0:T(4,128)(2,1)}), bf16[4,4,6656]{2,1,0:T(4,128)(2,1)S(1)}, u32[]{:S(2)}, u32[]{:S(2)}) async-start(bf16[4,4,6656]{2,1,0:T(4,128)(2,1)} %broadcast_in_dim.52), calls=%async_computation | async-start | bytes 425984 | tf_op jit(solution)/shard_map/all_to_all | solution.py:29
  9.8 2.9 %all-to-all-done = bf16[4,4,6656]{2,1,0:T(4,128)(2,1)S(1)} async-done(((bf16[4,4,6656]{2,1,0:T(4,128)(2,1)}), bf16[4,4,6656]{2,1,0:T(4,128)(2,1)S(1)}, u32[]{:S(2)}, u32[]{:S(2)}) %all-to-all-start) | async-done | bytes 213024 | tf_op jit(solution)/shard_map/all_to_all | solution.py:29
  15.4 3.9 %collective-permute-start.4 = (bf16[16,6656]{1,0:T(8,128)(2,1)}, bf16[16,6656]{1,0:T(8,128)(2,1)S(1)}, u32[]{:S(2)}, u32[]{:S(2)}) collective-permute-start(bf16[16,6656]{1,0:T(8,128)(2,1)} %reshape.127), channel_id=1, source_target_pairs={{0,28},{4,0},{8,4},{12,8},{16,12},{20,16},{24,20},{28,24},{1,29},{... | collective-permute-start | bytes 638984 | tf_op jit(solution)/shard_map/ppermute | solution.py:239
  19.6 3.9 %collective-permute-done.1 = bf16[16,6656]{1,0:T(8,128)(2,1)} collective-permute-done((bf16[16,6656]{1,0:T(8,128)(2,1)}, bf16[16,6656]{1,0:T(8,128)(2,1)}, u32[]{:S(2)}, u32[]{:S(2)}) %collective-permute-start.1) | collective-permute-done | bytes 213024 | tf_op jit(solution)/shard_map/ppermute | solution.py:239
  23.5 3.2 %collective-permute-start.5 = (bf16[16,6656]{1,0:T(8,128)(2,1)S(1)}, bf16[16,6656]{1,0:T(8,128)(2,1)S(1)}, u32[]{:S(2)}, u32[]{:S(2)}) collective-permute-start(bf16[16,6656]{1,0:T(8,128)(2,1)S(1)} %collective-permute-done.4), channel_id=1, source_target_pairs={{0,28},{4,0},{8,4},{12,8},{16,12},{20,16},{24,20},{28,24},{1,29},{... | collective-permute-start | bytes 638984 | tf_op jit(solution)/shard_map/ppermute | solution.py:239
  27.7 3.0 %collective-permute-done.2 = bf16[16,6656]{1,0:T(8,128)(2,1)S(1)} collective-permute-done((bf16[16,6656]{1,0:T(8,128)(2,1)}, bf16[16,6656]{1,0:T(8,128)(2,1)S(1)}, u32[]{:S(2)}, u32[]{:S(2)}) %collective-permute-start.2) | collective-permute-done | bytes 213024 | tf_op jit(solution)/shard_map/ppermute | solution.py:239
  30.8 3.2 %collective-permute-start.6 = (bf16[16,6656]{1,0:T(8,128)(2,1)S(1)}, bf16[16,6656]{1,0:T(8,128)(2,1)S(1)}, u32[]{:S(2)}, u32[]{:S(2)}) collective-permute-start(bf16[16,6656]{1,0:T(8,128)(2,1)S(1)} %collective-permute-done.5), channel_id=1, source_target_pairs={{0,28},{4,0},{8,4},{12,8},{16,12},{20,16},{24,20},{28,24},{1,29},{... | collective-permute-start | bytes 638984 | tf_op jit(solution)/shard_map/ppermute | solution.py:239
  38.7 3.5 %collective-permute-start.9 = (bf16[8,6656]{1,0:T(8,128)(2,1)S(1)}, bf16[8,6656]{1,0:T(8,128)(2,1)S(1)}, u32[]{:S(2)}, u32[]{:S(2)}) collective-permute-start(bf16[8,6656]{1,0:T(8,128)(2,1)S(1)} %slice.40), channel_id=1, source_target_pairs={{0,28},{4,0},{8,4},{12,8},{16,12},{20,16},{24,20},{28,24},{1,29},{... | collective-permute-start | bytes 319496 | tf_op jit(solution)/shard_map/ppermute | solution.py:239
  42.3 2.5 %collective-permute-done.8 = bf16[8,6656]{1,0:T(8,128)(2,1)S(1)} collective-permute-done((bf16[8,6656]{1,0:T(8,128)(2,1)S(1)}, bf16[8,6656]{1,0:T(8,128)(2,1)S(1)}, u32[]{:S(2)}, u32[]{:S(2)}) %collective-permute-start.8) | collective-permute-done | bytes 106528 | tf_op jit(solution)/shard_map/ppermute | solution.py:239
  47.7 6.7 %all-to-all-start.1 = ((bf16[16,208,128]{2,1,0:T(8,128)(2,1)}), bf16[16,208,128]{2,1,0:T(8,128)(2,1)S(1)}, u32[]{:S(2)}, u32[]{:S(2)}) async-start(bf16[16,208,128]{2,1,0:T(8,128)(2,1)} %broadcast_in_dim.62), calls=%async_computation.1 | async-start | bytes 1703936 | tf_op jit(solution)/shard_map/all_to_all | solution.py:29
  57.0 5.7 %shard_map.93.target_ref = bf16[3328,128]{1,0:T(8,128)(2,1)} custom-call(bf16[3328,640]{1,0:T(8,128)(2,1)} %bitcast.73, bf16[3328,640]{1,0:T(8,128)(2,1)} %collective-permute-done.b_ref, bf16[128,640]{1,0:T(8,128)(2,1)} %fusion.26.ra_ref, bf16[128,640]{1,0:T(8,128)(2,1)} %fusion.25.rb_ref), custom_call_target="tpu_custom_call" | custom-call | flops 1090519040 | bytes 10223616 | tf_op jit(solution)/shard_map/pallas_call | solution.py:48
  62.7 8.7 %all-to-all-done.1 = bf16[16,208,128]{2,1,0:T(8,128)(2,1)S(1)} async-done(((bf16[16,208,128]{2,1,0:T(8,128)(2,1)}), bf16[16,208,128]{2,1,0:T(8,128)(2,1)S(1)}, u32[]{:S(2)}, u32[]{:S(2)}) %all-to-all-start.1) | async-done | bytes 852000 | tf_op jit(solution)/shard_map/all_to_all | solution.py:29
  72.2 5.9 %shard_map.94 = (f32[128,1280]{1,0:T(8,128)}, s16[128,1408]{1,0:T(8,128)(2,1)}) custom-call(bf16[3328,128]{1,0:T(8,128)(2,1)} %bitcast.82, bf16[3328,640]{1,0:T(8,128)(2,1)} %bitcast.74, bf16[3328,640]{1,0:T(8,128)(2,1)} %collective-permute-done.b_ref), custom_call_target="tpu_custom_call" | custom-call | flops 1090519040 | bytes 9371648 | tf_op jit(solution)/shard_map/pallas_call | solution.py:91
  78.1 2.6 %collective-permute-start.11 = (s16[128,1408]{1,0:T(8,128)(2,1)}, s16[128,1408]{1,0:T(8,128)(2,1)S(1)}, u32[]{:S(2)}, u32[]{:S(2)}) collective-permute-start(s16[128,1408]{1,0:T(8,128)(2,1)} %get-tuple-element.23), channel_id=1, source_target_pairs={{0,1},{1,0},{2,3},{3,2},{4,5},{5,4},{6,7},{7,6},{8,9},{9,8},{10,11... | collective-permute-start | bytes 1081352 | tf_op jit(solution)/shard_map/ppermute | solution.py:25
  82.0 5.2 %collective-permute-done.11.coded_ref = s16[128,1408]{1,0:T(8,128)(2,1)S(1)} collective-permute-done((s16[128,1408]{1,0:T(8,128)(2,1)}, s16[128,1408]{1,0:T(8,128)(2,1)S(1)}, u32[]{:S(2)}, u32[]{:S(2)}) %collective-permute-start.11) | collective-permute-done | bytes 360480 | tf_op jit(solution)/shard_map/ppermute | solution.py:25
  88.0 2.3 %shard_map.95 = (bf16[128,640]{1,0:T(8,128)(2,1)}, bf16[128,640]{1,0:T(8,128)(2,1)}, f32[16,3,128]{2,1,0:T(4,128)}) custom-call(f32[128,1280]{1,0:T(8,128)} %get-tuple-element.22.logits_ref, s16[128,1408]{1,0:T(8,128)(2,1)} %copy-done.9, s32[128,2]{1,0:T(8,128)} %copy.44.spots_ref), custom_call_target="tpu_custom_call" | custom-call | flops 1966080 | bytes 1966080 | tf_op jit(solution)/shard_map/pallas_call | solution.py:134
  90.3 4.5 %all-to-all-start.2 = ((f32[16,3,128]{2,1,0:T(4,128)}), f32[16,3,128]{2,1,0:T(4,128)S(1)}, u32[]{:S(2)}, u32[]{:S(2)}) async-start(f32[16,3,128]{2,1,0:T(4,128)} %get-tuple-element.24.own_ref), calls=%async_computation.2 | async-start | bytes 65536 | tf_op jit(solution)/shard_map/all_to_all | solution.py:29
  94.8 5.7 %shard_map.96.product_ref = bf16[3328,128]{1,0:T(8,128)(2,1)} custom-call(bf16[3328,640]{1,0:T(8,128)(2,1)} %bitcast.75, bf16[3328,640]{1,0:T(8,128)(2,1)} %collective-permute-done.b_ref, bf16[128,640]{1,0:T(8,128)(2,1)} %get-tuple-element.25.ra_ref, bf16[128,640]{1,0:T(8,128)(2,1)} %get-tuple-element.26.rb_ref), custom_call_target="tpu_custom_call" | custom-call | flops 1090519040 | bytes 10223616 | tf_op jit(solution)/shard_map/pallas_call | solution.py:48
  100.6 2.8 %all-to-all-done.2.stats_ref = f32[16,3,128]{2,1,0:T(4,128)S(1)} async-done(((f32[16,3,128]{2,1,0:T(4,128)}), f32[16,3,128]{2,1,0:T(4,128)S(1)}, u32[]{:S(2)}, u32[]{:S(2)}) %all-to-all-start.2) | async-done | bytes 24608 | tf_op jit(solution)/shard_map/all_to_all | solution.py:29
  105.7 5.5 %all-to-all-start.3 = ((bf16[16,208,128]{2,1,0:T(8,128)(2,1)}), bf16[16,208,128]{2,1,0:T(8,128)(2,1)S(1)}, u32[]{:S(2)}, u32[]{:S(2)}) async-start(bf16[16,208,128]{2,1,0:T(8,128)(2,1)} %bitcast.24), calls=%async_computation.3 | async-start | bytes 1703936 | tf_op jit(solution)/shard_map/all_to_all | solution.py:29
  113.3 15.1 %all-to-all-done.3 = bf16[16,208,128]{2,1,0:T(8,128)(2,1)S(1)} async-done(((bf16[16,208,128]{2,1,0:T(8,128)(2,1)}), bf16[16,208,128]{2,1,0:T(8,128)(2,1)S(1)}, u32[]{:S(2)}, u32[]{:S(2)}) %all-to-all-start.3) | async-done | bytes 852000 | tf_op jit(solution)/shard_map/all_to_all | solution.py:29
  128.8 2.4 %convolution_convert_fusion.2 = bf16[128,3328]{1,0:T(8,128)(2,1)S(1)} fusion(bf16[416,128]{1,0:T(8,128)(2,1)S(1)} %convolution_convert_fusion.3, bf16[416,6656]{1,0:T(8,128)(2,1)} %copy-done.3, s32[]{:T(128)S(6)} %select_n.196), kind=kOutput, calls=%fused_computation.5 | convolution fusion | flops 354844672 | bytes 3727364 | tf_op jit(solution)/shard_map/dot_general | solution.py:33
  133.1 2.4 %collective-permute-start.13 = (bf16[128,1664]{1,0:T(8,128)(2,1)}, bf16[128,1664]{1,0:T(8,128)(2,1)S(1)}, u32[]{:S(2)}, u32[]{:S(2)}) collective-permute-start(bf16[128,1664]{1,0:T(8,128)(2,1)} %get-tuple-element.41), channel_id=1, source_target_pairs={{0,64},{64,128},{128,192},{192,0},{1,65},{65,129},{129,193},{193,1... | collective-permute-start | bytes 1277960 | tf_op jit(solution)/shard_map/ppermute | solution.py:231
  135.5 4.9 %fusion = bf16[1,3328,640]{2,1,0:T(8,128)(2,1)} fusion(bf16[3328,128]{1,0:T(8,128)(2,1)} %collective-permute-done.22, bf16[3328,128]{1,0:T(8,128)(2,1)S(1)} %bitcast.84, bf16[128,640]{1,0:T(8,128)(2,1)} %collective-permute-done.23, bf16[128,640]{1,0:T(8,128)(2,1)S(1)} %get-tuple-element.43), kind=kOutput, calls=%fused_computation.2 | convolution fusion | flops 1096712192 | bytes 6291456 | tf_op jit(solution)/shard_map/dot_general | solution.py:33
  142.6 3.4 %collective-permute-start.15 = (bf16[32,3328]{1,0:T(8,128)(2,1)S(1)}, bf16[32,3328]{1,0:T(8,128)(2,1)S(1)}, u32[]{:S(2)}, u32[]{:S(2)}) collective-permute-start(bf16[32,3328]{1,0:T(8,128)(2,1)S(1)} %get-tuple-element.39), channel_id=1, source_target_pairs={{0,33},{32,1},{1,32},{33,0},{2,35},{34,3},{3,34},{35,2},{4,37},{36... | collective-permute-start | bytes 638984 | tf_op jit(solution)/shard_map/ppermute | solution.py:350
  146.5 3.8 %collective-permute-done.14 = bf16[32,3328]{1,0:T(8,128)(2,1)S(1)} collective-permute-done((bf16[32,3328]{1,0:T(8,128)(2,1)S(1)}, bf16[32,3328]{1,0:T(8,128)(2,1)S(1)}, u32[]{:S(2)}, u32[]{:S(2)}) %collective-permute-start.14) | collective-permute-done | bytes 213024 | tf_op jit(solution)/shard_map/ppermute | solution.py:350
  150.3 5.1 %collective-permute-done.15 = bf16[32,3328]{1,0:T(8,128)(2,1)S(1)} collective-permute-done((bf16[32,3328]{1,0:T(8,128)(2,1)S(1)}, bf16[32,3328]{1,0:T(8,128)(2,1)S(1)}, u32[]{:S(2)}, u32[]{:S(2)}) %collective-permute-start.15) | collective-permute-done | bytes 213024 | tf_op jit(solution)/shard_map/ppermute | solution.py:350
  156.3 4.3 %all-to-all-start.4 = ((bf16[8,4,3328]{2,1,0:T(4,128)(2,1)}), bf16[8,4,3328]{2,1,0:T(4,128)(2,1)S(1)}, u32[]{:S(2)}, u32[]{:S(2)}) async-start(bf16[8,4,3328]{2,1,0:T(4,128)(2,1)} %reshape.132), calls=%async_computation.4 | async-start | bytes 425984 | tf_op jit(solution)/shard_map/all_to_all | solution.py:29
  160.8 3.2 %convolution_convert_fusion = bf16[104,6656]{1,0:T(8,128)(2,1)} fusion(bf16[128,6656]{1,0:T(8,128)(2,1)} %collective-permute-done.18, bf16[128,6656]{1,0:T(8,128)(2,1)S(1)} %bitcast.87, bf16[104,128]{1,0:T(8,128)(2,1)S(1)} %get-tuple-element.51, bf16[104,128]{1,0:T(8,128)(2,1)S(1)} %dynamic-slice_convert_fusion), kind=kOutput, calls=%fused_computation | convolution fusion | flops 362033152 | bytes 4845568 | tf_op jit(solution)/shard_map/dot_general | solution.py:33
  164.0 6.6 %all-to-all-done.4 = bf16[8,4,3328]{2,1,0:T(4,128)(2,1)S(1)} async-done(((bf16[8,4,3328]{2,1,0:T(4,128)(2,1)}), bf16[8,4,3328]{2,1,0:T(4,128)(2,1)S(1)}, u32[]{:S(2)}, u32[]{:S(2)}) %all-to-all-start.4) | async-done | bytes 213024 | tf_op jit(solution)/shard_map/all_to_all | solution.py:29
  171.0 2.1 %collective-permute-start.20 = (bf16[4,3328]{1,0:T(4,128)(2,1)S(1)}, bf16[4,3328]{1,0:T(4,128)(2,1)S(1)}, u32[]{:S(2)}, u32[]{:S(2)}) collective-permute-start(bf16[4,3328]{1,0:T(4,128)(2,1)S(1)} %convert_element_type.135), channel_id=1, source_target_pairs={{0,64},{64,128},{128,192},{192,0},{1,65},{65,129},{129,193},{193,1... | collective-permute-start | bytes 79880 | tf_op jit(solution)/shard_map/ppermute | solution.py:231
  173.6 2.5 %collective-permute-done.19 = bf16[4,3328]{1,0:T(4,128)(2,1)S(1)} collective-permute-done((bf16[4,3328]{1,0:T(4,128)(2,1)S(1)}, bf16[4,3328]{1,0:T(4,128)(2,1)S(1)}, u32[]{:S(2)}, u32[]{:S(2)}) %collective-permute-start.19) | collective-permute-done | bytes 26656 | tf_op jit(solution)/shard_map/ppermute | solution.py:231
  (145 shorter events, 35.3 us)
Async XLA Ops:
  2.2 10.6 %all-to-all-start = ((bf16[4,4,6656]{2,1,0:T(4,128)(2,1)}), bf16[4,4,6656]{2,1,0:T(4,128)(2,1)S(1)}, u32[]{:S(2)}, u32[]{:S(2)}) async-start(bf16[4,4,6656]{2,1,0:T(4,128)(2,1)} %broadcast_in_dim.52), calls=%async_computation | async-start | bytes 425984 | tf_op jit(solution)/shard_map/all_to_all | solution.py:29
  6.6 27.4 %collective-permute-start.7 = (bf16[104,6656]{1,0:T(8,128)(2,1)}, bf16[104,6656]{1,0:T(8,128)(2,1)}, u32[]{:S(2)}, u32[]{:S(2)}) collective-permute-start(bf16[104,6656]{1,0:T(8,128)(2,1)} %bitcast.88), channel_id=1, source_target_pairs={{0,2},{2,0},{1,3},{3,1},{4,6},{6,4},{5,7},{7,5},{8,10},{10,8},{9,1... | collective-permute-start | bytes 4153352 | tf_op jit(solution)/shard_map/ppermute | solution.py:25
  7.3 2.4 %collective-permute-start.10 = (f32[104]{0:T(128)S(1)}, f32[104]{0:T(128)S(1)}, u32[]{:S(2)}, u32[]{:S(2)}) collective-permute-start(f32[104]{0:T(128)S(1)} %bitcast_convert_fusion), channel_id=1, source_target_pairs={{0,2},{2,0},{1,3},{3,1},{4,6},{6,4},{5,7},{7,5},{8,10},{10,8},{9,1... | collective-permute-start | bytes 1256 | tf_op jit(solution)/shard_map/ppermute | solution.py:25
  7.8 49.2 %collective-permute-start = (bf16[3328,640]{1,0:T(8,128)(2,1)}, bf16[3328,640]{1,0:T(8,128)(2,1)}, u32[]{:S(2)}, u32[]{:S(2)}) collective-permute-start(bf16[3328,640]{1,0:T(8,128)(2,1)} %bitcast.72), channel_id=1, source_target_pairs={{0,2},{2,0},{1,3},{3,1},{4,6},{6,4},{5,7},{7,5},{8,10},{10,8},{9,1... | collective-permute-start | bytes 12779528 | tf_op jit(solution)/shard_map/ppermute | solution.py:25
  13.5 10.0 %collective-permute-start.1 = (bf16[16,6656]{1,0:T(8,128)(2,1)}, bf16[16,6656]{1,0:T(8,128)(2,1)}, u32[]{:S(2)}, u32[]{:S(2)}) collective-permute-start(bf16[16,6656]{1,0:T(8,128)(2,1)} %reshape.127), channel_id=1, source_target_pairs={{0,4},{4,8},{8,12},{12,16},{16,20},{20,24},{24,28},{28,0},{1,5},{5... | collective-permute-start | bytes 638984 | tf_op jit(solution)/shard_map/ppermute | solution.py:239
  15.4 8.1 %collective-permute-start.4 = (bf16[16,6656]{1,0:T(8,128)(2,1)}, bf16[16,6656]{1,0:T(8,128)(2,1)S(1)}, u32[]{:S(2)}, u32[]{:S(2)}) collective-permute-start(bf16[16,6656]{1,0:T(8,128)(2,1)} %reshape.127), channel_id=1, source_target_pairs={{0,28},{4,0},{8,4},{12,8},{16,12},{20,16},{24,20},{28,24},{1,29},{... | collective-permute-start | bytes 638984 | tf_op jit(solution)/shard_map/ppermute | solution.py:239
  19.4 14.7 %copy-start.11 = (bf16[1,6656,104]{1,2,0:T(8,128)(2,1)S(1)}, bf16[1,6656,104]{1,2,0:T(8,128)(2,1)}, u32[]{:S(2)}) copy-start(bf16[1,6656,104]{1,2,0:T(8,128)(2,1)} %param.7) | copy-start | bytes 4153348
  23.5 7.3 %collective-permute-start.2 = (bf16[16,6656]{1,0:T(8,128)(2,1)}, bf16[16,6656]{1,0:T(8,128)(2,1)S(1)}, u32[]{:S(2)}, u32[]{:S(2)}) collective-permute-start(bf16[16,6656]{1,0:T(8,128)(2,1)} %collective-permute-done.1), channel_id=1, source_target_pairs={{0,4},{4,8},{8,12},{12,16},{16,20},{20,24},{24,28},{28,0},{1,5},{5... | collective-permute-start | bytes 638984 | tf_op jit(solution)/shard_map/ppermute | solution.py:239
  23.5 7.3 %collective-permute-start.5 = (bf16[16,6656]{1,0:T(8,128)(2,1)S(1)}, bf16[16,6656]{1,0:T(8,128)(2,1)S(1)}, u32[]{:S(2)}, u32[]{:S(2)}) collective-permute-start(bf16[16,6656]{1,0:T(8,128)(2,1)S(1)} %collective-permute-done.4), channel_id=1, source_target_pairs={{0,28},{4,0},{8,4},{12,8},{16,12},{20,16},{24,20},{28,24},{1,29},{... | collective-permute-start | bytes 638984 | tf_op jit(solution)/shard_map/ppermute | solution.py:239
  30.8 7.9 %collective-permute-start.3 = (bf16[16,6656]{1,0:T(8,128)(2,1)S(1)}, bf16[16,6656]{1,0:T(8,128)(2,1)S(1)}, u32[]{:S(2)}, u32[]{:S(2)}) collective-permute-start(bf16[16,6656]{1,0:T(8,128)(2,1)S(1)} %collective-permute-done.2), channel_id=1, source_target_pairs={{0,4},{4,8},{8,12},{12,16},{16,20},{20,24},{24,28},{28,0},{1,5},{5... | collective-permute-start | bytes 638984 | tf_op jit(solution)/shard_map/ppermute | solution.py:239
  30.8 7.9 %collective-permute-start.6 = (bf16[16,6656]{1,0:T(8,128)(2,1)S(1)}, bf16[16,6656]{1,0:T(8,128)(2,1)S(1)}, u32[]{:S(2)}, u32[]{:S(2)}) collective-permute-start(bf16[16,6656]{1,0:T(8,128)(2,1)S(1)} %collective-permute-done.5), channel_id=1, source_target_pairs={{0,28},{4,0},{8,4},{12,8},{16,12},{20,16},{24,20},{28,24},{1,29},{... | collective-permute-start | bytes 638984 | tf_op jit(solution)/shard_map/ppermute | solution.py:239
  36.8 9.7 %copy-start.3 = (bf16[416,6656]{1,0:T(8,128)(2,1)}, bf16[416,6656]{1,0:T(8,128)(2,1)S(1)}, u32[]{:S(2)}) copy-start(bf16[416,6656]{1,0:T(8,128)(2,1)S(1)} %pad_maximum_fusion) | copy-start | bytes 16613380
  38.6 6.2 %collective-permute-start.8 = (bf16[8,6656]{1,0:T(8,128)(2,1)S(1)}, bf16[8,6656]{1,0:T(8,128)(2,1)S(1)}, u32[]{:S(2)}, u32[]{:S(2)}) collective-permute-start(bf16[8,6656]{1,0:T(8,128)(2,1)S(1)} %slice.39), channel_id=1, source_target_pairs={{0,4},{4,8},{8,12},{12,16},{16,20},{20,24},{24,28},{28,0},{1,5},{5... | collective-permute-start | bytes 319496 | tf_op jit(solution)/shard_map/ppermute | solution.py:239
  38.7 6.1 %collective-permute-start.9 = (bf16[8,6656]{1,0:T(8,128)(2,1)S(1)}, bf16[8,6656]{1,0:T(8,128)(2,1)S(1)}, u32[]{:S(2)}, u32[]{:S(2)}) collective-permute-start(bf16[8,6656]{1,0:T(8,128)(2,1)S(1)} %slice.40), channel_id=1, source_target_pairs={{0,28},{4,0},{8,4},{12,8},{16,12},{20,16},{24,20},{28,24},{1,29},{... | collective-permute-start | bytes 319496 | tf_op jit(solution)/shard_map/ppermute | solution.py:239
  47.7 23.6 %all-to-all-start.1 = ((bf16[16,208,128]{2,1,0:T(8,128)(2,1)}), bf16[16,208,128]{2,1,0:T(8,128)(2,1)S(1)}, u32[]{:S(2)}, u32[]{:S(2)}) async-start(bf16[16,208,128]{2,1,0:T(8,128)(2,1)} %broadcast_in_dim.62), calls=%async_computation.1 | async-start | bytes 1703936 | tf_op jit(solution)/shard_map/all_to_all | solution.py:29
  78.1 9.1 %collective-permute-start.11 = (s16[128,1408]{1,0:T(8,128)(2,1)}, s16[128,1408]{1,0:T(8,128)(2,1)S(1)}, u32[]{:S(2)}, u32[]{:S(2)}) collective-permute-start(s16[128,1408]{1,0:T(8,128)(2,1)} %get-tuple-element.23), channel_id=1, source_target_pairs={{0,1},{1,0},{2,3},{3,2},{4,5},{5,4},{6,7},{7,6},{8,9},{9,8},{10,11... | collective-permute-start | bytes 1081352 | tf_op jit(solution)/shard_map/ppermute | solution.py:25
  90.3 13.0 %all-to-all-start.2 = ((f32[16,3,128]{2,1,0:T(4,128)}), f32[16,3,128]{2,1,0:T(4,128)S(1)}, u32[]{:S(2)}, u32[]{:S(2)}) async-start(f32[16,3,128]{2,1,0:T(4,128)} %get-tuple-element.24.own_ref), calls=%async_computation.2 | async-start | bytes 65536 | tf_op jit(solution)/shard_map/all_to_all | solution.py:29
  105.7 22.6 %all-to-all-start.3 = ((bf16[16,208,128]{2,1,0:T(8,128)(2,1)}), bf16[16,208,128]{2,1,0:T(8,128)(2,1)S(1)}, u32[]{:S(2)}, u32[]{:S(2)}) async-start(bf16[16,208,128]{2,1,0:T(8,128)(2,1)} %bitcast.24), calls=%async_computation.3 | async-start | bytes 1703936 | tf_op jit(solution)/shard_map/all_to_all | solution.py:29
  111.4 24.1 %collective-permute-start.22 = (bf16[3328,128]{1,0:T(8,128)(2,1)S(1)}, bf16[3328,128]{1,0:T(8,128)(2,1)}, u32[]{:S(2)}, u32[]{:S(2)}) collective-permute-start(bf16[3328,128]{1,0:T(8,128)(2,1)S(1)} %bitcast.83), channel_id=1, source_target_pairs={{0,2},{2,0},{1,3},{3,1},{4,6},{6,4},{5,7},{7,5},{8,10},{10,8},{9,1... | collective-permute-start | bytes 2555912 | tf_op jit(solution)/shard_map/ppermute | solution.py:25
  112.8 22.7 %collective-permute-start.23 = (bf16[128,640]{1,0:T(8,128)(2,1)}, bf16[128,640]{1,0:T(8,128)(2,1)}, u32[]{:S(2)}, u32[]{:S(2)}) collective-permute-start(bf16[128,640]{1,0:T(8,128)(2,1)} %get-tuple-element.44), channel_id=1, source_target_pairs={{0,2},{2,0},{1,3},{3,1},{4,6},{6,4},{5,7},{7,5},{8,10},{10,8},{9,1... | collective-permute-start | bytes 491528 | tf_op jit(solution)/shard_map/ppermute | solution.py:25
  132.3 9.5 %collective-permute-start.12 = (bf16[128,1664]{1,0:T(8,128)(2,1)}, bf16[128,1664]{1,0:T(8,128)(2,1)S(1)}, u32[]{:S(2)}, u32[]{:S(2)}) collective-permute-start(bf16[128,1664]{1,0:T(8,128)(2,1)} %get-tuple-element.42), channel_id=1, source_target_pairs={{0,192},{64,0},{128,64},{192,128},{1,193},{65,1},{129,65},{193,129... | collective-permute-start | bytes 1277960 | tf_op jit(solution)/shard_map/ppermute | solution.py:231
  133.1 8.7 %collective-permute-start.13 = (bf16[128,1664]{1,0:T(8,128)(2,1)}, bf16[128,1664]{1,0:T(8,128)(2,1)S(1)}, u32[]{:S(2)}, u32[]{:S(2)}) collective-permute-start(bf16[128,1664]{1,0:T(8,128)(2,1)} %get-tuple-element.41), channel_id=1, source_target_pairs={{0,64},{64,128},{128,192},{192,0},{1,65},{65,129},{129,193},{193,1... | collective-permute-start | bytes 1277960 | tf_op jit(solution)/shard_map/ppermute | solution.py:231
  135.5 25.2 %collective-permute-start.18 = (bf16[128,6656]{1,0:T(8,128)(2,1)}, bf16[128,6656]{1,0:T(8,128)(2,1)}, u32[]{:S(2)}, u32[]{:S(2)}) collective-permute-start(bf16[128,6656]{1,0:T(8,128)(2,1)} %bitcast.86), channel_id=1, source_target_pairs={{0,2},{2,0},{1,3},{3,1},{4,6},{6,4},{5,7},{7,5},{8,10},{10,8},{9,1... | collective-permute-start | bytes 5111816 | tf_op jit(solution)/shard_map/ppermute | solution.py:25
  142.1 18.7 %copy-start.8 = (bf16[8,16,6656]{2,1,0:T(8,128)(2,1)S(1)}, bf16[8,16,6656]{2,1,0:T(8,128)(2,1)}, u32[]{:S(2)}) copy-start(bf16[8,16,6656]{2,1,0:T(8,128)(2,1)} %copy-done.7) | copy-start | bytes 5111812
  142.1 8.2 %collective-permute-start.14 = (bf16[32,3328]{1,0:T(8,128)(2,1)S(1)}, bf16[32,3328]{1,0:T(8,128)(2,1)S(1)}, u32[]{:S(2)}, u32[]{:S(2)}) collective-permute-start(bf16[32,3328]{1,0:T(8,128)(2,1)S(1)} %get-tuple-element.38), channel_id=1, source_target_pairs={{0,32},{32,0},{1,33},{33,1},{2,34},{34,2},{3,35},{35,3},{4,36},{36... | collective-permute-start | bytes 638984 | tf_op jit(solution)/shard_map/ppermute | solution.py:350
  142.6 12.8 %collective-permute-start.15 = (bf16[32,3328]{1,0:T(8,128)(2,1)S(1)}, bf16[32,3328]{1,0:T(8,128)(2,1)S(1)}, u32[]{:S(2)}, u32[]{:S(2)}) collective-permute-start(bf16[32,3328]{1,0:T(8,128)(2,1)S(1)} %get-tuple-element.39), channel_id=1, source_target_pairs={{0,33},{32,1},{1,32},{33,0},{2,35},{34,3},{3,34},{35,2},{4,37},{36... | collective-permute-start | bytes 638984 | tf_op jit(solution)/shard_map/ppermute | solution.py:350
  146.0 9.4 %collective-permute-start.16 = (bf16[32,3328]{1,0:T(8,128)(2,1)S(1)}, bf16[32,3328]{1,0:T(8,128)(2,1)S(1)}, u32[]{:S(2)}, u32[]{:S(2)}) collective-permute-start(bf16[32,3328]{1,0:T(8,128)(2,1)S(1)} %get-tuple-element.40), channel_id=1, source_target_pairs={{0,1},{32,33},{1,0},{33,32},{2,3},{34,35},{3,2},{35,34},{4,5},{36,... | collective-permute-start | bytes 638984 | tf_op jit(solution)/shard_map/ppermute | solution.py:350
  146.4 14.3 %collective-permute-start.17 = (f32[104,128]{1,0:T(8,128)S(1)}, f32[104,128]{1,0:T(8,128)S(1)}, u32[]{:S(2)}, u32[]{:S(2)}) collective-permute-start(f32[104,128]{1,0:T(8,128)S(1)} %get-tuple-element.48), channel_id=1, source_target_pairs={{0,2},{2,0},{1,3},{3,1},{4,6},{6,4},{5,7},{7,5},{8,10},{10,8},{9,1... | collective-permute-start | bytes 159752 | tf_op jit(solution)/shard_map/ppermute | solution.py:25
  156.3 14.3 %all-to-all-start.4 = ((bf16[8,4,3328]{2,1,0:T(4,128)(2,1)}), bf16[8,4,3328]{2,1,0:T(4,128)(2,1)S(1)}, u32[]{:S(2)}, u32[]{:S(2)}) async-start(bf16[8,4,3328]{2,1,0:T(4,128)(2,1)} %reshape.132), calls=%async_computation.4 | async-start | bytes 425984 | tf_op jit(solution)/shard_map/all_to_all | solution.py:29
  170.7 5.4 %collective-permute-start.19 = (bf16[4,3328]{1,0:T(4,128)(2,1)S(1)}, bf16[4,3328]{1,0:T(4,128)(2,1)S(1)}, u32[]{:S(2)}, u32[]{:S(2)}) collective-permute-start(bf16[4,3328]{1,0:T(4,128)(2,1)S(1)} %convert_element_type.135), channel_id=1, source_target_pairs={{0,128},{64,192},{128,0},{192,64},{1,129},{65,193},{129,1},{193,65... | collective-permute-start | bytes 79880 | tf_op jit(solution)/shard_map/ppermute | solution.py:231
  171.0 5.2 %collective-permute-start.20 = (bf16[4,3328]{1,0:T(4,128)(2,1)S(1)}, bf16[4,3328]{1,0:T(4,128)(2,1)S(1)}, u32[]{:S(2)}, u32[]{:S(2)}) collective-permute-start(bf16[4,3328]{1,0:T(4,128)(2,1)S(1)} %convert_element_type.135), channel_id=1, source_target_pairs={{0,64},{64,128},{128,192},{192,0},{1,65},{65,129},{129,193},{193,1... | collective-permute-start | bytes 79880 | tf_op jit(solution)/shard_map/ppermute | solution.py:231
  173.1 5.1 %collective-permute-start.21 = (bf16[4,3328]{1,0:T(4,128)(2,1)S(1)}, bf16[4,3328]{1,0:T(4,128)(2,1)S(1)}, u32[]{:S(2)}, u32[]{:S(2)}) collective-permute-start(bf16[4,3328]{1,0:T(4,128)(2,1)S(1)} %convert_element_type.135), channel_id=1, source_target_pairs={{0,192},{64,0},{128,64},{192,128},{1,193},{65,1},{129,65},{193,129... | collective-permute-start | bytes 79880 | tf_op jit(solution)/shard_map/ppermute | solution.py:231
  (14 other events, 72.8 us)
